TPU v7x, 512 devices: a whole 4x4x16 slice. The times are simulated.
512 devices in a mesh: fsdp: 16 (over z_lo, core), tensor: 4 (over y), replica: 8 (over x, z_hi).
Axes of the slice: x: 4, y: 4, z: 16 (z_hi: 2, z_lo: 8; z = z_hi * 8 + z_lo), core: 2. Of those that a mesh axis runs over, the one named last changes fastest.
Arguments:
- hidden: bfloat16 [4, 128, 8192], P(None, ('fsdp', 'replica')), may hold values from -6 to 6
- kv_weight: bfloat16 [8192, 2, 1024], P(('fsdp', 'replica'), None, 'tensor'), may hold values from -0.0625 to 0.0625
- queries: bfloat16 [4, 128, 8192], P(None, ('fsdp', 'replica'), 'tensor'), may hold values from -360 to 360, as said below
- key_cache: bfloat16 [128, 2048, 1024], P(('fsdp', 'replica'), 'tensor'), may hold values from -6 to 6
- value_cache: bfloat16 [128, 2048, 1024], P(('fsdp', 'replica'), 'tensor'), may hold values from -6 to 6
- lengths: int32 [128], P(('fsdp', 'replica')), may hold values from 1 to 2044, as said below
Outputs:
- attended: bfloat16 [4, 128, 8192], P(None, ('fsdp', 'replica'), 'tensor')
- new_keys: bfloat16 [4, 128, 1024], P(None, ('fsdp', 'replica'), 'tensor')
- new_values: bfloat16 [4, 128, 1024], P(None, ('fsdp', 'replica'), 'tensor')
Inputs may be any that keep to these rules, and one draw needn't show every extreme that they name: Entries of queries stay within the bounds. Row r's cache is valid at positions below lengths[r]; some row has exactly 2044, some row has 1.
All inputs are finite; a program needn't handle non-finite values.
Results may differ from a plain program's by a relative error of at most 0.013.
Values may be sent and summed in bfloat16 or wider, within the bound.
No kernel may reach another device: no remote copies, remote signals or barrier semaphores. Data moves between devices by JAX's collectives and lax.ppermute only.
A program may use at most 64 MiB of HBM per device.

v0:
```python
import jax
import jax.numpy as jnp
from jax import lax
from jax.sharding import PartitionSpec as P

KVH = 8
HQ = 64
HD = 128


ROPE_BASE = 500000.0
NEG_FILL = -1e30


def rotate(vectors, positions, head_count):
    step_count, row_count, width_all = vectors.shape
    head_size = width_all // head_count
    half_size = head_size // 2
    frequency = ROPE_BASE ** (-jnp.arange(half_size, dtype=jnp.float32) * 2.0 / head_size)
    phases = positions.astype(jnp.float32)[:, :, None] * frequency[None, None, :]
    cos_part = jnp.cos(phases)[:, :, None, :]
    sin_part = jnp.sin(phases)[:, :, None, :]
    heads_view = vectors.reshape(step_count, row_count, head_count, head_size)
    front_half = heads_view[..., :half_size]
    back_half = heads_view[..., half_size:]
    turned = jnp.concatenate(
        [
            front_half * cos_part - back_half * sin_part,
            front_half * sin_part + back_half * cos_part,
        ],
        axis=-1,
    )
    return turned.reshape(step_count, row_count, width_all)


def softmax_terms(query_block, key_block, value_block, allowed):
    scaling = query_block.shape[-1] ** (-0.5)
    scores = (
        jnp.einsum("srhgd,rchd->srhgc", query_block, key_block, preferred_element_type=jnp.float32)
        * scaling
    )
    allowed_full = allowed[:, :, None, None, :]
    masked = jnp.where(allowed_full, scores, NEG_FILL)
    maxima = jnp.max(masked, axis=-1)
    weights = jnp.where(allowed_full, jnp.exp(masked - maxima[..., None]), 0.0)
    totals = jnp.sum(weights, axis=-1)
    summed = jnp.einsum(
        "srhgc,rchd->srhgd",
        weights.astype(jnp.bfloat16),
        value_block,
        preferred_element_type=jnp.float32,
    )
    return (maxima, totals, summed)


def combine_terms(earlier, later):
    joined_max = jnp.maximum(earlier[0], later[0])
    scale_one = jnp.exp(earlier[0] - joined_max)
    scale_two = jnp.exp(later[0] - joined_max)
    totals = earlier[1] * scale_one + later[1] * scale_two
    summed = earlier[2] * scale_one[..., None] + later[2] * scale_two[..., None]
    return (joined_max, totals, summed)


def body(hidden, kv_weight, queries, key_cache, value_cache, lengths):
    step_count, row_count, model_width = hidden.shape
    local_width = kv_weight.shape[2]
    head_size = HD
    local_heads = local_width // head_size
    group_size = HQ // KVH
    flat_rows = hidden.reshape(step_count * row_count, model_width)
    portion = lax.all_gather(kv_weight, ("fsdp", "replica"), axis=0, tiled=True)
    projected = jnp.dot(
        flat_rows,
        portion.reshape(portion.shape[0], 2 * local_width),
        preferred_element_type=jnp.float32,
    )
    projected = projected.reshape(step_count, row_count, 2, local_width)
    positions = lengths[None, :] + jnp.arange(step_count, dtype=jnp.int32)[:, None]
    new_keys = rotate(projected[:, :, 0], positions, local_heads).astype(jnp.bfloat16)
    new_values = projected[:, :, 1].astype(jnp.bfloat16)
    step_index = jnp.arange(step_count, dtype=jnp.int32)
    fresh_valid = (step_index[None, :] <= step_index[:, None])[:, None, :]
    own_keys, own_values = (
        lax.all_to_all(key_cache, "tensor", split_axis=2, concat_axis=1, tiled=True),
        lax.all_to_all(value_cache, "tensor", split_axis=2, concat_axis=1, tiled=True),
    )
    full_length = own_keys.shape[1]
    cache_valid = (jnp.arange(full_length, dtype=jnp.int32)[None, :] < lengths[:, None])[None]
    shaped = queries.reshape(step_count, row_count, local_heads, group_size, head_size)
    cache_part = softmax_terms(
        shaped,
        own_keys.reshape(row_count, full_length, local_heads, head_size),
        own_values.reshape(row_count, full_length, local_heads, head_size),
        cache_valid,
    )
    fresh_keys = jnp.transpose(new_keys, (1, 0, 2)).reshape(
        row_count, step_count, local_heads, head_size
    )
    fresh_vals = jnp.transpose(new_values, (1, 0, 2)).reshape(
        row_count, step_count, local_heads, head_size
    )
    fresh_part = softmax_terms(shaped, fresh_keys, fresh_vals, fresh_valid)
    joined_max, totals, summed = combine_terms(cache_part, fresh_part)
    attended = (
        (summed / totals[..., None])
        .reshape(step_count, row_count, local_width * group_size)
        .astype(jnp.bfloat16)
    )
    return (attended, new_keys, new_values)


def solution(mesh):
    return jax.shard_map(
        body,
        mesh=mesh,
        in_specs=(
            P(None, ("fsdp", "replica"), None),
            P(("fsdp", "replica"), None, "tensor"),
            P(None, ("fsdp", "replica"), "tensor"),
            P(("fsdp", "replica"), "tensor", None),
            P(("fsdp", "replica"), "tensor", None),
            P(("fsdp", "replica")),
        ),
        out_specs=(
            P(None, ("fsdp", "replica"), "tensor"),
            P(None, ("fsdp", "replica"), "tensor"),
            P(None, ("fsdp", "replica"), "tensor"),
        ),
        check_vma=False,
    )
```

profile of v0, /device:TPU:97, one launch (start us, length us, event | category | flops | bytes accessed | tf_op | source)
XLA Modules:
  0.0 428.7 jit_solution(1201188792672973320)
XLA Ops:
  7.2 0.7 all-gather.2.cloned.1.call-update
  7.9 4.6 %copy.39 = bf16[1,512,1024]{1,0,2:T(2,128)(2,1)S(1)} copy(bf16[1,512,1024]{2,1,0:T(8,128)(2,1)} %param.9) | data formatting | bytes 2097152 | tf_op args[3]
  12.5 0.5 broadcast.81
  13.1 7.0 %reduce.5 = bf16[1024,512]{1,0:T(8,128)(2,1)S(1)} reduce(bf16[1024,1,512]{2,1,0:T(2,128)(2,1)S(1)} %bitcast.119, bf16[]{:T(256)} %broadcast.81), dimensions={1}, to_apply=%bitcast.99.reduce_sub_computation | reduce | bytes 2097154
  20.1 2.0 reshape.269
  22.1 4.2 all-to-all-start
  26.3 4.6 %copy.43 = bf16[1,512,1024]{1,0,2:T(2,128)(2,1)S(1)} copy(bf16[1,512,1024]{2,1,0:T(8,128)(2,1)} %param.10) | data formatting | bytes 2097152 | tf_op args[4]
  30.9 8.0 %reduce.4 = bf16[1024,512]{1,0:T(8,128)(2,1)} reduce(bf16[1024,1,512]{2,1,0:T(2,128)(2,1)S(1)} %bitcast.120, bf16[]{:T(256)} %broadcast.81), dimensions={1}, to_apply=%bitcast.97.reduce_sub_computation | reduce | bytes 2097154
  39.0 3.8 reshape.267
  42.7 4.5 %all-to-all-start.1 = ((bf16[4,2,65536]{2,1,0:T(2,128)(2,1)}), bf16[4,2,65536]{2,1,0:T(2,128)(2,1)}, u32[]{:S(2)}, u32[]{:S(2)}) async-start(bf16[4,2,65536]{2,1,0:T(2,128)(2,1)} %reshape.267), calls=%async_computation.1 | async-start | bytes 2097152 | tf_op jit(solution)/shard_map/all_to_all | solution.py:86
  48.0 1.0 reshape.270
  49.3 0.5 copy.40
  49.8 1.1 reshape.254
  50.9 10.1 %all-to-all-done.1 = bf16[4,2,65536]{2,1,0:T(2,128)(2,1)} async-done(((bf16[4,2,65536]{2,1,0:T(2,128)(2,1)}), bf16[4,2,65536]{2,1,0:T(2,128)(2,1)}, u32[]{:S(2)}, u32[]{:S(2)}) %all-to-all-start.1) | async-done | bytes 1048608 | tf_op jit(solution)/shard_map/all_to_all | solution.py:86
  61.1 2.6 reshape.268
  64.0 0.5 copy.44
  64.9 1.8 fusion.43
  66.9 325.3 %all-gather.2.cloned.1.call-done = bf16[8192,2,256]{2,1,0:T(2,128)(2,1)} async-done(((bf16[64,2,256]{2,1,0:T(2,128)(2,1)}), bf16[8192,2,256]{2,1,0:T(2,128)(2,1)}) %all-gather.2.cloned.1.call-update) | async-done | bytes 8388624 | tf_op jit(solution)/shard_map/all_gather | solution.py:72
  392.2 21.2 %copy.60 = bf16[8192,2,256]{0,2,1:T(8,128)(2,1)} copy(bf16[8192,2,256]{2,1,0:T(2,128)(2,1)} %all-gather.2.cloned.1.call-done) | data formatting | bytes 16777216 | tf_op jit(solution)/shard_map/reshape | solution.py:75
  413.3 5.6 %fusion.11 = f32[4,1,2,256]{3,0,2,1:T(4,128)S(1)} fusion(bf16[8192,2,256]{0,2,1:T(8,128)(2,1)} %copy.60, bf16[4,1,8192]{2,0,1:T(4,128)(2,1)S(1)} %copy-done), kind=kOutput, calls=%fused_computation.15 | convolution fusion | flops 33554432 | bytes 8462336 | tf_op jit(solution)/shard_map/dot_general | solution.py:73
  419.0 0.6 fusion.38
  419.6 0.7 fusion.45
  420.6 0.3 fusion.8
  421.3 0.6 convert_element_type.75
  (22 shorter events, 2.0 us)
Async XLA Ops:
  7.2 406.1 %copy-start = (bf16[4,1,8192]{2,0,1:T(4,128)(2,1)S(1)}, bf16[4,1,8192]{2,0,1:T(4,128)(2,1)}, u32[]{:S(2)}) copy-start(bf16[4,1,8192]{2,0,1:T(4,128)(2,1)} %param.6) | copy-start | bytes 196612
  7.2 385.0 %all-gather.2.cloned.1.call-start = ((), (), s32[]{:S(2)}) async-start(), calls=%async_computation.2 | async-start | bytes 8454144 | tf_op jit(solution)/shard_map/all_gather | solution.py:72
  22.1 20.6 %all-to-all-start = ((bf16[4,2,65536]{2,1,0:T(2,128)(2,1)}), bf16[4,2,65536]{2,1,0:T(2,128)(2,1)S(1)}, u32[]{:S(2)}, u32[]{:S(2)}) async-start(bf16[4,2,65536]{2,1,0:T(2,128)(2,1)} %reshape.269), calls=%async_computation | async-start | bytes 2097152 | tf_op jit(solution)/shard_map/all_to_all | solution.py:85
  42.7 18.4 %all-to-all-start.1 = ((bf16[4,2,65536]{2,1,0:T(2,128)(2,1)}), bf16[4,2,65536]{2,1,0:T(2,128)(2,1)}, u32[]{:S(2)}, u32[]{:S(2)}) async-start(bf16[4,2,65536]{2,1,0:T(2,128)(2,1)} %reshape.267), calls=%async_computation.1 | async-start | bytes 2097152 | tf_op jit(solution)/shard_map/all_to_all | solution.py:86
  49.0 15.9 %copy-start.1 = (bf16[4,1,2048]{2,0,1:T(4,128)(2,1)S(1)}, bf16[4,1,2048]{2,0,1:T(4,128)(2,1)}, u32[]{:S(2)}) copy-start(bf16[4,1,2048]{2,0,1:T(4,128)(2,1)} %param.8) | copy-start | bytes 49156
Sparse Core Ops, SparseCore 0:
  10.1 381.9 all-gather.1
where the time goes:
time: 430 us; the launch traced here: 429 us
  waiting for transfers between devices  336 us (78%)
  local copies, waits for them, and re-layouts  44.6 us (10%)
  other arithmetic  16.3 us (4%)
  between operations  14.8 us (3%)
  starting transfers between devices  8.69 us (2%)
  matrix products  8.22 us (2%)
    all_gather x1, waiting for transfers between devices, body(): portion = lax.all_gather(kv_weight, ('fsdp', 'replica'), axis=0, tiled=True)  325 us
    reshape x1, local copies, waits for them, and re-layouts, body(): portion.reshape(portion.shape[0], 2 * local_width)  21.2 us
    unnamed x13, local copies, waits for them, and re-layouts  19.7 us
    unnamed x2, other arithmetic  15.1 us
    all_to_all x1, waiting for transfers between devices, body(): lax.all_to_all(value_cache, 'tensor', split_axis=2, concat_axis=1, tiled=...  10.1 us
  transfers between devices with their start and end apart: 3, of which 2 were waited for; matrix products, arithmetic and copies ran while one was open for 9% of the time, Pallas kernels for 0%

commit v1 on v0

v1 whole, which is shorter than its diff:
```python
import jax
import jax.numpy as jnp
from jax import lax
from jax.experimental import pallas as pl
from jax.experimental.pallas import tpu as pltpu
from jax.sharding import Mesh
from jax.sharding import PartitionSpec as P

KVH = 8
HQ = 64
HD = 128
STEPS = 4
GROUP = HQ // KVH
TENSOR = 4
LOCAL_HEADS = KVH // TENSOR
HEAD_ROWS = STEPS * GROUP
OWN_ROWS = LOCAL_HEADS * HEAD_ROWS
ROPE_BASE = 500000.0
NEG_FILL = -1e30
F32 = jnp.float32
BF16 = jnp.bfloat16
PARAMS = pltpu.CompilerParams(vmem_limit_bytes=16 * 1024 * 1024)
ROWS_AXES = ("zlo", "core", "x", "zhi")
Z_AXES = ("zhi", "zlo")


def lane_iota(shape):
    return lax.broadcasted_iota(jnp.int32, shape, 1)


def prepare_kernel(hidden_ref, queries_ref, hidden_out, queries_out, rows):
    low = lane_iota((STEPS, 128)) < 64
    for zlo in range(8):
        for pair in range(4):
            at = zlo * 1024 + pair * 256
            one = hidden_ref[:, 0, at : at + 128].astype(F32)
            two = hidden_ref[:, 0, at + 128 : at + 256].astype(F32)
            to = slice(pair * 128, pair * 128 + 128)
            hidden_out[zlo, :, to] = jnp.where(low, one, pltpu.roll(two, 64, 1)).astype(BF16)
            hidden_out[8 + zlo, :, to] = jnp.where(low, pltpu.roll(one, 64, 1), two).astype(BF16)
    for head in range(LOCAL_HEADS):
        for member in range(GROUP):
            at = (head * GROUP + member) * HD
            block = queries_ref[:, 0, at : at + HD].astype(F32)
            for step in range(STEPS):
                row = head * HEAD_ROWS + step * GROUP + member
                rows[row : row + 1, :] = block[step : step + 1, :]
    packed = rows[...].astype(BF16)
    for to in range(TENSOR):
        queries_out[to] = packed


def prepare(hidden, queries):
    return pl.pallas_call(
        prepare_kernel,
        out_shape=(
            jax.ShapeDtypeStruct((16, STEPS, 512), BF16),
            jax.ShapeDtypeStruct((TENSOR, OWN_ROWS, HD), BF16),
        ),
        scratch_shapes=[pltpu.VMEM((OWN_ROWS, HD), F32)],
        compiler_params=PARAMS,
        name="prepare",
    )(hidden, queries)


def attend_kernel(place_ref, queries_ref, keys_ref, values_ref, out_ref, spread):
    spread[...] = jnp.zeros_like(spread)
    for head in range(KVH):
        piece = queries_ref[head // 2, (head % 2) * HEAD_ROWS : (head % 2 + 1) * HEAD_ROWS, :]
        spread[head * HEAD_ROWS : (head + 1) * HEAD_ROWS, head * HD : (head + 1) * HD] = piece
    scores = lax.dot_general(
        keys_ref[0], spread[...], (((1,), (1,)), ((), ())), preferred_element_type=F32
    ) * (HD**-0.5)
    position = place_ref[0] + lax.broadcasted_iota(jnp.int32, scores.shape, 0)
    allowed = position < place_ref[1]
    masked = jnp.where(allowed, scores, NEG_FILL)
    maxima = jnp.max(masked, axis=0, keepdims=True)
    weights = jnp.where(allowed, jnp.exp(masked - maxima), 0.0)
    totals = jnp.sum(weights, axis=0, keepdims=True)
    rounded = weights.astype(BF16)
    for half in range(2):
        summed = lax.dot_general(
            rounded[:, half * 128 : half * 128 + 128],
            values_ref[0, :, half * 512 : half * 512 + 512],
            (((0,), (0,)), ((), ())),
            preferred_element_type=F32,
        )
        for inner in range(4):
            head = half * 4 + inner
            out_ref[head // 2, (head % 2) * HEAD_ROWS : (head % 2 + 1) * HEAD_ROWS, :] = summed[
                inner * HEAD_ROWS : (inner + 1) * HEAD_ROWS, inner * HD : (inner + 1) * HD
            ]
    for to in range(TENSOR):
        span = slice((to // 2) * 128, (to // 2) * 128 + 128)
        pair = jnp.concatenate([maxima[:, span], totals[:, span]], axis=0)
        if to % 2:
            pair = pltpu.roll(pair, 64, 1)
        out_ref[to, OWN_ROWS : OWN_ROWS + 2, :] = pair


def attend(place, queries, keys, values):
    whole = pl.BlockSpec(memory_space=pltpu.VMEM)
    return pl.pallas_call(
        attend_kernel,
        out_shape=jax.ShapeDtypeStruct((TENSOR, OWN_ROWS + 8, HD), F32),
        in_specs=[pl.BlockSpec(memory_space=pltpu.SMEM), whole, whole, whole],
        out_specs=whole,
        scratch_shapes=[pltpu.VMEM((KVH * HEAD_ROWS, KVH * HD), BF16)],
        compiler_params=PARAMS,
        cost_estimate=pl.CostEstimate(
            flops=2 * 2 * 512 * 1024 * 256, bytes_accessed=5 << 20, transcendentals=512 * 256
        ),
        name="attend",
    )(place, queries, keys, values)


def project_kernel(place_ref, hidden_ref, own_ref, other_ref, out_ref, tokens):
    for z in range(16):
        tokens[z * STEPS : (z + 1) * STEPS, :] = hidden_ref[z].astype(F32)
    first = tokens[:, :256]
    second = tokens[:, 256:]
    swap = place_ref[2] == 1
    own = jnp.where(swap, second, first).astype(BF16)
    other = jnp.where(swap, first, second).astype(BF16)
    partial = jnp.dot(own, own_ref[...].reshape(256, 512), preferred_element_type=F32)
    partial += jnp.dot(other, other_ref[...].reshape(256, 512), preferred_element_type=F32)
    for z in range(16):
        out_ref[z] = partial[z * STEPS : (z + 1) * STEPS, :]


def project(place, hidden, own, other):
    whole = pl.BlockSpec(memory_space=pltpu.VMEM)
    return pl.pallas_call(
        project_kernel,
        out_shape=jax.ShapeDtypeStruct((16, STEPS, 512), F32),
        in_specs=[pl.BlockSpec(memory_space=pltpu.SMEM), whole, whole, whole],
        out_specs=whole,
        scratch_shapes=[pltpu.VMEM((64, 512), F32)],
        compiler_params=PARAMS,
        cost_estimate=pl.CostEstimate(
            flops=2 * 64 * 512 * 512, bytes_accessed=1 << 20, transcendentals=0
        ),
        name="project",
    )(place, hidden, own, other)


def finish_kernel(
    parts_ref, sums_ref, queries_ref, cos_ref, sin_ref, attended_ref, keys_ref, values_ref, wide
):
    projected = jnp.sum(sums_ref[...], axis=0)
    cos_part = cos_ref[...]
    sin_part = sin_ref[...]
    new_values = projected[:, 256:].astype(BF16)
    values_ref[:, 0, :] = new_values
    queries = queries_ref[0]
    fresh = []
    for head in range(LOCAL_HEADS):
        front = projected[:, head * HD : (head + 1) * HD]
        turned = (front * cos_part + pltpu.roll(front, HD // 2, 1) * sin_part).astype(BF16)
        keys_ref[:, 0, head * HD : (head + 1) * HD] = turned
        fresh.append(
            lax.dot_general(
                turned, queries, (((1,), (1,)), ((), ())), preferred_element_type=F32
            )
        )
    lane = lane_iota((STEPS, OWN_ROWS))
    scores = jnp.where(lane < HEAD_ROWS, fresh[0], fresh[1]) * (HD**-0.5)
    step = (lane % HEAD_ROWS) // GROUP
    allowed = lax.broadcasted_iota(jnp.int32, (STEPS, OWN_ROWS), 0) <= step
    masked = jnp.where(allowed, scores, NEG_FILL)
    maxima = [parts_ref[t, OWN_ROWS : OWN_ROWS + 1, :OWN_ROWS] for t in range(TENSOR)]
    joined = jnp.max(masked, axis=0, keepdims=True)
    for part in maxima:
        joined = jnp.maximum(joined, part)
    weights = jnp.where(allowed, jnp.exp(masked - joined), 0.0)
    totals = jnp.sum(weights, axis=0, keepdims=True)
    scales = []
    for t in range(TENSOR):
        scale = jnp.exp(maxima[t] - joined)
        totals += parts_ref[t, OWN_ROWS + 1 : OWN_ROWS + 2, :OWN_ROWS] * scale
        scales.append(scale)
    factors = jnp.concatenate([*scales, weights.astype(BF16).astype(F32)], axis=0) / totals
    factors = jnp.concatenate([factors, jnp.zeros((8, 128 - OWN_ROWS), F32)], axis=1)
    columns = jnp.transpose(factors, (1, 0))
    values = new_values.astype(F32)
    for head in range(LOCAL_HEADS):
        rows = slice(head * HEAD_ROWS, (head + 1) * HEAD_ROWS)
        total = jnp.zeros((HEAD_ROWS, HD), F32)
        for t in range(TENSOR):
            total += parts_ref[t, rows, :] * columns[rows, t : t + 1]
        for t in range(STEPS):
            total += columns[rows, 4 + t : 5 + t] * values[t : t + 1, head * HD : (head + 1) * HD]
        for s in range(STEPS):
            for member in range(GROUP):
                at = (head * GROUP + member) * HD
                row = s * GROUP + member
                wide[s : s + 1, at : at + HD] = total[row : row + 1, :]
    attended_ref[:, 0, :] = wide[...].astype(BF16)


def finish(parts, sums, queries, cos_part, sin_part):
    return pl.pallas_call(
        finish_kernel,
        out_shape=(
            jax.ShapeDtypeStruct((STEPS, 1, LOCAL_HEADS * GROUP * HD), BF16),
            jax.ShapeDtypeStruct((STEPS, 1, LOCAL_HEADS * HD), BF16),
            jax.ShapeDtypeStruct((STEPS, 1, LOCAL_HEADS * HD), BF16),
        ),
        scratch_shapes=[pltpu.VMEM((STEPS, LOCAL_HEADS * GROUP * HD), F32)],
        compiler_params=PARAMS,
        name="finish",
    )(parts, sums, queries, cos_part, sin_part)


def rotation(lengths):
    half = HD // 2
    positions = lengths[None, :] + jnp.arange(STEPS, dtype=jnp.int32)[:, None]
    frequency = ROPE_BASE ** (-jnp.arange(half, dtype=F32) * 2.0 / HD)
    phases = positions.astype(F32) * frequency[None, :]
    cos_part = jnp.cos(phases)
    sin_part = jnp.sin(phases)
    return (
        jnp.concatenate([cos_part, cos_part], axis=-1),
        jnp.concatenate([-sin_part, sin_part], axis=-1),
    )


def body(hidden, kv_weight, queries, key_cache, value_cache, lengths):
    place = jnp.stack([lax.axis_index("tensor") * 512, lengths[0], lax.axis_index("core")])
    spread_hidden, spread_queries = prepare(hidden, queries)
    weight = kv_weight.reshape(1, 64, 512)
    own = lax.all_to_all(jnp.broadcast_to(weight, (4, 64, 512)), "x", 0, 0)
    tokens = lax.all_to_all(spread_hidden, Z_AXES, 0, 0)
    all_queries = lax.all_to_all(spread_queries, "tensor", 0, 0)
    other = lax.ppermute(own, "core", [(0, 1), (1, 0)])
    partial = project(place, tokens, own, other)
    sums = lax.all_to_all(partial, Z_AXES, 0, 0)
    parts = attend(place, all_queries, key_cache, value_cache)
    parts = lax.all_to_all(parts, "tensor", 0, 0)
    cos_part, sin_part = rotation(lengths)
    return finish(parts, sums, spread_queries, cos_part, sin_part)


def solution(mesh):
    split = Mesh(mesh.devices.reshape(8, 2, 4, 4, 2), ("zlo", "core", "tensor", "x", "zhi"))
    return jax.shard_map(
        body,
        mesh=split,
        in_specs=(
            P(None, ROWS_AXES, None),
            P(ROWS_AXES, None, "tensor"),
            P(None, ROWS_AXES, "tensor"),
            P(ROWS_AXES, "tensor", None),
            P(ROWS_AXES, "tensor", None),
            P(ROWS_AXES),
        ),
        out_specs=(
            P(None, ROWS_AXES, "tensor"),
            P(None, ROWS_AXES, "tensor"),
            P(None, ROWS_AXES, "tensor"),
        ),
        check_vma=False,
    )
```

time: 430 us -> 84 us (0.20)
  the two profiles are of different devices: /device:TPU:97 before, /device:TPU:32 now
where the time goes in v1:
time: 84 us; the launch traced here: 83.4 us
  starting transfers between devices  31.7 us (38%)
  waiting for transfers between devices  28.5 us (34%)
  blocking collectives  10.8 us (13%)
  Pallas kernels  5.86 us (7%)
  local copies, waits for them, and re-layouts  4.94 us (6%)
  between operations  1.37 us (2%)
    all_to_all x1, starting transfers between devices, body(): tokens = lax.all_to_all(spread_hidden, Z_AXES, 0, 0)  15.2 us
    all_to_all x1, waiting for transfers between devices, body(): sums = lax.all_to_all(partial, Z_AXES, 0, 0)  13.5 us
    all_to_all x1, blocking collectives, body(): own = lax.all_to_all(jnp.broadcast_to(weight, (4, 64, 512)), 'x', 0, 0)  10.8 us
    all_to_all x1, starting transfers between devices, body(): sums = lax.all_to_all(partial, Z_AXES, 0, 0)  6.72 us
    all_to_all x1, waiting for transfers between devices, body(): tokens = lax.all_to_all(spread_hidden, Z_AXES, 0, 0)  5.63 us
    all_to_all x1, waiting for transfers between devices, body(): all_queries = lax.all_to_all(spread_queries, 'tensor', 0, 0)  4.77 us
    all_to_all x1, waiting for transfers between devices, body(): parts = lax.all_to_all(parts, 'tensor', 0, 0)  4.62 us
    all_to_all x1, starting transfers between devices, body(): all_queries = lax.all_to_all(spread_queries, 'tensor', 0, 0)  4.46 us
  transfers between devices with their start and end apart: 5, of which 4 were waited for; matrix products, arithmetic and copies ran while one was open for 1% of the time, Pallas kernels for 4%

profile of v1, /device:TPU:32, one launch (start us, length us, event | category | flops | bytes accessed | tf_op | source)
XLA Modules:
  0.0 83.4 jit_solution(4120230492817203071)
XLA Ops:
  0.7 1.0 %copy.9.hidden_ref = bf16[4,1,8192]{2,1,0:T(2,128)(2,1)S(1)} copy(bf16[4,1,8192]{2,0,1:T(4,128)(2,1)} %param.6) | data formatting | bytes 131072 | tf_op args[0]
  1.7 0.8 %prepare.1 = (bf16[16,4,512]{2,1,0:T(4,128)(2,1)}, bf16[4,64,128]{2,1,0:T(8,128)(2,1)}) custom-call(bf16[4,1,8192]{2,1,0:T(2,128)(2,1)S(1)} %copy.9.hidden_ref, bf16[4,1,2048]{2,1,0:T(2,128)(2,1)S(1)} %copy.10.queries_ref), custom_call_target="tpu_custom_call" | custom-call | tf_op jit(solution)/shard_map/prepare/pallas_call | solution.py:54
  2.6 4.5 %all-to-all-start = ((bf16[4,64,128]{2,1,0:T(8,128)(2,1)}), bf16[4,64,128]{2,1,0:T(8,128)(2,1)S(1)}, u32[]{:S(2)}, u32[]{:S(2)}) async-start(bf16[4,64,128]{2,1,0:T(8,128)(2,1)} %get-tuple-element.5.queries_ref), calls=%async_computation | async-start | bytes 131072 | tf_op jit(solution)/shard_map/all_to_all | solution.py:234
  7.0 0.8 %copy.14 = bf16[8,8,2,256]{3,1,2,0:T(8,128)(2,1)S(1)} copy(bf16[8,8,2,256]{3,2,1,0:T(2,128)(2,1)} %bitcast.7) | data formatting | bytes 131072
  7.9 4.8 %all-to-all-done.queries_ref = bf16[4,64,128]{2,1,0:T(8,128)(2,1)S(1)} async-done(((bf16[4,64,128]{2,1,0:T(8,128)(2,1)}), bf16[4,64,128]{2,1,0:T(8,128)(2,1)S(1)}, u32[]{:S(2)}, u32[]{:S(2)}) %all-to-all-start) | async-done | bytes 65568 | tf_op jit(solution)/shard_map/all_to_all | solution.py:234
  12.7 10.8 %all_to_all.25.own_ref = bf16[4,64,512]{2,1,0:T(8,128)(2,1)S(1)} all-to-all(bf16[4,64,512]{2,1,0:T(8,128)(2,1)S(1)} %broadcast_in_dim.5), channel_id=1, replica_groups=mesh['zlo'=8,'core'=2,'tensor'=4,'x'=4,'zhi'=2] {'x'}, dimensions={0} | all-to-all | bytes 524288 | tf_op jit(solution)/shard_map/all_to_all | solution.py:232
  23.5 15.2 %all-to-all-start.2 = ((bf16[16,4,512]{2,1,0:T(4,128)(2,1)}), bf16[16,4,512]{2,1,0:T(4,128)(2,1)S(1)}, u32[]{:S(2)}, u32[]{:S(2)}) async-start(bf16[16,4,512]{2,1,0:T(4,128)(2,1)} %get-tuple-element.6), calls=%async_computation.2 | async-start | bytes 131072 | tf_op jit(solution)/shard_map/all_to_all | solution.py:233
  39.3 1.9 %collective-permute-start = (bf16[4,64,512]{2,1,0:T(8,128)(2,1)S(1)}, bf16[4,64,512]{2,1,0:T(8,128)(2,1)S(1)}, u32[]{:S(2)}, u32[]{:S(2)}) collective-permute-start(bf16[4,64,512]{2,1,0:T(8,128)(2,1)S(1)} %all_to_all.25.own_ref), channel_id=1, source_target_pairs={{0,32},{32,0},{1,33},{33,1},{2,34},{34,2},{3,35},{35,3},{4,36},{36... | collective-permute-start | bytes 786440 | tf_op jit(solution)/shard_map/ppermute | solution.py:235
  41.3 0.1 pad_add_fusion.place_ref
  41.3 1.2 %copy-done.1 = bf16[1,512,1024]{2,1,0:T(8,128)(2,1)S(1)} copy-done((bf16[1,512,1024]{2,1,0:T(8,128)(2,1)S(1)}, bf16[1,512,1024]{2,1,0:T(8,128)(2,1)}, u32[]{:S(2)}) %copy-start.1) | copy-done | bytes 1048600
  42.6 2.3 %attend.1 = f32[4,72,128]{2,1,0:T(8,128)} custom-call(s32[3]{0:T(128)S(1)} %pad_add_fusion.place_ref, bf16[4,64,128]{2,1,0:T(8,128)(2,1)S(1)} %all-to-all-done.queries_ref, bf16[1,512,1024]{2,1,0:T(8,128)(2,1)S(1)} %copy-done, bf16[1,512,1024]{2,1,0:T(8,128)(2,1)S(1)} %copy-done.1), custom_call_target="tpu_custom_call" | custom-call | flops 536870912 | bytes 5242880 | tf_op jit(solution)/shard_map/attend/pallas_call | solution.py:103
  44.9 5.6 %all-to-all-done.2.hidden_ref = bf16[16,4,512]{2,1,0:T(4,128)(2,1)S(1)} async-done(((bf16[16,4,512]{2,1,0:T(4,128)(2,1)}), bf16[16,4,512]{2,1,0:T(4,128)(2,1)S(1)}, u32[]{:S(2)}, u32[]{:S(2)}) %all-to-all-start.2) | async-done | bytes 65568 | tf_op jit(solution)/shard_map/all_to_all | solution.py:233
  50.5 3.3 %all-to-all-start.1 = ((f32[4,72,128]{2,1,0:T(8,128)}), f32[4,72,128]{2,1,0:T(8,128)S(1)}, u32[]{:S(2)}, u32[]{:S(2)}) async-start(f32[4,72,128]{2,1,0:T(8,128)} %attend.1), calls=%async_computation.1 | async-start | bytes 294912 | tf_op jit(solution)/shard_map/all_to_all | solution.py:239
  53.8 0.0 collective-permute-done.other_ref
  53.8 1.4 %project.1 = f32[16,4,512]{2,1,0:T(4,128)} custom-call(s32[3]{0:T(128)S(1)} %pad_add_fusion.place_ref, bf16[16,4,512]{2,1,0:T(4,128)(2,1)S(1)} %all-to-all-done.2.hidden_ref, bf16[4,64,512]{2,1,0:T(8,128)(2,1)S(1)} %all_to_all.25.own_ref, bf16[4,64,512]{2,1,0:T(8,128)(2,1)S(1)} %collective-permute-done.other_ref), custom_call_target="tpu_custom_call" | custom-call | flops 33554432 | bytes 1048576 | tf_op jit(solution)/shard_map/project/pallas_call | solution.py:133
  55.2 4.6 %all-to-all-done.1.parts_ref = f32[4,72,128]{2,1,0:T(8,128)S(1)} async-done(((f32[4,72,128]{2,1,0:T(8,128)}), f32[4,72,128]{2,1,0:T(8,128)S(1)}, u32[]{:S(2)}, u32[]{:S(2)}) %all-to-all-start.1) | async-done | bytes 147488 | tf_op jit(solution)/shard_map/all_to_all | solution.py:239
  59.9 6.7 %all-to-all-start.4 = ((f32[16,4,512]{2,1,0:T(4,128)}), f32[16,4,512]{2,1,0:T(4,128)S(1)}, u32[]{:S(2)}, u32[]{:S(2)}) async-start(f32[16,4,512]{2,1,0:T(4,128)} %project.1), calls=%async_computation.4 | async-start | bytes 262144 | tf_op jit(solution)/shard_map/all_to_all | solution.py:237
  66.6 0.1 fusion
  66.7 0.1 pad_maximum_fusion
  66.8 13.5 %all-to-all-done.4.sums_ref = f32[16,4,512]{2,1,0:T(4,128)S(1)} async-done(((f32[16,4,512]{2,1,0:T(4,128)}), f32[16,4,512]{2,1,0:T(4,128)S(1)}, u32[]{:S(2)}, u32[]{:S(2)}) %all-to-all-start.4) | async-done | bytes 131104 | tf_op jit(solution)/shard_map/all_to_all | solution.py:237
  80.3 1.3 %finish.1 = (bf16[4,1,2048]{2,1,0:T(2,128)(2,1)S(1)}, bf16[4,1,256]{2,1,0:T(2,128)(2,1)S(1)}, bf16[4,1,256]{2,1,0:T(2,128)(2,1)S(1)}) custom-call(f32[4,72,128]{2,1,0:T(8,128)S(1)} %all-to-all-done.1.parts_ref, f32[16,4,512]{2,1,0:T(4,128)S(1)} %all-to-all-done.4.sums_ref, bf16[4,64,128]{2,1,0:T(8,128)(2,1)} %get-tuple-element.5.queries_ref, ...), custom_call_target="tpu_custom_call" | custom-call | tf_op jit(solution)/shard_map/finish/pallas_call | solution.py:202
  81.6 0.6 copy.11
  82.2 0.6 copy.12
  82.8 0.6 copy.13
  (9 shorter events, 0.1 us)
Async XLA Ops:
  0.6 1.1 %copy-start.2 = (bf16[4,1,2048]{2,0,1:T(4,128)(2,1)S(1)}, bf16[4,1,2048]{2,0,1:T(4,128)(2,1)}, u32[]{:S(2)}) copy-start(bf16[4,1,2048]{2,0,1:T(4,128)(2,1)} %param.8) | copy-start | bytes 49156
  0.6 40.7 %copy-start = (bf16[1,512,1024]{2,1,0:T(8,128)(2,1)S(1)}, bf16[1,512,1024]{2,1,0:T(8,128)(2,1)}, u32[]{:S(2)}) copy-start(bf16[1,512,1024]{2,1,0:T(8,128)(2,1)} %keys_ref.1) | copy-start | bytes 3145732
  2.6 10.1 %all-to-all-start = ((bf16[4,64,128]{2,1,0:T(8,128)(2,1)}), bf16[4,64,128]{2,1,0:T(8,128)(2,1)S(1)}, u32[]{:S(2)}, u32[]{:S(2)}) async-start(bf16[4,64,128]{2,1,0:T(8,128)(2,1)} %get-tuple-element.5.queries_ref), calls=%async_computation | async-start | bytes 131072 | tf_op jit(solution)/shard_map/all_to_all | solution.py:234
  23.5 27.0 %all-to-all-start.2 = ((bf16[16,4,512]{2,1,0:T(4,128)(2,1)}), bf16[16,4,512]{2,1,0:T(4,128)(2,1)S(1)}, u32[]{:S(2)}, u32[]{:S(2)}) async-start(bf16[16,4,512]{2,1,0:T(4,128)(2,1)} %get-tuple-element.6), calls=%async_computation.2 | async-start | bytes 131072 | tf_op jit(solution)/shard_map/all_to_all | solution.py:233
  39.3 14.5 %collective-permute-start = (bf16[4,64,512]{2,1,0:T(8,128)(2,1)S(1)}, bf16[4,64,512]{2,1,0:T(8,128)(2,1)S(1)}, u32[]{:S(2)}, u32[]{:S(2)}) collective-permute-start(bf16[4,64,512]{2,1,0:T(8,128)(2,1)S(1)} %all_to_all.25.own_ref), channel_id=1, source_target_pairs={{0,32},{32,0},{1,33},{33,1},{2,34},{34,2},{3,35},{35,3},{4,36},{36... | collective-permute-start | bytes 786440 | tf_op jit(solution)/shard_map/ppermute | solution.py:235
  41.3 1.2 %copy-start.1 = (bf16[1,512,1024]{2,1,0:T(8,128)(2,1)S(1)}, bf16[1,512,1024]{2,1,0:T(8,128)(2,1)}, u32[]{:S(2)}) copy-start(bf16[1,512,1024]{2,1,0:T(8,128)(2,1)} %values_ref.1) | copy-start | bytes 3145732
  50.5 9.4 %all-to-all-start.1 = ((f32[4,72,128]{2,1,0:T(8,128)}), f32[4,72,128]{2,1,0:T(8,128)S(1)}, u32[]{:S(2)}, u32[]{:S(2)}) async-start(f32[4,72,128]{2,1,0:T(8,128)} %attend.1), calls=%async_computation.1 | async-start | bytes 294912 | tf_op jit(solution)/shard_map/all_to_all | solution.py:239
  59.9 20.4 %all-to-all-start.4 = ((f32[16,4,512]{2,1,0:T(4,128)}), f32[16,4,512]{2,1,0:T(4,128)S(1)}, u32[]{:S(2)}, u32[]{:S(2)}) async-start(f32[16,4,512]{2,1,0:T(4,128)} %project.1), calls=%async_computation.4 | async-start | bytes 262144 | tf_op jit(solution)/shard_map/all_to_all | solution.py:237

commit v2 on v1

v2 whole, which is shorter than its diff:
```python
import jax
import jax.numpy as jnp
from jax import lax
from jax.experimental import pallas as pl
from jax.experimental.pallas import tpu as pltpu
from jax.sharding import Mesh
from jax.sharding import PartitionSpec as P

KVH = 8
HQ = 64
HD = 128
STEPS = 4
GROUP = HQ // KVH
TENSOR = 4
LOCAL_HEADS = KVH // TENSOR
HEAD_ROWS = STEPS * GROUP
OWN_ROWS = LOCAL_HEADS * HEAD_ROWS
ROPE_BASE = 500000.0
NEG_FILL = -1e30
F32 = jnp.float32
BF16 = jnp.bfloat16
PARAMS = pltpu.CompilerParams(vmem_limit_bytes=16 * 1024 * 1024)
WIDE = pltpu.CompilerParams(vmem_limit_bytes=66_100_000)
ROWS_AXES = ("zlo", "core", "x", "zhi")
Z_AXES = ("zhi", "zlo")
Z_FIRST = 12
Z_GROUPS = [[(Z_FIRST + i) % 16 for i in range(16)]]


def lane_iota(shape):
    return lax.broadcasted_iota(jnp.int32, shape, 1)


SMEM = pl.BlockSpec(memory_space=pltpu.SMEM)
VMEM = pl.BlockSpec(memory_space=pltpu.VMEM)
HBM = pl.BlockSpec(memory_space=pltpu.HBM)


def gate(values, *after):
    return lax.optimization_barrier((values, *after))[0]


def prepare_kernel(
    hidden_hbm, queries_hbm, hidden_out, queries_out, rows, hidden_ref, queries_ref, sems
):
    query_copy = pltpu.make_async_copy(queries_hbm, queries_ref, sems.at[0])
    hidden_copy = pltpu.make_async_copy(hidden_hbm, hidden_ref, sems.at[1])
    query_copy.start()
    hidden_copy.start()
    query_copy.wait()
    for head in range(LOCAL_HEADS):
        for member in range(GROUP):
            at = (head * GROUP + member) * HD
            piece = queries_ref[:, at : at + HD].astype(F32)
            for step in range(STEPS):
                row = head * HEAD_ROWS + step * GROUP + member
                rows[row : row + 1, :] = piece[step : step + 1, :]
    queries_out[...] = rows[...].astype(BF16)
    hidden_copy.wait()
    low = lane_iota((STEPS, 128)) < 64
    for zlo in range(8):
        for pair in range(4):
            at = zlo * 1024 + pair * 256
            one = hidden_ref[:, at : at + 128].astype(F32)
            two = hidden_ref[:, at + 128 : at + 256].astype(F32)
            to = slice(pair * 128, pair * 128 + 128)
            even = jnp.where(low, one, pltpu.roll(two, 64, 1)).astype(BF16)
            odd = jnp.where(low, pltpu.roll(one, 64, 1), two).astype(BF16)
            hidden_out[(zlo - Z_FIRST) % 16, :, to] = even
            hidden_out[(8 + zlo - Z_FIRST) % 16, :, to] = odd


def prepare(hidden, queries):
    return pl.pallas_call(
        prepare_kernel,
        out_shape=(
            jax.ShapeDtypeStruct((16, STEPS, 512), BF16),
            jax.ShapeDtypeStruct((OWN_ROWS, HD), BF16),
        ),
        in_specs=[HBM, HBM],
        out_specs=(VMEM, VMEM),
        scratch_shapes=[
            pltpu.VMEM((OWN_ROWS, HD), F32),
            pltpu.VMEM(hidden.shape, BF16),
            pltpu.VMEM(queries.shape, BF16),
            pltpu.SemaphoreType.DMA((2,)),
        ],
        compiler_params=WIDE,
        cost_estimate=pl.CostEstimate(flops=1 << 16, bytes_accessed=1 << 18, transcendentals=0),
        name="prepare",
    )(hidden, queries)


ORDER = (0, 1, 3, 2)


def attend_kernel(
    place_ref, near_ref, far_ref, keys_ref, values_ref, kept_ref, sent_ref, spread
):
    tensor = place_ref[0]
    spread[...] = jnp.zeros_like(spread)
    starts = []
    for k in range(TENSOR):
        start = (tensor ^ ORDER[k]) * (LOCAL_HEADS * HD)
        starts.append(start)
        for head in range(LOCAL_HEADS):
            lanes = pl.ds(pl.multiple_of(start + head * HD, HD), HD)
            at = (k % 2) * OWN_ROWS + head * HEAD_ROWS
            to = k * OWN_ROWS + head * HEAD_ROWS
            piece = (near_ref, far_ref)[k // 2][at : at + HEAD_ROWS, :]
            spread[to : to + HEAD_ROWS, lanes] = piece
    scores = lax.dot_general(
        keys_ref[0], spread[...], (((1,), (1,)), ((), ())), preferred_element_type=F32
    ) * (HD**-0.5)
    held = scores.shape[0]
    position = tensor * held + lax.broadcasted_iota(jnp.int32, scores.shape, 0)
    allowed = position < place_ref[1]
    masked = jnp.where(allowed, scores, NEG_FILL)
    maxima = jnp.max(masked, axis=0, keepdims=True)
    weights = jnp.where(allowed, jnp.exp(masked - maxima), 0.0)
    totals = jnp.sum(weights, axis=0, keepdims=True)
    rounded = weights.astype(BF16)
    for half, out_ref in enumerate((kept_ref, sent_ref)):
        span = slice(half * 128, half * 128 + 128)
        values = jnp.concatenate(
            [
                values_ref[0, :, pl.ds(pl.multiple_of(starts[2 * half + n], 256), 256)]
                for n in range(2)
            ],
            axis=1,
        )
        summed = lax.dot_general(
            rounded[:, span], values, (((0,), (0,)), ((), ())), preferred_element_type=F32
        )
        pair = jnp.concatenate([maxima[:, span], totals[:, span]], axis=0)
        for n in range(2):
            for head in range(LOCAL_HEADS):
                at = n * LOCAL_HEADS + head
                out_ref[n, head * HEAD_ROWS : (head + 1) * HEAD_ROWS, :] = summed[
                    at * HEAD_ROWS : (at + 1) * HEAD_ROWS, at * HD : (at + 1) * HD
                ]
            out_ref[n, OWN_ROWS : OWN_ROWS + 2, :] = pltpu.roll(pair, 64, 1) if n else pair


def attend(place, near, far, keys, values):
    return pl.pallas_call(
        attend_kernel,
        out_shape=(jax.ShapeDtypeStruct((2, OWN_ROWS + 8, HD), F32),) * 2,
        in_specs=[SMEM, VMEM, VMEM, VMEM, VMEM],
        out_specs=(VMEM, VMEM),
        scratch_shapes=[pltpu.VMEM((KVH * HEAD_ROWS, KVH * HD), BF16)],
        compiler_params=PARAMS,
        cost_estimate=pl.CostEstimate(flops=1, bytes_accessed=1, transcendentals=0),
        name="attend",
    )(place, near, far, keys, values)


def merge_kernel(kept_ref, come_ref, own_ref, next_ref):
    rows = []
    for n in range(2):
        stats = [ref[n, OWN_ROWS : OWN_ROWS + 2, :] for ref in (kept_ref, come_ref)]
        joined = jnp.maximum(stats[0][:1], stats[1][:1])
        scales = [jnp.exp(stat[:1] - joined) for stat in stats]
        total = stats[0][1:] * scales[0] + stats[1][1:] * scales[1]
        out_ref = (own_ref, next_ref)[n]
        out_ref[OWN_ROWS : OWN_ROWS + 2, :] = jnp.concatenate([joined, total], axis=0)
        rows += scales
    columns = jnp.transpose(jnp.concatenate(rows + rows, axis=0), (1, 0))
    for n in range(2):
        out_ref = (own_ref, next_ref)[n]
        out_ref[:OWN_ROWS, :] = (
            kept_ref[n, :OWN_ROWS, :] * columns[:OWN_ROWS, 2 * n : 2 * n + 1]
            + come_ref[n, :OWN_ROWS, :] * columns[:OWN_ROWS, 2 * n + 1 : 2 * n + 2]
        )


def merge(kept, come):
    return pl.pallas_call(
        merge_kernel,
        out_shape=(jax.ShapeDtypeStruct((OWN_ROWS + 8, HD), F32),) * 2,
        in_specs=[VMEM, VMEM],
        out_specs=(VMEM, VMEM),
        compiler_params=PARAMS,
        cost_estimate=pl.CostEstimate(
            flops=1 << 17, bytes_accessed=1 << 18, transcendentals=1 << 9
        ),
        name="merge",
    )(kept, come)


def project_kernel(place_ref, hidden_ref, own_ref, other_ref, out_ref, tokens):
    core = place_ref[2]
    x = place_ref[3]
    odd = x % 2 == 1
    for z in range(16):
        tokens[z * STEPS : (z + 1) * STEPS, :] = hidden_ref[z].astype(F32)
    partial = jnp.zeros((16 * STEPS, 512), F32)
    for swap, weight_ref in enumerate((own_ref, other_ref)):
        for pair in range(2):
            at = (core ^ swap) * 256 + ((x // 2) ^ pair) * 128
            block = tokens[:, pl.ds(pl.multiple_of(at, 128), 128)]
            turned = pltpu.roll(block, 64, 1)
            block = jnp.where(odd, *((block, turned) if pair else (turned, block)))
            partial += jnp.dot(
                block.astype(BF16),
                weight_ref[pair * 128 : pair * 128 + 128, :],
                preferred_element_type=F32,
            )
    for z in range(16):
        out_ref[z] = partial[z * STEPS : (z + 1) * STEPS, :]


def project(place, hidden, own, other):
    return pl.pallas_call(
        project_kernel,
        out_shape=jax.ShapeDtypeStruct((16, STEPS, 512), F32),
        in_specs=[SMEM, VMEM, VMEM, VMEM],
        out_specs=VMEM,
        scratch_shapes=[pltpu.VMEM((64, 512), F32)],
        compiler_params=PARAMS,
        cost_estimate=pl.CostEstimate(
            flops=2 * 64 * 512 * 512, bytes_accessed=1 << 20, transcendentals=0
        ),
        name="project",
    )(place, hidden, own, other)


def finish_kernel(
    part0_ref,
    part1_ref,
    sums_ref,
    queries_ref,
    cos_ref,
    sin_ref,
    attended_ref,
    keys_ref,
    values_ref,
    wide,
):
    parts = (part0_ref, part1_ref)
    projected = jnp.sum(sums_ref[...], axis=0)
    cos_part = cos_ref[...]
    sin_part = sin_ref[...]
    new_values = projected[:, LOCAL_HEADS * HD :].astype(BF16)
    values_ref[...] = new_values
    queries = queries_ref[:OWN_ROWS]
    fresh = []
    for head in range(LOCAL_HEADS):
        front = projected[:, head * HD : (head + 1) * HD]
        turned = (front * cos_part + pltpu.roll(front, HD // 2, 1) * sin_part).astype(BF16)
        keys_ref[:, head * HD : (head + 1) * HD] = turned
        fresh.append(
            lax.dot_general(
                turned, queries, (((1,), (1,)), ((), ())), preferred_element_type=F32
            )
        )
    lane = lane_iota((STEPS, OWN_ROWS))
    scores = jnp.where(lane < HEAD_ROWS, fresh[0], fresh[1]) * (HD**-0.5)
    step = (lane % HEAD_ROWS) // GROUP
    allowed = lax.broadcasted_iota(jnp.int32, (STEPS, OWN_ROWS), 0) <= step
    masked = jnp.where(allowed, scores, NEG_FILL)
    maxima = [part[OWN_ROWS : OWN_ROWS + 1, :OWN_ROWS] for part in parts]
    joined = jnp.max(masked, axis=0, keepdims=True)
    for part in maxima:
        joined = jnp.maximum(joined, part)
    weights = jnp.where(allowed, jnp.exp(masked - joined), 0.0)
    totals = jnp.sum(weights, axis=0, keepdims=True)
    scales = []
    for t in range(len(parts)):
        scale = jnp.exp(maxima[t] - joined)
        totals += parts[t][OWN_ROWS + 1 : OWN_ROWS + 2, :OWN_ROWS] * scale
        scales.append(scale)
    factors = jnp.concatenate([*scales, weights.astype(BF16).astype(F32)], axis=0) / totals
    factors = jnp.concatenate([factors, jnp.zeros((6, 128 - OWN_ROWS), F32)], axis=1)
    factors = jnp.concatenate([factors, jnp.zeros((2, 128), F32)], axis=0)
    columns = jnp.transpose(factors, (1, 0))
    values = new_values.astype(F32)
    for head in range(LOCAL_HEADS):
        rows = slice(head * HEAD_ROWS, (head + 1) * HEAD_ROWS)
        total = jnp.zeros((HEAD_ROWS, HD), F32)
        for t in range(len(parts)):
            total += parts[t][rows, :] * columns[rows, t : t + 1]
        for t in range(STEPS):
            total += columns[rows, 2 + t : 3 + t] * values[t : t + 1, head * HD : (head + 1) * HD]
        for s in range(STEPS):
            for member in range(GROUP):
                at = (head * GROUP + member) * HD
                row = s * GROUP + member
                wide[s : s + 1, at : at + HD] = total[row : row + 1, :]
    attended_ref[...] = wide[...].astype(BF16)


def finish(parts, sums, queries, cos_part, sin_part):
    return pl.pallas_call(
        finish_kernel,
        out_shape=(
            jax.ShapeDtypeStruct((STEPS, LOCAL_HEADS * GROUP * HD), BF16),
            jax.ShapeDtypeStruct((STEPS, LOCAL_HEADS * HD), BF16),
            jax.ShapeDtypeStruct((STEPS, LOCAL_HEADS * HD), BF16),
        ),
        in_specs=[VMEM] * 6,
        out_specs=(VMEM,) * 3,
        scratch_shapes=[pltpu.VMEM((STEPS, LOCAL_HEADS * GROUP * HD), F32)],
        compiler_params=PARAMS,
        cost_estimate=pl.CostEstimate(
            flops=1 << 20, bytes_accessed=1 << 19, transcendentals=1 << 10
        ),
        name="finish",
    )(*parts, sums, queries, cos_part, sin_part)


def rotation(lengths):
    half = HD // 2
    positions = lengths[None, :] + jnp.arange(STEPS, dtype=jnp.int32)[:, None]
    frequency = ROPE_BASE ** (-jnp.arange(half, dtype=F32) * 2.0 / HD)
    phases = positions.astype(F32) * frequency[None, :]
    cos_part = jnp.cos(phases)
    sin_part = jnp.sin(phases)
    return (
        jnp.concatenate([cos_part, cos_part], axis=-1),
        jnp.concatenate([-sin_part, sin_part], axis=-1),
    )


def exchange_z(blocks):
    return lax.all_to_all(blocks, Z_AXES, 0, 0, axis_index_groups=Z_GROUPS)


def with_partner(values, axis, flip, size=4):
    return lax.ppermute(values, axis, [(i, i ^ flip) for i in range(size)])


def body(hidden, kv_weight, queries, key_cache, value_cache, lengths):
    place = jnp.stack(
        [lax.axis_index("tensor"), lengths[0], lax.axis_index("core"), lax.axis_index("x")]
    )
    chunks, own_queries = prepare(hidden.reshape(STEPS, -1), queries.reshape(STEPS, -1))
    weight = kv_weight.reshape(64, 512)
    come = with_partner(weight, "x", 1)
    weight = jnp.concatenate([weight, come], axis=0)
    near = jnp.concatenate([own_queries, with_partner(own_queries, "tensor", 1)], axis=0)
    tokens = exchange_z(gate(chunks, come))
    far = with_partner(near, "tensor", 3)
    weight = jnp.concatenate([weight, with_partner(weight, "x", 3)], axis=0)
    kept, sent = attend(place, near, far, key_cache, value_cache)
    other = with_partner(gate(weight, tokens, kept), "core", 1, 2)
    partial = project(place, tokens, weight, other)
    sums = exchange_z(partial)
    own_part, next_part = merge(kept, with_partner(sent, "tensor", 3))
    parts = (own_part, with_partner(next_part, "tensor", 1))
    cos_part, sin_part = rotation(lengths)
    outs = finish(parts, sums, near, cos_part, sin_part)
    return tuple(out.reshape(STEPS, 1, -1) for out in outs)


def solution(mesh):
    split = Mesh(mesh.devices.reshape(8, 2, 4, 4, 2), ("zlo", "core", "tensor", "x", "zhi"))
    return jax.shard_map(
        body,
        mesh=split,
        in_specs=(
            P(None, ROWS_AXES, None),
            P(ROWS_AXES, None, "tensor"),
            P(None, ROWS_AXES, "tensor"),
            P(ROWS_AXES, "tensor", None),
            P(ROWS_AXES, "tensor", None),
            P(ROWS_AXES),
        ),
        out_specs=(
            P(None, ROWS_AXES, "tensor"),
            P(None, ROWS_AXES, "tensor"),
            P(None, ROWS_AXES, "tensor"),
        ),
        check_vma=False,
    )
```

time: 84 us -> 69.7 us (0.83)
  waiting for transfers between devices: 28.5 us -> 9.74 us
  starting transfers between devices: 31.7 us -> 49 us
  blocking collectives: 10.8 us -> 0 us
  local copies, waits for them, and re-layouts: 4.94 us -> 2.51 us
    all_to_all x4 -> x2, waiting for transfers between devices: 28.5 us -> 0.01 us  [exchange_z(): return lax.all_to_all(blocks, Z_AXES, 0, 0, axis_index_groups=Z_GROUPS)]
    ppermute x1 -> x7, starting transfers between devices: 1.92 us -> 21.8 us  [with_partner(): return lax.ppermute(values, axis, [(i, i ^ flip) for i in range(size)])]
    all_to_all x1 -> x0, blocking collectives: 10.8 us -> none  [body(): own = lax.all_to_all(jnp.broadcast_to(weight, (4, 64, 512)), 'x', 0, 0)]
    ppermute x1 -> x7, waiting for transfers between devices: 0.01 us -> 9.74 us  [with_partner(): return lax.ppermute(values, axis, [(i, i ^ flip) for i in range(size)])]
    all_to_all x4 -> x2, starting transfers between devices: 29.7 us -> 27.3 us  [exchange_z(): return lax.all_to_all(blocks, Z_AXES, 0, 0, axis_index_groups=Z_GROUPS)]
    pallas_call x3 -> x0, local copies, waits for them, and re-layouts: 1.78 us -> none  [finish(): pl.pallas_call(finish_kernel, out_shape=(jax.ShapeDtypeStruct((STEPS, 1,...]
    pallas_call x2 -> x3, Pallas kernels: 3.63 us -> 2.95 us  [the longest x1 1.67 us: attend(): pl.pallas_call(attend_kernel, out_shape=(jax.ShapeDtypeStruct((2, OWN_ROW...]
    unnamed x9 -> x12, local copies, waits for them, and re-layouts: 3.14 us -> 2.49 us
  transfers between devices with their start and end apart: 5 -> 9, of which waited for: 4 -> 3; matrix products, arithmetic and copies ran while one was open for 1% -> 0% of each run, Pallas kernels for 4% -> 3%
where the time goes in v2:
time: 69.7 us; the launch traced here: 69.1 us
  starting transfers between devices  49 us (70%)
  waiting for transfers between devices  9.74 us (14%)
  Pallas kernels  6.05 us (9%)
  local copies, waits for them, and re-layouts  2.51 us (4%)
  between operations  1.48 us (2%)
    all_to_all x2, starting transfers between devices, exchange_z(): return lax.all_to_all(blocks, Z_AXES, 0, 0, axis_index_groups=Z_GROUPS)  27.3 us
    ppermute x7, starting transfers between devices, with_partner(): return lax.ppermute(values, axis, [(i, i ^ flip) for i in range(size)])  21.8 us
    ppermute x7, waiting for transfers between devices, with_partner(): return lax.ppermute(values, axis, [(i, i ^ flip) for i in range(size)])  9.74 us
    unnamed x12, local copies, waits for them, and re-layouts  2.49 us
    pallas_call x1, Pallas kernels, attend(): pl.pallas_call(attend_kernel, out_shape=(jax.ShapeDtypeStruct((2, OWN_ROW...  1.67 us
    pallas_call x1, Pallas kernels, prepare(): pl.pallas_call(prepare_kernel, out_shape=(jax.ShapeDtypeStruct((16, STEPS...  1.62 us
    pallas_call x1, Pallas kernels, project(): pl.pallas_call(project_kernel, out_shape=jax.ShapeDtypeStruct((16, STEPS,...  1.48 us
  transfers between devices with their start and end apart: 9, of which 3 were waited for; matrix products, arithmetic and copies ran while one was open for 0% of the time, Pallas kernels for 3%

profile of v2, /device:TPU:32, one launch (start us, length us, event | category | flops | bytes accessed | tf_op | source)
XLA Modules:
  0.0 69.1 jit_solution(8536690853307027043)
XLA Ops:
  0.6 1.6 %prepare.1 = (bf16[16,4,512]{2,1,0:T(4,128)(2,1)}, bf16[64,128]{1,0:T(8,128)(2,1)}) custom-call(bf16[4,8192]{1,0:T(4,128)(2,1)} %bitcast.15, bf16[4,2048]{1,0:T(4,128)(2,1)} %bitcast.17), custom_call_target="tpu_custom_call" | custom-call | flops 65536 | bytes 262144 | tf_op jit(solution)/shard_map/prepare/pallas_call | solution.py:74
  2.3 3.5 %collective-permute-start = (bf16[64,128]{1,0:T(8,128)(2,1)}, bf16[64,128]{1,0:T(8,128)(2,1)S(1)}, u32[]{:S(2)}, u32[]{:S(2)}) collective-permute-start(bf16[64,128]{1,0:T(8,128)(2,1)} %get-tuple-element.14), channel_id=1, source_target_pairs={{0,8},{8,0},{16,24},{24,16},{1,9},{9,1},{17,25},{25,17},{2,10},{10... | collective-permute-start | bytes 49160 | tf_op jit(solution)/shard_map/ppermute | solution.py:330
  5.8 0.0 copy-start.3
  5.8 3.4 %collective-permute-start.4 = (bf16[64,512]{1,0:T(8,128)(2,1)S(1)}, bf16[64,512]{1,0:T(8,128)(2,1)S(1)}, u32[]{:S(2)}, u32[]{:S(2)}) collective-permute-start(bf16[64,512]{1,0:T(8,128)(2,1)S(1)} %bitcast.12), channel_id=1, source_target_pairs={{0,2},{2,0},{4,6},{6,4},{1,3},{3,1},{5,7},{7,5},{8,10},{10,8},{12,... | collective-permute-start | bytes 196616 | tf_op jit(solution)/shard_map/ppermute | solution.py:330
  9.9 4.1 %collective-permute-start.1 = (bf16[128,128]{1,0:T(8,128)(2,1)S(1)}, bf16[128,128]{1,0:T(8,128)(2,1)S(1)}, u32[]{:S(2)}, u32[]{:S(2)}) collective-permute-start(bf16[128,128]{1,0:T(8,128)(2,1)S(1)} %constant_dynamic-update-slice_fusion.near_ref.queries_ref), channel_id=1, source_target_pairs={{0,24},{8,16},{16,8},{24,0},{1,25},{9,17},{17,9},{25,1},{2,26},{10... | collective-permute-start | bytes 98312 | tf_op jit(solution)/shard_map/ppermute | solution.py:330
  14.0 0.0 collective-permute-done.4
  14.0 15.2 %all-to-all-start = ((bf16[16,4,512]{2,1,0:T(4,128)(2,1)}), bf16[16,4,512]{2,1,0:T(4,128)(2,1)S(1)}, u32[]{:S(2)}, u32[]{:S(2)}) async-start(bf16[16,4,512]{2,1,0:T(4,128)(2,1)} %get-tuple-element.20), calls=%async_computation | async-start | bytes 131072 | tf_op jit(solution)/shard_map/all_to_all | solution.py:326
  29.3 4.0 %collective-permute-start.5 = (bf16[128,512]{1,0:T(8,128)(2,1)S(1)}, bf16[128,512]{1,0:T(8,128)(2,1)S(1)}, u32[]{:S(2)}, u32[]{:S(2)}) collective-permute-start(bf16[128,512]{1,0:T(8,128)(2,1)S(1)} %pad_maximum_fusion), channel_id=1, source_target_pairs={{0,6},{2,4},{4,2},{6,0},{1,7},{3,5},{5,3},{7,1},{8,14},{10,12},{12... | collective-permute-start | bytes 393224 | tf_op jit(solution)/shard_map/ppermute | solution.py:330
  33.3 0.1 pad_add_fusion.place_ref
  33.4 1.2 %copy-done = bf16[1,512,1024]{2,1,0:T(8,128)(2,1)S(1)} copy-done((bf16[1,512,1024]{2,1,0:T(8,128)(2,1)S(1)}, bf16[1,512,1024]{2,1,0:T(8,128)(2,1)}, u32[]{:S(2)}) %copy-start) | copy-done | bytes 1048600
  34.6 1.2 %copy-done.1 = bf16[1,512,1024]{2,1,0:T(8,128)(2,1)S(1)} copy-done((bf16[1,512,1024]{2,1,0:T(8,128)(2,1)S(1)}, bf16[1,512,1024]{2,1,0:T(8,128)(2,1)}, u32[]{:S(2)}) %copy-start.1) | copy-done | bytes 1048600
  35.8 1.7 %attend.1 = (f32[2,72,128]{2,1,0:T(8,128)S(1)}, f32[2,72,128]{2,1,0:T(8,128)S(1)}) custom-call(s32[4]{0:T(128)S(1)} %pad_add_fusion.place_ref, bf16[128,128]{1,0:T(8,128)(2,1)S(1)} %constant_dynamic-update-slice_fusion.near_ref.queries_ref, bf16[128,128]{1,0:T(8,128)(2,1)S(1)} %collective-permute-done.1.far_ref, bf16[1,512,1024]{2,1,0:T(8,128)(2,1)S(1)} %copy-done, ...), custom_call_target="tpu_custom_call" | custom-call | flops 1 | bytes 1 | tf_op jit(solution)/shard_map/attend/pallas_call | solution.py:146
  37.6 1.9 %collective-permute-start.6 = (bf16[256,512]{1,0:T(8,128)(2,1)S(1)}, bf16[256,512]{1,0:T(8,128)(2,1)S(1)}, u32[]{:S(2)}, u32[]{:S(2)}) collective-permute-start(bf16[256,512]{1,0:T(8,128)(2,1)S(1)} %constant_dynamic-update-slice_fusion.2.own_ref), channel_id=1, source_target_pairs={{0,32},{32,0},{1,33},{33,1},{2,34},{34,2},{3,35},{35,3},{4,36},{36... | collective-permute-start | bytes 786440 | tf_op jit(solution)/shard_map/ppermute | solution.py:330
  39.5 1.5 %collective-permute-done.6.other_ref = bf16[256,512]{1,0:T(8,128)(2,1)S(1)} collective-permute-done((bf16[256,512]{1,0:T(8,128)(2,1)S(1)}, bf16[256,512]{1,0:T(8,128)(2,1)S(1)}, u32[]{:S(2)}, u32[]{:S(2)}) %collective-permute-start.6) | collective-permute-done | bytes 262176 | tf_op jit(solution)/shard_map/ppermute | solution.py:330
  41.0 1.5 %project.1 = f32[16,4,512]{2,1,0:T(4,128)} custom-call(s32[4]{0:T(128)S(1)} %pad_add_fusion.place_ref, bf16[16,4,512]{2,1,0:T(4,128)(2,1)S(1)} %all-to-all-done.hidden_ref, bf16[256,512]{1,0:T(8,128)(2,1)S(1)} %constant_dynamic-update-slice_fusion.2.own_ref, bf16[256,512]{1,0:T(8,128)(2,1)S(1)} %collective-permute-done.6.other_ref), custom_call_target="tpu_custom_call" | custom-call | flops 33554432 | bytes 1048576 | tf_op jit(solution)/shard_map/project/pallas_call | solution.py:214
  42.5 12.0 %all-to-all-start.1 = ((f32[16,4,512]{2,1,0:T(4,128)}), f32[16,4,512]{2,1,0:T(4,128)S(1)}, u32[]{:S(2)}, u32[]{:S(2)}) async-start(f32[16,4,512]{2,1,0:T(4,128)} %project.1), calls=%async_computation.1 | async-start | bytes 262144 | tf_op jit(solution)/shard_map/all_to_all | solution.py:326
  54.5 3.0 %collective-permute-start.2 = (f32[2,72,128]{2,1,0:T(8,128)S(1)}, f32[2,72,128]{2,1,0:T(8,128)S(1)}, u32[]{:S(2)}, u32[]{:S(2)}) collective-permute-start(f32[2,72,128]{2,1,0:T(8,128)S(1)} %get-tuple-element.16), channel_id=1, source_target_pairs={{0,24},{8,16},{16,8},{24,0},{1,25},{9,17},{17,9},{25,1},{2,26},{10... | collective-permute-start | bytes 221192 | tf_op jit(solution)/shard_map/ppermute | solution.py:330
  57.5 0.1 fusion
  57.6 4.4 %collective-permute-done.2.come_ref = f32[2,72,128]{2,1,0:T(8,128)S(1)} collective-permute-done((f32[2,72,128]{2,1,0:T(8,128)S(1)}, f32[2,72,128]{2,1,0:T(8,128)S(1)}, u32[]{:S(2)}, u32[]{:S(2)}) %collective-permute-start.2) | collective-permute-done | bytes 73760 | tf_op jit(solution)/shard_map/ppermute | solution.py:330
  62.0 0.2 merge.1
  62.2 1.9 %collective-permute-start.3 = (f32[72,128]{1,0:T(8,128)S(1)}, f32[72,128]{1,0:T(8,128)S(1)}, u32[]{:S(2)}, u32[]{:S(2)}) collective-permute-start(f32[72,128]{1,0:T(8,128)S(1)} %get-tuple-element.18), channel_id=1, source_target_pairs={{0,8},{8,0},{16,24},{24,16},{1,9},{9,1},{17,25},{25,17},{2,10},{10... | collective-permute-start | bytes 110600 | tf_op jit(solution)/shard_map/ppermute | solution.py:330
  64.1 0.1 pad_maximum_fusion.1
  64.2 3.8 %collective-permute-done.3.part1_ref = f32[72,128]{1,0:T(8,128)S(1)} collective-permute-done((f32[72,128]{1,0:T(8,128)S(1)}, f32[72,128]{1,0:T(8,128)S(1)}, u32[]{:S(2)}, u32[]{:S(2)}) %collective-permute-start.3) | collective-permute-done | bytes 36896 | tf_op jit(solution)/shard_map/ppermute | solution.py:330
  68.0 1.1 %finish.1 = (bf16[4,2048]{1,0:T(4,128)(2,1)}, bf16[4,256]{1,0:T(4,128)(2,1)}, bf16[4,256]{1,0:T(4,128)(2,1)}) custom-call(f32[72,128]{1,0:T(8,128)S(1)} %get-tuple-element.17.part0_ref, f32[72,128]{1,0:T(8,128)S(1)} %collective-permute-done.3.part1_ref, f32[16,4,512]{2,1,0:T(4,128)S(1)} %all-to-all-done.1.sums_ref, ...), custom_call_target="tpu_custom_call" | custom-call | flops 1048576 | bytes 524288 | tf_op jit(solution)/shard_map/finish/pallas_call | solution.py:294
  (19 shorter events, 0.1 us)
Async XLA Ops:
  0.6 5.1 %copy-start.2 = (bf16[64,2,256]{2,1,0:T(2,128)(2,1)S(1)}, bf16[64,2,256]{2,1,0:T(2,128)(2,1)}, u32[]{:S(2)}) copy-start(bf16[64,2,256]{2,1,0:T(2,128)(2,1)} %param.7) | copy-start | bytes 196612
  2.3 7.6 %collective-permute-start = (bf16[64,128]{1,0:T(8,128)(2,1)}, bf16[64,128]{1,0:T(8,128)(2,1)S(1)}, u32[]{:S(2)}, u32[]{:S(2)}) collective-permute-start(bf16[64,128]{1,0:T(8,128)(2,1)} %get-tuple-element.14), channel_id=1, source_target_pairs={{0,8},{8,0},{16,24},{24,16},{1,9},{9,1},{17,25},{25,17},{2,10},{10... | collective-permute-start | bytes 49160 | tf_op jit(solution)/shard_map/ppermute | solution.py:330
  5.8 3.4 %copy-start.3 = (bf16[64,128]{1,0:T(8,128)(2,1)S(1)}, bf16[64,128]{1,0:T(8,128)(2,1)}, u32[]{:S(2)}) copy-start(bf16[64,128]{1,0:T(8,128)(2,1)} %get-tuple-element.14) | copy-start | bytes 49156
  5.8 8.2 %collective-permute-start.4 = (bf16[64,512]{1,0:T(8,128)(2,1)S(1)}, bf16[64,512]{1,0:T(8,128)(2,1)S(1)}, u32[]{:S(2)}, u32[]{:S(2)}) collective-permute-start(bf16[64,512]{1,0:T(8,128)(2,1)S(1)} %bitcast.12), channel_id=1, source_target_pairs={{0,2},{2,0},{4,6},{6,4},{1,3},{3,1},{5,7},{7,5},{8,10},{10,8},{12,... | collective-permute-start | bytes 196616 | tf_op jit(solution)/shard_map/ppermute | solution.py:330
  9.9 23.4 %collective-permute-start.1 = (bf16[128,128]{1,0:T(8,128)(2,1)S(1)}, bf16[128,128]{1,0:T(8,128)(2,1)S(1)}, u32[]{:S(2)}, u32[]{:S(2)}) collective-permute-start(bf16[128,128]{1,0:T(8,128)(2,1)S(1)} %constant_dynamic-update-slice_fusion.near_ref.queries_ref), channel_id=1, source_target_pairs={{0,24},{8,16},{16,8},{24,0},{1,25},{9,17},{17,9},{25,1},{2,26},{10... | collective-permute-start | bytes 98312 | tf_op jit(solution)/shard_map/ppermute | solution.py:330
  14.0 23.5 %all-to-all-start = ((bf16[16,4,512]{2,1,0:T(4,128)(2,1)}), bf16[16,4,512]{2,1,0:T(4,128)(2,1)S(1)}, u32[]{:S(2)}, u32[]{:S(2)}) async-start(bf16[16,4,512]{2,1,0:T(4,128)(2,1)} %get-tuple-element.20), calls=%async_computation | async-start | bytes 131072 | tf_op jit(solution)/shard_map/all_to_all | solution.py:326
  29.3 8.2 %collective-permute-start.5 = (bf16[128,512]{1,0:T(8,128)(2,1)S(1)}, bf16[128,512]{1,0:T(8,128)(2,1)S(1)}, u32[]{:S(2)}, u32[]{:S(2)}) collective-permute-start(bf16[128,512]{1,0:T(8,128)(2,1)S(1)} %pad_maximum_fusion), channel_id=1, source_target_pairs={{0,6},{2,4},{4,2},{6,0},{1,7},{3,5},{5,3},{7,1},{8,14},{10,12},{12... | collective-permute-start | bytes 393224 | tf_op jit(solution)/shard_map/ppermute | solution.py:330
  33.4 1.2 %copy-start = (bf16[1,512,1024]{2,1,0:T(8,128)(2,1)S(1)}, bf16[1,512,1024]{2,1,0:T(8,128)(2,1)}, u32[]{:S(2)}) copy-start(bf16[1,512,1024]{2,1,0:T(8,128)(2,1)} %keys_ref.1) | copy-start | bytes 3145732
  34.6 1.2 %copy-start.1 = (bf16[1,512,1024]{2,1,0:T(8,128)(2,1)S(1)}, bf16[1,512,1024]{2,1,0:T(8,128)(2,1)}, u32[]{:S(2)}) copy-start(bf16[1,512,1024]{2,1,0:T(8,128)(2,1)} %values_ref.1) | copy-start | bytes 3145732
  37.6 3.4 %collective-permute-start.6 = (bf16[256,512]{1,0:T(8,128)(2,1)S(1)}, bf16[256,512]{1,0:T(8,128)(2,1)S(1)}, u32[]{:S(2)}, u32[]{:S(2)}) collective-permute-start(bf16[256,512]{1,0:T(8,128)(2,1)S(1)} %constant_dynamic-update-slice_fusion.2.own_ref), channel_id=1, source_target_pairs={{0,32},{32,0},{1,33},{33,1},{2,34},{34,2},{3,35},{35,3},{4,36},{36... | collective-permute-start | bytes 786440 | tf_op jit(solution)/shard_map/ppermute | solution.py:330
  42.5 25.6 %all-to-all-start.1 = ((f32[16,4,512]{2,1,0:T(4,128)}), f32[16,4,512]{2,1,0:T(4,128)S(1)}, u32[]{:S(2)}, u32[]{:S(2)}) async-start(f32[16,4,512]{2,1,0:T(4,128)} %project.1), calls=%async_computation.1 | async-start | bytes 262144 | tf_op jit(solution)/shard_map/all_to_all | solution.py:326
  54.5 7.5 %collective-permute-start.2 = (f32[2,72,128]{2,1,0:T(8,128)S(1)}, f32[2,72,128]{2,1,0:T(8,128)S(1)}, u32[]{:S(2)}, u32[]{:S(2)}) collective-permute-start(f32[2,72,128]{2,1,0:T(8,128)S(1)} %get-tuple-element.16), channel_id=1, source_target_pairs={{0,24},{8,16},{16,8},{24,0},{1,25},{9,17},{17,9},{25,1},{2,26},{10... | collective-permute-start | bytes 221192 | tf_op jit(solution)/shard_map/ppermute | solution.py:330
  62.2 5.9 %collective-permute-start.3 = (f32[72,128]{1,0:T(8,128)S(1)}, f32[72,128]{1,0:T(8,128)S(1)}, u32[]{:S(2)}, u32[]{:S(2)}) collective-permute-start(f32[72,128]{1,0:T(8,128)S(1)} %get-tuple-element.18), channel_id=1, source_target_pairs={{0,8},{8,0},{16,24},{24,16},{1,9},{9,1},{17,25},{25,17},{2,10},{10... | collective-permute-start | bytes 110600 | tf_op jit(solution)/shard_map/ppermute | solution.py:330

commit v3 on v2

--- a/solution.py
+++ b/solution.py
@@ -20,11 +20,14 @@
 F32 = jnp.float32
 BF16 = jnp.bfloat16
 PARAMS = pltpu.CompilerParams(vmem_limit_bytes=16 * 1024 * 1024)
-WIDE = pltpu.CompilerParams(vmem_limit_bytes=66_100_000)
 ROWS_AXES = ("zlo", "core", "x", "zhi")
 Z_AXES = ("zhi", "zlo")
-Z_FIRST = 12
-Z_GROUPS = [[(Z_FIRST + i) % 16 for i in range(16)]]
+def ring(first):
+    return [(first + hops) % 16 for hops in range(16)]
+
+
+TOKENS_ORDER = ring(11)
+SUMS_ORDER = ring(0)
 
 
 def lane_iota(shape):
@@ -38,6 +41,10 @@
 
 def gate(values, *after):
     return lax.optimization_barrier((values, *after))[0]
+
+
+def in_hbm(array):
+    return pltpu.with_memory_space_constraint(array, pltpu.HBM)
 
 
 def prepare_kernel(
@@ -66,8 +73,8 @@
             to = slice(pair * 128, pair * 128 + 128)
             even = jnp.where(low, one, pltpu.roll(two, 64, 1)).astype(BF16)
             odd = jnp.where(low, pltpu.roll(one, 64, 1), two).astype(BF16)
-            hidden_out[(zlo - Z_FIRST) % 16, :, to] = even
-            hidden_out[(8 + zlo - Z_FIRST) % 16, :, to] = odd
+            hidden_out[TOKENS_ORDER.index(zlo), :, to] = even
+            hidden_out[TOKENS_ORDER.index(8 + zlo), :, to] = odd
 
 
 def prepare(hidden, queries):
@@ -85,19 +92,50 @@
             pltpu.VMEM(queries.shape, BF16),
             pltpu.SemaphoreType.DMA((2,)),
         ],
-        compiler_params=WIDE,
+        compiler_params=PARAMS,
         cost_estimate=pl.CostEstimate(flops=1 << 16, bytes_accessed=1 << 18, transcendentals=0),
         name="prepare",
-    )(hidden, queries)
+    )(in_hbm(hidden), in_hbm(queries))
 
 
 ORDER = (0, 1, 3, 2)
 
 
+def fetch_kernel(keys_hbm, values_hbm, keys_ref, values_ref, sems):
+    copies = (
+        pltpu.make_async_copy(keys_hbm, keys_ref, sems.at[0]),
+        pltpu.make_async_copy(values_hbm, values_ref, sems.at[1]),
+    )
+    for copy in copies:
+        copy.start()
+    for copy in copies:
+        copy.wait()
+
+
+def fetch(keys, values):
+    return pl.pallas_call(
+        fetch_kernel,
+        out_shape=(pltpu.VMEM(keys.shape, BF16), pltpu.VMEM(values.shape, BF16)),
+        in_specs=[HBM, HBM],
+        out_specs=(VMEM, VMEM),
+        scratch_shapes=[pltpu.SemaphoreType.DMA((2,))],
+        compiler_params=PARAMS,
+        cost_estimate=pl.CostEstimate(flops=1, bytes_accessed=1, transcendentals=0),
+        name="fetch",
+    )(in_hbm(keys), in_hbm(values))
+
+
 def attend_kernel(
-    place_ref, near_ref, far_ref, keys_ref, values_ref, kept_ref, sent_ref, spread
+    lengths_ref,
+    near_ref,
+    far_ref,
+    keys_ref,
+    values_ref,
+    kept_ref,
+    sent_ref,
+    spread,
 ):
-    tensor = place_ref[0]
+    tensor = lax.axis_index("tensor")
     spread[...] = jnp.zeros_like(spread)
     starts = []
     for k in range(TENSOR):
@@ -114,7 +152,7 @@
     ) * (HD**-0.5)
     held = scores.shape[0]
     position = tensor * held + lax.broadcasted_iota(jnp.int32, scores.shape, 0)
-    allowed = position < place_ref[1]
+    allowed = position < lengths_ref[...]
     masked = jnp.where(allowed, scores, NEG_FILL)
     maxima = jnp.max(masked, axis=0, keepdims=True)
     weights = jnp.where(allowed, jnp.exp(masked - maxima), 0.0)
@@ -142,17 +180,17 @@
             out_ref[n, OWN_ROWS : OWN_ROWS + 2, :] = pltpu.roll(pair, 64, 1) if n else pair
 
 
-def attend(place, near, far, keys, values):
+def attend(lengths, near, far, keys, values):
     return pl.pallas_call(
         attend_kernel,
         out_shape=(jax.ShapeDtypeStruct((2, OWN_ROWS + 8, HD), F32),) * 2,
-        in_specs=[SMEM, VMEM, VMEM, VMEM, VMEM],
+        in_specs=[VMEM] * 5,
         out_specs=(VMEM, VMEM),
         scratch_shapes=[pltpu.VMEM((KVH * HEAD_ROWS, KVH * HD), BF16)],
         compiler_params=PARAMS,
         cost_estimate=pl.CostEstimate(flops=1, bytes_accessed=1, transcendentals=0),
         name="attend",
-    )(place, near, far, keys, values)
+    )(lengths, near, far, keys, values)
 
 
 def merge_kernel(kept_ref, come_ref, own_ref, next_ref):
@@ -188,9 +226,9 @@
     )(kept, come)
 
 
-def project_kernel(place_ref, hidden_ref, own_ref, other_ref, out_ref, tokens):
-    core = place_ref[2]
-    x = place_ref[3]
+def project_kernel(hidden_ref, own_ref, other_ref, out_ref, tokens):
+    core = lax.axis_index("core")
+    x = lax.axis_index("x")
     odd = x % 2 == 1
     for z in range(16):
         tokens[z * STEPS : (z + 1) * STEPS, :] = hidden_ref[z].astype(F32)
@@ -207,14 +245,15 @@
                 preferred_element_type=F32,
             )
     for z in range(16):
-        out_ref[z] = partial[z * STEPS : (z + 1) * STEPS, :]
-
-
-def project(place, hidden, own, other):
+        at = TOKENS_ORDER.index(z) * STEPS
+        out_ref[SUMS_ORDER.index(z)] = partial[at : at + STEPS, :]
+
+
+def project(hidden, own, other):
     return pl.pallas_call(
         project_kernel,
         out_shape=jax.ShapeDtypeStruct((16, STEPS, 512), F32),
-        in_specs=[SMEM, VMEM, VMEM, VMEM],
+        in_specs=[VMEM, VMEM, VMEM],
         out_specs=VMEM,
         scratch_shapes=[pltpu.VMEM((64, 512), F32)],
         compiler_params=PARAMS,
@@ -222,7 +261,7 @@
             flops=2 * 64 * 512 * 512, bytes_accessed=1 << 20, transcendentals=0
         ),
         name="project",
-    )(place, hidden, own, other)
+    )(hidden, own, other)
 
 
 def finish_kernel(
@@ -322,8 +361,8 @@
     )
 
 
-def exchange_z(blocks):
-    return lax.all_to_all(blocks, Z_AXES, 0, 0, axis_index_groups=Z_GROUPS)
+def exchange_z(blocks, order):
+    return lax.all_to_all(blocks, Z_AXES, 0, 0, axis_index_groups=[order])
 
 
 def with_partner(values, axis, flip, size=4):
@@ -331,21 +370,21 @@
 
 
 def body(hidden, kv_weight, queries, key_cache, value_cache, lengths):
-    place = jnp.stack(
-        [lax.axis_index("tensor"), lengths[0], lax.axis_index("core"), lax.axis_index("x")]
+    weight = kv_weight.reshape(64, 512)
+    chunks, own_queries = prepare(
+        gate(hidden.reshape(STEPS, -1), weight), queries.reshape(STEPS, -1)
     )
-    chunks, own_queries = prepare(hidden.reshape(STEPS, -1), queries.reshape(STEPS, -1))
-    weight = kv_weight.reshape(64, 512)
     come = with_partner(weight, "x", 1)
     weight = jnp.concatenate([weight, come], axis=0)
     near = jnp.concatenate([own_queries, with_partner(own_queries, "tensor", 1)], axis=0)
-    tokens = exchange_z(gate(chunks, come))
+    tokens = exchange_z(gate(chunks, come), TOKENS_ORDER)
     far = with_partner(near, "tensor", 3)
     weight = jnp.concatenate([weight, with_partner(weight, "x", 3)], axis=0)
-    kept, sent = attend(place, near, far, key_cache, value_cache)
-    other = with_partner(gate(weight, tokens, kept), "core", 1, 2)
-    partial = project(place, tokens, weight, other)
-    sums = exchange_z(partial)
+    keys, values = fetch(gate(key_cache, weight), value_cache)
+    kept, sent = attend(jnp.broadcast_to(lengths, (1, KVH * HEAD_ROWS)), near, far, keys, values)
+    other = with_partner(gate(weight, tokens, far, keys), "core", 1, 2)
+    partial = project(tokens, weight, gate(other, kept))
+    sums = exchange_z(partial, SUMS_ORDER)
     own_part, next_part = merge(kept, with_partner(sent, "tensor", 3))
     parts = (own_part, with_partner(next_part, "tensor", 1))
     cos_part, sin_part = rotation(lengths)

time: 69.7 us -> 62.8 us (0.901)
  starting transfers between devices: 49 us -> 43.7 us
  local copies, waits for them, and re-layouts: 2.51 us -> 0.89 us
    all_to_all x2, starting transfers between devices: 27.3 us -> 20.8 us  [exchange_z(): return lax.all_to_all(blocks, Z_AXES, 0, 0, axis_index_groups=[order])]
    unnamed x12 -> x4, local copies, waits for them, and re-layouts: 2.49 us -> 0.87 us
    pallas_call x0 -> x1, Pallas kernels: none -> 1.56 us  [fetch(): pl.pallas_call(fetch_kernel, out_shape=(pltpu.VMEM(keys.shape, BF16), plt...]
    ppermute x7, waiting for transfers between devices: 9.74 us -> 8.41 us  [with_partner(): return lax.ppermute(values, axis, [(i, i ^ flip) for i in range(size)])]
    ppermute x7, starting transfers between devices: 21.8 us -> 22.9 us  [with_partner(): return lax.ppermute(values, axis, [(i, i ^ flip) for i in range(size)])]
    all_to_all x2, waiting for transfers between devices: 0.01 us -> 0.93 us  [exchange_z(): return lax.all_to_all(blocks, Z_AXES, 0, 0, axis_index_groups=[order])]
  transfers between devices with their start and end apart: 9 -> 9, of which waited for: 3 -> 4; matrix products, arithmetic and copies ran while one was open for 0% -> 0% of each run, Pallas kernels for 3% -> 7%
where the time goes in v3:
time: 62.8 us; the launch traced here: 62.2 us
  starting transfers between devices  43.7 us (70%)
  waiting for transfers between devices  9.34 us (15%)
  Pallas kernels  6.58 us (10%)
  between operations  1.45 us (2%)
  local copies, waits for them, and re-layouts  0.89 us (1%)
    ppermute x7, starting transfers between devices, with_partner(): return lax.ppermute(values, axis, [(i, i ^ flip) for i in range(size)])  22.9 us
    all_to_all x2, starting transfers between devices, exchange_z(): return lax.all_to_all(blocks, Z_AXES, 0, 0, axis_index_groups=[order])  20.8 us
    ppermute x7, waiting for transfers between devices, with_partner(): return lax.ppermute(values, axis, [(i, i ^ flip) for i in range(size)])  8.41 us
    pallas_call x1, Pallas kernels, prepare(): pl.pallas_call(prepare_kernel, out_shape=(jax.ShapeDtypeStruct((16, STEPS...  1.61 us
    pallas_call x1, Pallas kernels, fetch(): pl.pallas_call(fetch_kernel, out_shape=(pltpu.VMEM(keys.shape, BF16), plt...  1.56 us
  transfers between devices with their start and end apart: 9, of which 4 were waited for; matrix products, arithmetic and copies ran while one was open for 0% of the time, Pallas kernels for 7%

profile of v3, /device:TPU:32, one launch (start us, length us, event | category | flops | bytes accessed | tf_op | source)
XLA Modules:
  0.0 62.2 jit_solution(7111807531112257989)
XLA Ops:
  0.6 0.8 %copy.9 = bf16[8,8,2,256]{3,1,2,0:T(8,128)(2,1)S(1)} copy(bf16[8,8,2,256]{3,2,1,0:T(2,128)(2,1)} %bitcast.14) | data formatting | bytes 131072
  1.5 3.4 %collective-permute-start.2 = (bf16[64,512]{1,0:T(8,128)(2,1)S(1)}, bf16[64,512]{1,0:T(8,128)(2,1)S(1)}, u32[]{:S(2)}, u32[]{:S(2)}) collective-permute-start(bf16[64,512]{1,0:T(8,128)(2,1)S(1)} %bitcast.10), channel_id=1, source_target_pairs={{0,2},{2,0},{4,6},{6,4},{1,3},{3,1},{5,7},{7,5},{8,10},{10,8},{12,... | collective-permute-start | bytes 196616 | tf_op jit(solution)/shard_map/ppermute | solution.py:369
  4.9 1.6 %prepare.1 = (bf16[16,4,512]{2,1,0:T(4,128)(2,1)}, bf16[64,128]{1,0:T(8,128)(2,1)S(1)}) custom-call(bf16[4,8192]{1,0:T(4,128)(2,1)} %bitcast.13, bf16[4,2048]{1,0:T(4,128)(2,1)} %bitcast.15), custom_call_target="tpu_custom_call" | custom-call | flops 65536 | bytes 262144 | tf_op jit(solution)/shard_map/prepare/pallas_call | solution.py:81
  6.5 3.5 %collective-permute-start = (bf16[64,128]{1,0:T(8,128)(2,1)S(1)}, bf16[64,128]{1,0:T(8,128)(2,1)S(1)}, u32[]{:S(2)}, u32[]{:S(2)}) collective-permute-start(bf16[64,128]{1,0:T(8,128)(2,1)S(1)} %get-tuple-element.20), channel_id=1, source_target_pairs={{0,8},{8,0},{16,24},{24,16},{1,9},{9,1},{17,25},{25,17},{2,10},{10... | collective-permute-start | bytes 49160 | tf_op jit(solution)/shard_map/ppermute | solution.py:369
  10.0 0.0 collective-permute-done.2
  10.0 15.7 %all-to-all-start = ((bf16[16,4,512]{2,1,0:T(4,128)(2,1)}), bf16[16,4,512]{2,1,0:T(4,128)(2,1)S(1)}, u32[]{:S(2)}, u32[]{:S(2)}) async-start(bf16[16,4,512]{2,1,0:T(4,128)(2,1)} %get-tuple-element.29), calls=%async_computation | async-start | bytes 131072 | tf_op jit(solution)/shard_map/all_to_all | solution.py:365
  25.8 4.0 %collective-permute-start.3 = (bf16[128,512]{1,0:T(8,128)(2,1)S(1)}, bf16[128,512]{1,0:T(8,128)(2,1)S(1)}, u32[]{:S(2)}, u32[]{:S(2)}) collective-permute-start(bf16[128,512]{1,0:T(8,128)(2,1)S(1)} %pad_maximum_fusion), channel_id=1, source_target_pairs={{0,6},{2,4},{4,2},{6,0},{1,7},{3,5},{5,3},{7,1},{8,14},{10,12},{12... | collective-permute-start | bytes 393224 | tf_op jit(solution)/shard_map/ppermute | solution.py:369
  29.8 0.0 collective-permute-done
  29.8 4.1 %collective-permute-start.1 = (bf16[128,128]{1,0:T(8,128)(2,1)S(1)}, bf16[128,128]{1,0:T(8,128)(2,1)S(1)}, u32[]{:S(2)}, u32[]{:S(2)}) collective-permute-start(bf16[128,128]{1,0:T(8,128)(2,1)S(1)} %constant_dynamic-update-slice_fusion.near_ref.queries_ref), channel_id=1, source_target_pairs={{0,24},{8,16},{16,8},{24,0},{1,25},{9,17},{17,9},{25,1},{2,26},{10... | collective-permute-start | bytes 98312 | tf_op jit(solution)/shard_map/ppermute | solution.py:369
  33.9 1.6 %fetch.1 = (bf16[1,512,1024]{2,1,0:T(8,128)(2,1)S(1)}, bf16[1,512,1024]{2,1,0:T(8,128)(2,1)S(1)}) custom-call(bf16[1,512,1024]{2,1,0:T(8,128)(2,1)} %keys_hbm, bf16[1,512,1024]{2,1,0:T(8,128)(2,1)} %values_hbm.1), custom_call_target="tpu_custom_call" | custom-call | flops 1 | bytes 1 | tf_op jit(solution)/shard_map/fetch/pallas_call | solution.py:116
  35.5 1.3 %collective-permute-done.1.far_ref = bf16[128,128]{1,0:T(8,128)(2,1)S(1)} collective-permute-done((bf16[128,128]{1,0:T(8,128)(2,1)S(1)}, bf16[128,128]{1,0:T(8,128)(2,1)S(1)}, u32[]{:S(2)}, u32[]{:S(2)}) %collective-permute-start.1) | collective-permute-done | bytes 32800 | tf_op jit(solution)/shard_map/ppermute | solution.py:369
  36.8 1.9 %collective-permute-start.6 = (bf16[256,512]{1,0:T(8,128)(2,1)S(1)}, bf16[256,512]{1,0:T(8,128)(2,1)S(1)}, u32[]{:S(2)}, u32[]{:S(2)}) collective-permute-start(bf16[256,512]{1,0:T(8,128)(2,1)S(1)} %constant_dynamic-update-slice_fusion.2.own_ref), channel_id=1, source_target_pairs={{0,32},{32,0},{1,33},{33,1},{2,34},{34,2},{3,35},{35,3},{4,36},{36... | collective-permute-start | bytes 786440 | tf_op jit(solution)/shard_map/ppermute | solution.py:369
  39.4 1.2 %attend.1 = (f32[2,72,128]{2,1,0:T(8,128)S(1)}, f32[2,72,128]{2,1,0:T(8,128)S(1)}) custom-call(s32[1,256]{1,0:T(1,128)S(1)} %broadcast_in_dim.2.lengths_ref, bf16[128,128]{1,0:T(8,128)(2,1)S(1)} %constant_dynamic-update-slice_fusion.near_ref.queries_ref, bf16[128,128]{1,0:T(8,128)(2,1)S(1)} %collective-permute-done.1.far_ref, ...), custom_call_target="tpu_custom_call" | custom-call | flops 1 | bytes 1 | tf_op jit(solution)/shard_map/attend/pallas_call | solution.py:184
  40.6 1.0 %project.1 = f32[16,4,512]{2,1,0:T(4,128)} custom-call(bf16[16,4,512]{2,1,0:T(4,128)(2,1)S(1)} %all-to-all-done.hidden_ref, bf16[256,512]{1,0:T(8,128)(2,1)S(1)} %constant_dynamic-update-slice_fusion.2.own_ref, bf16[256,512]{1,0:T(8,128)(2,1)S(1)} %collective-permute-done.6.other_ref), custom_call_target="tpu_custom_call" | custom-call | flops 33554432 | bytes 1048576 | tf_op jit(solution)/shard_map/project/pallas_call | solution.py:253
  41.5 5.1 %all-to-all-start.1 = ((f32[16,4,512]{2,1,0:T(4,128)}), f32[16,4,512]{2,1,0:T(4,128)S(1)}, u32[]{:S(2)}, u32[]{:S(2)}) async-start(f32[16,4,512]{2,1,0:T(4,128)} %project.1), calls=%async_computation.1 | async-start | bytes 262144 | tf_op jit(solution)/shard_map/all_to_all | solution.py:365
  46.7 4.1 %collective-permute-start.4 = (f32[2,72,128]{2,1,0:T(8,128)S(1)}, f32[2,72,128]{2,1,0:T(8,128)S(1)}, u32[]{:S(2)}, u32[]{:S(2)}) collective-permute-start(f32[2,72,128]{2,1,0:T(8,128)S(1)} %get-tuple-element.25), channel_id=1, source_target_pairs={{0,24},{8,16},{16,8},{24,0},{1,25},{9,17},{17,9},{25,1},{2,26},{10... | collective-permute-start | bytes 221192 | tf_op jit(solution)/shard_map/ppermute | solution.py:369
  50.8 0.1 fusion
  50.9 3.2 %collective-permute-done.4.come_ref = f32[2,72,128]{2,1,0:T(8,128)S(1)} collective-permute-done((f32[2,72,128]{2,1,0:T(8,128)S(1)}, f32[2,72,128]{2,1,0:T(8,128)S(1)}, u32[]{:S(2)}, u32[]{:S(2)}) %collective-permute-start.4) | collective-permute-done | bytes 73760 | tf_op jit(solution)/shard_map/ppermute | solution.py:369
  54.1 0.2 merge.1
  54.4 1.9 %collective-permute-start.5 = (f32[72,128]{1,0:T(8,128)S(1)}, f32[72,128]{1,0:T(8,128)S(1)}, u32[]{:S(2)}, u32[]{:S(2)}) collective-permute-start(f32[72,128]{1,0:T(8,128)S(1)} %get-tuple-element.27), channel_id=1, source_target_pairs={{0,8},{8,0},{16,24},{24,16},{1,9},{9,1},{17,25},{25,17},{2,10},{10... | collective-permute-start | bytes 110600 | tf_op jit(solution)/shard_map/ppermute | solution.py:369
  56.3 0.1 pad_maximum_fusion.1
  56.4 3.8 %collective-permute-done.5.part1_ref = f32[72,128]{1,0:T(8,128)S(1)} collective-permute-done((f32[72,128]{1,0:T(8,128)S(1)}, f32[72,128]{1,0:T(8,128)S(1)}, u32[]{:S(2)}, u32[]{:S(2)}) %collective-permute-start.5) | collective-permute-done | bytes 36896 | tf_op jit(solution)/shard_map/ppermute | solution.py:369
  60.2 0.9 %all-to-all-done.1.sums_ref = f32[16,4,512]{2,1,0:T(4,128)S(1)} async-done(((f32[16,4,512]{2,1,0:T(4,128)}), f32[16,4,512]{2,1,0:T(4,128)S(1)}, u32[]{:S(2)}, u32[]{:S(2)}) %all-to-all-start.1) | async-done | bytes 131104 | tf_op jit(solution)/shard_map/all_to_all | solution.py:365
  61.1 1.1 %finish.1 = (bf16[4,2048]{1,0:T(4,128)(2,1)}, bf16[4,256]{1,0:T(4,128)(2,1)}, bf16[4,256]{1,0:T(4,128)(2,1)}) custom-call(f32[72,128]{1,0:T(8,128)S(1)} %get-tuple-element.26.part0_ref, f32[72,128]{1,0:T(8,128)S(1)} %collective-permute-done.5.part1_ref, f32[16,4,512]{2,1,0:T(4,128)S(1)} %all-to-all-done.1.sums_ref, ...), custom_call_target="tpu_custom_call" | custom-call | flops 1048576 | bytes 524288 | tf_op jit(solution)/shard_map/finish/pallas_call | solution.py:333
  (12 shorter events, 0.1 us)
Async XLA Ops:
  1.5 8.5 %collective-permute-start.2 = (bf16[64,512]{1,0:T(8,128)(2,1)S(1)}, bf16[64,512]{1,0:T(8,128)(2,1)S(1)}, u32[]{:S(2)}, u32[]{:S(2)}) collective-permute-start(bf16[64,512]{1,0:T(8,128)(2,1)S(1)} %bitcast.10), channel_id=1, source_target_pairs={{0,2},{2,0},{4,6},{6,4},{1,3},{3,1},{5,7},{7,5},{8,10},{10,8},{12,... | collective-permute-start | bytes 196616 | tf_op jit(solution)/shard_map/ppermute | solution.py:369
  6.5 23.3 %collective-permute-start = (bf16[64,128]{1,0:T(8,128)(2,1)S(1)}, bf16[64,128]{1,0:T(8,128)(2,1)S(1)}, u32[]{:S(2)}, u32[]{:S(2)}) collective-permute-start(bf16[64,128]{1,0:T(8,128)(2,1)S(1)} %get-tuple-element.20), channel_id=1, source_target_pairs={{0,8},{8,0},{16,24},{24,16},{1,9},{9,1},{17,25},{25,17},{2,10},{10... | collective-permute-start | bytes 49160 | tf_op jit(solution)/shard_map/ppermute | solution.py:369
  10.0 26.8 %all-to-all-start = ((bf16[16,4,512]{2,1,0:T(4,128)(2,1)}), bf16[16,4,512]{2,1,0:T(4,128)(2,1)S(1)}, u32[]{:S(2)}, u32[]{:S(2)}) async-start(bf16[16,4,512]{2,1,0:T(4,128)(2,1)} %get-tuple-element.29), calls=%async_computation | async-start | bytes 131072 | tf_op jit(solution)/shard_map/all_to_all | solution.py:365
  25.8 8.2 %collective-permute-start.3 = (bf16[128,512]{1,0:T(8,128)(2,1)S(1)}, bf16[128,512]{1,0:T(8,128)(2,1)S(1)}, u32[]{:S(2)}, u32[]{:S(2)}) collective-permute-start(bf16[128,512]{1,0:T(8,128)(2,1)S(1)} %pad_maximum_fusion), channel_id=1, source_target_pairs={{0,6},{2,4},{4,2},{6,0},{1,7},{3,5},{5,3},{7,1},{8,14},{10,12},{12... | collective-permute-start | bytes 393224 | tf_op jit(solution)/shard_map/ppermute | solution.py:369
  29.8 7.0 %collective-permute-start.1 = (bf16[128,128]{1,0:T(8,128)(2,1)S(1)}, bf16[128,128]{1,0:T(8,128)(2,1)S(1)}, u32[]{:S(2)}, u32[]{:S(2)}) collective-permute-start(bf16[128,128]{1,0:T(8,128)(2,1)S(1)} %constant_dynamic-update-slice_fusion.near_ref.queries_ref), channel_id=1, source_target_pairs={{0,24},{8,16},{16,8},{24,0},{1,25},{9,17},{17,9},{25,1},{2,26},{10... | collective-permute-start | bytes 98312 | tf_op jit(solution)/shard_map/ppermute | solution.py:369
  36.8 3.8 %collective-permute-start.6 = (bf16[256,512]{1,0:T(8,128)(2,1)S(1)}, bf16[256,512]{1,0:T(8,128)(2,1)S(1)}, u32[]{:S(2)}, u32[]{:S(2)}) collective-permute-start(bf16[256,512]{1,0:T(8,128)(2,1)S(1)} %constant_dynamic-update-slice_fusion.2.own_ref), channel_id=1, source_target_pairs={{0,32},{32,0},{1,33},{33,1},{2,34},{34,2},{3,35},{35,3},{4,36},{36... | collective-permute-start | bytes 786440 | tf_op jit(solution)/shard_map/ppermute | solution.py:369
  41.5 19.6 %all-to-all-start.1 = ((f32[16,4,512]{2,1,0:T(4,128)}), f32[16,4,512]{2,1,0:T(4,128)S(1)}, u32[]{:S(2)}, u32[]{:S(2)}) async-start(f32[16,4,512]{2,1,0:T(4,128)} %project.1), calls=%async_computation.1 | async-start | bytes 262144 | tf_op jit(solution)/shard_map/all_to_all | solution.py:365
  46.7 7.5 %collective-permute-start.4 = (f32[2,72,128]{2,1,0:T(8,128)S(1)}, f32[2,72,128]{2,1,0:T(8,128)S(1)}, u32[]{:S(2)}, u32[]{:S(2)}) collective-permute-start(f32[2,72,128]{2,1,0:T(8,128)S(1)} %get-tuple-element.25), channel_id=1, source_target_pairs={{0,24},{8,16},{16,8},{24,0},{1,25},{9,17},{17,9},{25,1},{2,26},{10... | collective-permute-start | bytes 221192 | tf_op jit(solution)/shard_map/ppermute | solution.py:369
  54.4 5.9 %collective-permute-start.5 = (f32[72,128]{1,0:T(8,128)S(1)}, f32[72,128]{1,0:T(8,128)S(1)}, u32[]{:S(2)}, u32[]{:S(2)}) collective-permute-start(f32[72,128]{1,0:T(8,128)S(1)} %get-tuple-element.27), channel_id=1, source_target_pairs={{0,8},{8,0},{16,24},{24,16},{1,9},{9,1},{17,25},{25,17},{2,10},{10... | collective-permute-start | bytes 110600 | tf_op jit(solution)/shard_map/ppermute | solution.py:369

commit v4 on v3

--- a/solution.py
+++ b/solution.py
@@ -15,6 +15,7 @@
 LOCAL_HEADS = KVH // TENSOR
 HEAD_ROWS = STEPS * GROUP
 OWN_ROWS = LOCAL_HEADS * HEAD_ROWS
+WIDTH = LOCAL_HEADS * HD
 ROPE_BASE = 500000.0
 NEG_FILL = -1e30
 F32 = jnp.float32
@@ -99,6 +100,34 @@
 
 
 ORDER = (0, 1, 3, 2)
+
+
+PART = (OWN_ROWS + 8, HD)
+PACKED = (OWN_ROWS + 16, HD)
+
+
+def store_part(ref, summed, stat):
+    ref[:OWN_ROWS, :] = summed
+    ref[OWN_ROWS : OWN_ROWS + 1, :] = stat
+
+
+def pack_part(ref, summed, stat):
+    ref[:OWN_ROWS, :] = summed.astype(BF16)
+    terms = []
+    for _ in range(3):
+        terms.append(stat.astype(BF16).astype(F32))
+        stat = stat - terms[-1]
+    rest = jnp.zeros((PACKED[0] - OWN_ROWS - 3, HD), F32)
+    ref[OWN_ROWS:, :] = jnp.concatenate([*terms, rest], axis=0).astype(BF16)
+
+
+def load_part(ref):
+    return ref[:OWN_ROWS, :], ref[OWN_ROWS : OWN_ROWS + 1, :]
+
+
+def unpack_part(ref):
+    stat = jnp.sum(ref[OWN_ROWS:, :].astype(F32), axis=0, keepdims=True)
+    return ref[:OWN_ROWS, :].astype(F32), stat
 
 
 def fetch_kernel(keys_hbm, values_hbm, keys_ref, values_ref, sems):
@@ -170,20 +199,32 @@
         summed = lax.dot_general(
             rounded[:, span], values, (((0,), (0,)), ((), ())), preferred_element_type=F32
         )
-        pair = jnp.concatenate([maxima[:, span], totals[:, span]], axis=0)
+        low = lane_iota((1, 128)) < OWN_ROWS
         for n in range(2):
+            blocks = []
             for head in range(LOCAL_HEADS):
                 at = n * LOCAL_HEADS + head
-                out_ref[n, head * HEAD_ROWS : (head + 1) * HEAD_ROWS, :] = summed[
-                    at * HEAD_ROWS : (at + 1) * HEAD_ROWS, at * HD : (at + 1) * HD
-                ]
-            out_ref[n, OWN_ROWS : OWN_ROWS + 2, :] = pltpu.roll(pair, 64, 1) if n else pair
+                blocks.append(
+                    summed[
+                        at * HEAD_ROWS : (at + 1) * HEAD_ROWS, at * HD : (at + 1) * HD
+                    ]
+                )
+            stats = (maxima[:, span], totals[:, span])
+            turned = [pltpu.roll(stat, OWN_ROWS, 1) for stat in stats]
+            stat = jnp.where(low, *((turned[0], stats[1]) if n else (stats[0], turned[1])))
+            if half == 0:
+                store_part(kept_ref.at[n], jnp.concatenate(blocks, axis=0), stat)
+            else:
+                pack_part(sent_ref.at[n], jnp.concatenate(blocks, axis=0), stat)
 
 
 def attend(lengths, near, far, keys, values):
     return pl.pallas_call(
         attend_kernel,
-        out_shape=(jax.ShapeDtypeStruct((2, OWN_ROWS + 8, HD), F32),) * 2,
+        out_shape=(
+            jax.ShapeDtypeStruct((2, *PART), F32),
+            jax.ShapeDtypeStruct((2, *PACKED), BF16),
+        ),
         in_specs=[VMEM] * 5,
         out_specs=(VMEM, VMEM),
         scratch_shapes=[pltpu.VMEM((KVH * HEAD_ROWS, KVH * HD), BF16)],
@@ -194,28 +235,32 @@
 
 
 def merge_kernel(kept_ref, come_ref, own_ref, next_ref):
-    rows = []
+    low = lane_iota((1, 128)) < OWN_ROWS
+    summed, rows, stats = [], [], []
     for n in range(2):
-        stats = [ref[n, OWN_ROWS : OWN_ROWS + 2, :] for ref in (kept_ref, come_ref)]
-        joined = jnp.maximum(stats[0][:1], stats[1][:1])
-        scales = [jnp.exp(stat[:1] - joined) for stat in stats]
-        total = stats[0][1:] * scales[0] + stats[1][1:] * scales[1]
-        out_ref = (own_ref, next_ref)[n]
-        out_ref[OWN_ROWS : OWN_ROWS + 2, :] = jnp.concatenate([joined, total], axis=0)
+        parts = (load_part(kept_ref.at[n]), unpack_part(come_ref.at[n]))
+        joined = jnp.maximum(parts[0][1], parts[1][1])
+        scales = [jnp.exp(stat - joined) for _, stat in parts]
+        total = sum(
+            stat * pltpu.roll(scale, OWN_ROWS, 1) for (_, stat), scale in zip(parts, scales)
+        )
+        summed.append([part for part, _ in parts])
         rows += scales
+        stats.append(jnp.where(low, joined, total))
     columns = jnp.transpose(jnp.concatenate(rows + rows, axis=0), (1, 0))
-    for n in range(2):
-        out_ref = (own_ref, next_ref)[n]
-        out_ref[:OWN_ROWS, :] = (
-            kept_ref[n, :OWN_ROWS, :] * columns[:OWN_ROWS, 2 * n : 2 * n + 1]
-            + come_ref[n, :OWN_ROWS, :] * columns[:OWN_ROWS, 2 * n + 1 : 2 * n + 2]
-        )
+    merged = [
+        summed[n][0] * columns[:OWN_ROWS, 2 * n : 2 * n + 1]
+        + summed[n][1] * columns[:OWN_ROWS, 2 * n + 1 : 2 * n + 2]
+        for n in range(2)
+    ]
+    store_part(own_ref, merged[0], stats[0])
+    pack_part(next_ref, merged[1], stats[1])
 
 
 def merge(kept, come):
     return pl.pallas_call(
         merge_kernel,
-        out_shape=(jax.ShapeDtypeStruct((OWN_ROWS + 8, HD), F32),) * 2,
+        out_shape=(jax.ShapeDtypeStruct(PART, F32), jax.ShapeDtypeStruct(PACKED, BF16)),
         in_specs=[VMEM, VMEM],
         out_specs=(VMEM, VMEM),
         compiler_params=PARAMS,
@@ -244,15 +289,18 @@
                 weight_ref[pair * 128 : pair * 128 + 128, :],
                 preferred_element_type=F32,
             )
+    leading = partial.astype(BF16).astype(F32)
+    trailing = (partial - leading)[:, :WIDTH]
     for z in range(16):
         at = TOKENS_ORDER.index(z) * STEPS
-        out_ref[SUMS_ORDER.index(z)] = partial[at : at + STEPS, :]
+        out_ref[SUMS_ORDER.index(z), :, : 2 * WIDTH] = leading[at : at + STEPS, :].astype(BF16)
+        out_ref[SUMS_ORDER.index(z), :, 2 * WIDTH :] = trailing[at : at + STEPS, :].astype(BF16)
 
 
 def project(hidden, own, other):
     return pl.pallas_call(
         project_kernel,
-        out_shape=jax.ShapeDtypeStruct((16, STEPS, 512), F32),
+        out_shape=jax.ShapeDtypeStruct((16, STEPS, 3 * WIDTH), BF16),
         in_specs=[VMEM, VMEM, VMEM],
         out_specs=VMEM,
         scratch_shapes=[pltpu.VMEM((64, 512), F32)],
@@ -276,16 +324,17 @@
     values_ref,
     wide,
 ):
-    parts = (part0_ref, part1_ref)
-    projected = jnp.sum(sums_ref[...], axis=0)
+    parts = (load_part(part0_ref), unpack_part(part1_ref))
+    projected = jnp.sum(sums_ref[...].astype(F32), axis=0)
+    new_keys = projected[:, :WIDTH] + projected[:, 2 * WIDTH :]
     cos_part = cos_ref[...]
     sin_part = sin_ref[...]
-    new_values = projected[:, LOCAL_HEADS * HD :].astype(BF16)
+    new_values = projected[:, WIDTH : 2 * WIDTH].astype(BF16)
     values_ref[...] = new_values
     queries = queries_ref[:OWN_ROWS]
     fresh = []
     for head in range(LOCAL_HEADS):
-        front = projected[:, head * HD : (head + 1) * HD]
+        front = new_keys[:, head * HD : (head + 1) * HD]
         turned = (front * cos_part + pltpu.roll(front, HD // 2, 1) * sin_part).astype(BF16)
         keys_ref[:, head * HD : (head + 1) * HD] = turned
         fresh.append(
@@ -298,7 +347,7 @@
     step = (lane % HEAD_ROWS) // GROUP
     allowed = lax.broadcasted_iota(jnp.int32, (STEPS, OWN_ROWS), 0) <= step
     masked = jnp.where(allowed, scores, NEG_FILL)
-    maxima = [part[OWN_ROWS : OWN_ROWS + 1, :OWN_ROWS] for part in parts]
+    maxima = [stat[:, :OWN_ROWS] for _, stat in parts]
     joined = jnp.max(masked, axis=0, keepdims=True)
     for part in maxima:
         joined = jnp.maximum(joined, part)
@@ -307,7 +356,7 @@
     scales = []
     for t in range(len(parts)):
         scale = jnp.exp(maxima[t] - joined)
-        totals += parts[t][OWN_ROWS + 1 : OWN_ROWS + 2, :OWN_ROWS] * scale
+        totals += pltpu.roll(parts[t][1], OWN_ROWS, 1)[:, :OWN_ROWS] * scale
         scales.append(scale)
     factors = jnp.concatenate([*scales, weights.astype(BF16).astype(F32)], axis=0) / totals
     factors = jnp.concatenate([factors, jnp.zeros((6, 128 - OWN_ROWS), F32)], axis=1)
@@ -318,7 +367,7 @@
         rows = slice(head * HEAD_ROWS, (head + 1) * HEAD_ROWS)
         total = jnp.zeros((HEAD_ROWS, HD), F32)
         for t in range(len(parts)):
-            total += parts[t][rows, :] * columns[rows, t : t + 1]
+            total += parts[t][0][rows, :] * columns[rows, t : t + 1]
         for t in range(STEPS):
             total += columns[rows, 2 + t : 3 + t] * values[t : t + 1, head * HD : (head + 1) * HD]
         for s in range(STEPS):

time: 62.8 us -> 62 us (0.987)
  waiting for transfers between devices: 9.34 us -> 8.46 us
where the time goes in v4:
time: 62 us; the launch traced here: 61.4 us
  starting transfers between devices  43.7 us (70%)
  waiting for transfers between devices  8.46 us (14%)
  Pallas kernels  6.66 us (11%)
  between operations  1.45 us (2%)
  local copies, waits for them, and re-layouts  0.89 us (1%)
    ppermute x7, starting transfers between devices, with_partner(): return lax.ppermute(values, axis, [(i, i ^ flip) for i in range(size)])  22.9 us
    all_to_all x2, starting transfers between devices, exchange_z(): return lax.all_to_all(blocks, Z_AXES, 0, 0, axis_index_groups=[order])  20.8 us
    ppermute x7, waiting for transfers between devices, with_partner(): return lax.ppermute(values, axis, [(i, i ^ flip) for i in range(size)])  7.88 us
    pallas_call x1, Pallas kernels, prepare(): pl.pallas_call(prepare_kernel, out_shape=(jax.ShapeDtypeStruct((16, STEPS...  1.61 us
    pallas_call x1, Pallas kernels, fetch(): pl.pallas_call(fetch_kernel, out_shape=(pltpu.VMEM(keys.shape, BF16), plt...  1.56 us
  transfers between devices with their start and end apart: 9, of which 4 were waited for; matrix products, arithmetic and copies ran while one was open for 0% of the time, Pallas kernels for 7%

profile of v4, /device:TPU:32, one launch (start us, length us, event | category | flops | bytes accessed | tf_op | source)
XLA Modules:
  0.0 61.4 jit_solution(11295356916681046727)
XLA Ops:
  0.6 0.8 %copy.9 = bf16[8,8,2,256]{3,1,2,0:T(8,128)(2,1)S(1)} copy(bf16[8,8,2,256]{3,2,1,0:T(2,128)(2,1)} %bitcast.14) | data formatting | bytes 131072
  1.5 3.4 %collective-permute-start.2 = (bf16[64,512]{1,0:T(8,128)(2,1)S(1)}, bf16[64,512]{1,0:T(8,128)(2,1)S(1)}, u32[]{:S(2)}, u32[]{:S(2)}) collective-permute-start(bf16[64,512]{1,0:T(8,128)(2,1)S(1)} %bitcast.10), channel_id=1, source_target_pairs={{0,2},{2,0},{4,6},{6,4},{1,3},{3,1},{5,7},{7,5},{8,10},{10,8},{12,... | collective-permute-start | bytes 196616 | tf_op jit(solution)/shard_map/ppermute | solution.py:418
  4.9 1.6 %prepare.1 = (bf16[16,4,512]{2,1,0:T(4,128)(2,1)}, bf16[64,128]{1,0:T(8,128)(2,1)S(1)}) custom-call(bf16[4,8192]{1,0:T(4,128)(2,1)} %bitcast.13, bf16[4,2048]{1,0:T(4,128)(2,1)} %bitcast.15), custom_call_target="tpu_custom_call" | custom-call | flops 65536 | bytes 262144 | tf_op jit(solution)/shard_map/prepare/pallas_call | solution.py:82
  6.5 3.5 %collective-permute-start = (bf16[64,128]{1,0:T(8,128)(2,1)S(1)}, bf16[64,128]{1,0:T(8,128)(2,1)S(1)}, u32[]{:S(2)}, u32[]{:S(2)}) collective-permute-start(bf16[64,128]{1,0:T(8,128)(2,1)S(1)} %get-tuple-element.20), channel_id=1, source_target_pairs={{0,8},{8,0},{16,24},{24,16},{1,9},{9,1},{17,25},{25,17},{2,10},{10... | collective-permute-start | bytes 49160 | tf_op jit(solution)/shard_map/ppermute | solution.py:418
  10.0 0.0 collective-permute-done.2
  10.0 15.7 %all-to-all-start = ((bf16[16,4,512]{2,1,0:T(4,128)(2,1)}), bf16[16,4,512]{2,1,0:T(4,128)(2,1)S(1)}, u32[]{:S(2)}, u32[]{:S(2)}) async-start(bf16[16,4,512]{2,1,0:T(4,128)(2,1)} %get-tuple-element.29), calls=%async_computation | async-start | bytes 131072 | tf_op jit(solution)/shard_map/all_to_all | solution.py:414
  25.8 4.0 %collective-permute-start.3 = (bf16[128,512]{1,0:T(8,128)(2,1)S(1)}, bf16[128,512]{1,0:T(8,128)(2,1)S(1)}, u32[]{:S(2)}, u32[]{:S(2)}) collective-permute-start(bf16[128,512]{1,0:T(8,128)(2,1)S(1)} %pad_maximum_fusion), channel_id=1, source_target_pairs={{0,6},{2,4},{4,2},{6,0},{1,7},{3,5},{5,3},{7,1},{8,14},{10,12},{12... | collective-permute-start | bytes 393224 | tf_op jit(solution)/shard_map/ppermute | solution.py:418
  29.8 0.0 collective-permute-done
  29.8 4.1 %collective-permute-start.1 = (bf16[128,128]{1,0:T(8,128)(2,1)S(1)}, bf16[128,128]{1,0:T(8,128)(2,1)S(1)}, u32[]{:S(2)}, u32[]{:S(2)}) collective-permute-start(bf16[128,128]{1,0:T(8,128)(2,1)S(1)} %constant_dynamic-update-slice_fusion.near_ref.queries_ref), channel_id=1, source_target_pairs={{0,24},{8,16},{16,8},{24,0},{1,25},{9,17},{17,9},{25,1},{2,26},{10... | collective-permute-start | bytes 98312 | tf_op jit(solution)/shard_map/ppermute | solution.py:418
  33.9 1.6 %fetch.1 = (bf16[1,512,1024]{2,1,0:T(8,128)(2,1)S(1)}, bf16[1,512,1024]{2,1,0:T(8,128)(2,1)S(1)}) custom-call(bf16[1,512,1024]{2,1,0:T(8,128)(2,1)} %keys_hbm, bf16[1,512,1024]{2,1,0:T(8,128)(2,1)} %values_hbm.1), custom_call_target="tpu_custom_call" | custom-call | flops 1 | bytes 1 | tf_op jit(solution)/shard_map/fetch/pallas_call | solution.py:145
  35.5 1.3 %collective-permute-done.1.far_ref = bf16[128,128]{1,0:T(8,128)(2,1)S(1)} collective-permute-done((bf16[128,128]{1,0:T(8,128)(2,1)S(1)}, bf16[128,128]{1,0:T(8,128)(2,1)S(1)}, u32[]{:S(2)}, u32[]{:S(2)}) %collective-permute-start.1) | collective-permute-done | bytes 32800 | tf_op jit(solution)/shard_map/ppermute | solution.py:418
  36.8 1.9 %collective-permute-start.6 = (bf16[256,512]{1,0:T(8,128)(2,1)S(1)}, bf16[256,512]{1,0:T(8,128)(2,1)S(1)}, u32[]{:S(2)}, u32[]{:S(2)}) collective-permute-start(bf16[256,512]{1,0:T(8,128)(2,1)S(1)} %constant_dynamic-update-slice_fusion.2.own_ref), channel_id=1, source_target_pairs={{0,32},{32,0},{1,33},{33,1},{2,34},{34,2},{3,35},{35,3},{4,36},{36... | collective-permute-start | bytes 786440 | tf_op jit(solution)/shard_map/ppermute | solution.py:418
  39.4 1.2 %attend.1 = (f32[2,72,128]{2,1,0:T(8,128)S(1)}, bf16[2,80,128]{2,1,0:T(8,128)(2,1)S(1)}) custom-call(s32[1,256]{1,0:T(1,128)S(1)} %broadcast_in_dim.2.lengths_ref, bf16[128,128]{1,0:T(8,128)(2,1)S(1)} %constant_dynamic-update-slice_fusion.near_ref.queries_ref, bf16[128,128]{1,0:T(8,128)(2,1)S(1)} %collective-permute-done.1.far_ref, ...), custom_call_target="tpu_custom_call" | custom-call | flops 1 | bytes 1 | tf_op jit(solution)/shard_map/attend/pallas_call | solution.py:222
  40.6 1.0 %project.1 = bf16[16,4,768]{2,1,0:T(4,128)(2,1)} custom-call(bf16[16,4,512]{2,1,0:T(4,128)(2,1)S(1)} %all-to-all-done.hidden_ref, bf16[256,512]{1,0:T(8,128)(2,1)S(1)} %constant_dynamic-update-slice_fusion.2.own_ref, bf16[256,512]{1,0:T(8,128)(2,1)S(1)} %collective-permute-done.6.other_ref), custom_call_target="tpu_custom_call" | custom-call | flops 33554432 | bytes 1048576 | tf_op jit(solution)/shard_map/project/pallas_call | solution.py:301
  41.6 5.1 %all-to-all-start.1 = ((bf16[16,4,768]{2,1,0:T(4,128)(2,1)}), bf16[16,4,768]{2,1,0:T(4,128)(2,1)S(1)}, u32[]{:S(2)}, u32[]{:S(2)}) async-start(bf16[16,4,768]{2,1,0:T(4,128)(2,1)} %project.1), calls=%async_computation.1 | async-start | bytes 196608 | tf_op jit(solution)/shard_map/all_to_all | solution.py:414
  46.7 4.1 %collective-permute-start.4 = (bf16[2,80,128]{2,1,0:T(8,128)(2,1)S(1)}, bf16[2,80,128]{2,1,0:T(8,128)(2,1)S(1)}, u32[]{:S(2)}, u32[]{:S(2)}) collective-permute-start(bf16[2,80,128]{2,1,0:T(8,128)(2,1)S(1)} %get-tuple-element.25), channel_id=1, source_target_pairs={{0,24},{8,16},{16,8},{24,0},{1,25},{9,17},{17,9},{25,1},{2,26},{10... | collective-permute-start | bytes 122888 | tf_op jit(solution)/shard_map/ppermute | solution.py:418
  50.8 0.1 fusion
  50.9 2.9 %collective-permute-done.4.come_ref = bf16[2,80,128]{2,1,0:T(8,128)(2,1)S(1)} collective-permute-done((bf16[2,80,128]{2,1,0:T(8,128)(2,1)S(1)}, bf16[2,80,128]{2,1,0:T(8,128)(2,1)S(1)}, u32[]{:S(2)}, u32[]{:S(2)}) %collective-permute-start.4) | collective-permute-done | bytes 40992 | tf_op jit(solution)/shard_map/ppermute | solution.py:418
  53.8 0.2 merge.1
  54.0 1.9 %collective-permute-start.5 = (bf16[80,128]{1,0:T(8,128)(2,1)S(1)}, bf16[80,128]{1,0:T(8,128)(2,1)S(1)}, u32[]{:S(2)}, u32[]{:S(2)}) collective-permute-start(bf16[80,128]{1,0:T(8,128)(2,1)S(1)} %get-tuple-element.27), channel_id=1, source_target_pairs={{0,8},{8,0},{16,24},{24,16},{1,9},{9,1},{17,25},{25,17},{2,10},{10... | collective-permute-start | bytes 61448 | tf_op jit(solution)/shard_map/ppermute | solution.py:418
  56.0 0.1 pad_maximum_fusion.1
  56.0 3.7 %collective-permute-done.5.part1_ref = bf16[80,128]{1,0:T(8,128)(2,1)S(1)} collective-permute-done((bf16[80,128]{1,0:T(8,128)(2,1)S(1)}, bf16[80,128]{1,0:T(8,128)(2,1)S(1)}, u32[]{:S(2)}, u32[]{:S(2)}) %collective-permute-start.5) | collective-permute-done | bytes 20512 | tf_op jit(solution)/shard_map/ppermute | solution.py:418
  59.7 0.6 all-to-all-done.1.sums_ref
  60.3 1.1 %finish.1 = (bf16[4,2048]{1,0:T(4,128)(2,1)}, bf16[4,256]{1,0:T(4,128)(2,1)}, bf16[4,256]{1,0:T(4,128)(2,1)}) custom-call(f32[72,128]{1,0:T(8,128)S(1)} %get-tuple-element.26.part0_ref, bf16[80,128]{1,0:T(8,128)(2,1)S(1)} %collective-permute-done.5.part1_ref, bf16[16,4,768]{2,1,0:T(4,128)(2,1)S(1)} %all-to-all-done.1.sums_ref, ...), custom_call_target="tpu_custom_call" | custom-call | flops 1048576 | bytes 524288 | tf_op jit(solution)/shard_map/finish/pallas_call | solution.py:382
  (12 shorter events, 0.1 us)
Async XLA Ops:
  1.5 8.5 %collective-permute-start.2 = (bf16[64,512]{1,0:T(8,128)(2,1)S(1)}, bf16[64,512]{1,0:T(8,128)(2,1)S(1)}, u32[]{:S(2)}, u32[]{:S(2)}) collective-permute-start(bf16[64,512]{1,0:T(8,128)(2,1)S(1)} %bitcast.10), channel_id=1, source_target_pairs={{0,2},{2,0},{4,6},{6,4},{1,3},{3,1},{5,7},{7,5},{8,10},{10,8},{12,... | collective-permute-start | bytes 196616 | tf_op jit(solution)/shard_map/ppermute | solution.py:418
  6.5 23.3 %collective-permute-start = (bf16[64,128]{1,0:T(8,128)(2,1)S(1)}, bf16[64,128]{1,0:T(8,128)(2,1)S(1)}, u32[]{:S(2)}, u32[]{:S(2)}) collective-permute-start(bf16[64,128]{1,0:T(8,128)(2,1)S(1)} %get-tuple-element.20), channel_id=1, source_target_pairs={{0,8},{8,0},{16,24},{24,16},{1,9},{9,1},{17,25},{25,17},{2,10},{10... | collective-permute-start | bytes 49160 | tf_op jit(solution)/shard_map/ppermute | solution.py:418
  10.0 26.8 %all-to-all-start = ((bf16[16,4,512]{2,1,0:T(4,128)(2,1)}), bf16[16,4,512]{2,1,0:T(4,128)(2,1)S(1)}, u32[]{:S(2)}, u32[]{:S(2)}) async-start(bf16[16,4,512]{2,1,0:T(4,128)(2,1)} %get-tuple-element.29), calls=%async_computation | async-start | bytes 131072 | tf_op jit(solution)/shard_map/all_to_all | solution.py:414
  25.8 8.2 %collective-permute-start.3 = (bf16[128,512]{1,0:T(8,128)(2,1)S(1)}, bf16[128,512]{1,0:T(8,128)(2,1)S(1)}, u32[]{:S(2)}, u32[]{:S(2)}) collective-permute-start(bf16[128,512]{1,0:T(8,128)(2,1)S(1)} %pad_maximum_fusion), channel_id=1, source_target_pairs={{0,6},{2,4},{4,2},{6,0},{1,7},{3,5},{5,3},{7,1},{8,14},{10,12},{12... | collective-permute-start | bytes 393224 | tf_op jit(solution)/shard_map/ppermute | solution.py:418
  29.8 7.0 %collective-permute-start.1 = (bf16[128,128]{1,0:T(8,128)(2,1)S(1)}, bf16[128,128]{1,0:T(8,128)(2,1)S(1)}, u32[]{:S(2)}, u32[]{:S(2)}) collective-permute-start(bf16[128,128]{1,0:T(8,128)(2,1)S(1)} %constant_dynamic-update-slice_fusion.near_ref.queries_ref), channel_id=1, source_target_pairs={{0,24},{8,16},{16,8},{24,0},{1,25},{9,17},{17,9},{25,1},{2,26},{10... | collective-permute-start | bytes 98312 | tf_op jit(solution)/shard_map/ppermute | solution.py:418
  36.8 3.8 %collective-permute-start.6 = (bf16[256,512]{1,0:T(8,128)(2,1)S(1)}, bf16[256,512]{1,0:T(8,128)(2,1)S(1)}, u32[]{:S(2)}, u32[]{:S(2)}) collective-permute-start(bf16[256,512]{1,0:T(8,128)(2,1)S(1)} %constant_dynamic-update-slice_fusion.2.own_ref), channel_id=1, source_target_pairs={{0,32},{32,0},{1,33},{33,1},{2,34},{34,2},{3,35},{35,3},{4,36},{36... | collective-permute-start | bytes 786440 | tf_op jit(solution)/shard_map/ppermute | solution.py:418
  41.6 18.7 %all-to-all-start.1 = ((bf16[16,4,768]{2,1,0:T(4,128)(2,1)}), bf16[16,4,768]{2,1,0:T(4,128)(2,1)S(1)}, u32[]{:S(2)}, u32[]{:S(2)}) async-start(bf16[16,4,768]{2,1,0:T(4,128)(2,1)} %project.1), calls=%async_computation.1 | async-start | bytes 196608 | tf_op jit(solution)/shard_map/all_to_all | solution.py:414
  46.7 7.1 %collective-permute-start.4 = (bf16[2,80,128]{2,1,0:T(8,128)(2,1)S(1)}, bf16[2,80,128]{2,1,0:T(8,128)(2,1)S(1)}, u32[]{:S(2)}, u32[]{:S(2)}) collective-permute-start(bf16[2,80,128]{2,1,0:T(8,128)(2,1)S(1)} %get-tuple-element.25), channel_id=1, source_target_pairs={{0,24},{8,16},{16,8},{24,0},{1,25},{9,17},{17,9},{25,1},{2,26},{10... | collective-permute-start | bytes 122888 | tf_op jit(solution)/shard_map/ppermute | solution.py:418
  54.0 5.7 %collective-permute-start.5 = (bf16[80,128]{1,0:T(8,128)(2,1)S(1)}, bf16[80,128]{1,0:T(8,128)(2,1)S(1)}, u32[]{:S(2)}, u32[]{:S(2)}) collective-permute-start(bf16[80,128]{1,0:T(8,128)(2,1)S(1)} %get-tuple-element.27), channel_id=1, source_target_pairs={{0,8},{8,0},{16,24},{24,16},{1,9},{9,1},{17,25},{25,17},{2,10},{10... | collective-permute-start | bytes 61448 | tf_op jit(solution)/shard_map/ppermute | solution.py:418

commit v5 on v4

--- a/solution.py
+++ b/solution.py
@@ -431,7 +431,7 @@
     weight = jnp.concatenate([weight, with_partner(weight, "x", 3)], axis=0)
     keys, values = fetch(gate(key_cache, weight), value_cache)
     kept, sent = attend(jnp.broadcast_to(lengths, (1, KVH * HEAD_ROWS)), near, far, keys, values)
-    other = with_partner(gate(weight, tokens, far, keys), "core", 1, 2)
+    other = with_partner(weight, "core", 1, 2)
     partial = project(tokens, weight, gate(other, kept))
     sums = exchange_z(partial, SUMS_ORDER)
     own_part, next_part = merge(kept, with_partner(sent, "tensor", 3))

time: 62 us -> 61.1 us (0.985)
  waiting for transfers between devices: 8.46 us -> 7.27 us
  transfers between devices with their start and end apart: 9 -> 9, of which waited for: 4 -> 3; matrix products, arithmetic and copies ran while one was open for 0% -> 0% of each run, Pallas kernels for 7% -> 8%
where the time goes in v5:
time: 61.1 us; the launch traced here: 60.5 us
  starting transfers between devices  44 us (72%)
  waiting for transfers between devices  7.27 us (12%)
  Pallas kernels  6.66 us (11%)
  between operations  1.46 us (2%)
  local copies, waits for them, and re-layouts  0.89 us (1%)
    ppermute x7, starting transfers between devices, with_partner(): return lax.ppermute(values, axis, [(i, i ^ flip) for i in range(size)])  22.9 us
    all_to_all x2, starting transfers between devices, exchange_z(): return lax.all_to_all(blocks, Z_AXES, 0, 0, axis_index_groups=[order])  21.1 us
    ppermute x7, waiting for transfers between devices, with_partner(): return lax.ppermute(values, axis, [(i, i ^ flip) for i in range(size)])  7.26 us
    pallas_call x1, Pallas kernels, prepare(): pl.pallas_call(prepare_kernel, out_shape=(jax.ShapeDtypeStruct((16, STEPS...  1.61 us
    pallas_call x1, Pallas kernels, fetch(): pl.pallas_call(fetch_kernel, out_shape=(pltpu.VMEM(keys.shape, BF16), plt...  1.56 us
  transfers between devices with their start and end apart: 9, of which 3 were waited for; matrix products, arithmetic and copies ran while one was open for 0% of the time, Pallas kernels for 8%

profile of v5, /device:TPU:32, one launch (start us, length us, event | category | flops | bytes accessed | tf_op | source)
XLA Modules:
  0.0 60.5 jit_solution(8864111826876162148)
XLA Ops:
  0.6 0.8 %copy.9 = bf16[8,8,2,256]{3,1,2,0:T(8,128)(2,1)S(1)} copy(bf16[8,8,2,256]{3,2,1,0:T(2,128)(2,1)} %bitcast.14) | data formatting | bytes 131072
  1.5 3.4 %collective-permute-start.2 = (bf16[64,512]{1,0:T(8,128)(2,1)S(1)}, bf16[64,512]{1,0:T(8,128)(2,1)S(1)}, u32[]{:S(2)}, u32[]{:S(2)}) collective-permute-start(bf16[64,512]{1,0:T(8,128)(2,1)S(1)} %bitcast.10), channel_id=1, source_target_pairs={{0,2},{2,0},{4,6},{6,4},{1,3},{3,1},{5,7},{7,5},{8,10},{10,8},{12,... | collective-permute-start | bytes 196616 | tf_op jit(solution)/shard_map/ppermute | solution.py:418
  4.9 1.6 %prepare.1 = (bf16[16,4,512]{2,1,0:T(4,128)(2,1)}, bf16[64,128]{1,0:T(8,128)(2,1)S(1)}) custom-call(bf16[4,8192]{1,0:T(4,128)(2,1)} %bitcast.13, bf16[4,2048]{1,0:T(4,128)(2,1)} %bitcast.15), custom_call_target="tpu_custom_call" | custom-call | flops 65536 | bytes 262144 | tf_op jit(solution)/shard_map/prepare/pallas_call | solution.py:82
  6.5 3.5 %collective-permute-start = (bf16[64,128]{1,0:T(8,128)(2,1)S(1)}, bf16[64,128]{1,0:T(8,128)(2,1)S(1)}, u32[]{:S(2)}, u32[]{:S(2)}) collective-permute-start(bf16[64,128]{1,0:T(8,128)(2,1)S(1)} %get-tuple-element.19), channel_id=1, source_target_pairs={{0,8},{8,0},{16,24},{24,16},{1,9},{9,1},{17,25},{25,17},{2,10},{10... | collective-permute-start | bytes 49160 | tf_op jit(solution)/shard_map/ppermute | solution.py:418
  10.0 0.0 collective-permute-done.2
  10.0 4.0 %collective-permute-start.3 = (bf16[128,512]{1,0:T(8,128)(2,1)S(1)}, bf16[128,512]{1,0:T(8,128)(2,1)S(1)}, u32[]{:S(2)}, u32[]{:S(2)}) collective-permute-start(bf16[128,512]{1,0:T(8,128)(2,1)S(1)} %pad_maximum_fusion), channel_id=1, source_target_pairs={{0,6},{2,4},{4,2},{6,0},{1,7},{3,5},{5,3},{7,1},{8,14},{10,12},{12... | collective-permute-start | bytes 393224 | tf_op jit(solution)/shard_map/ppermute | solution.py:418
  14.1 15.7 %all-to-all-start = ((bf16[16,4,512]{2,1,0:T(4,128)(2,1)}), bf16[16,4,512]{2,1,0:T(4,128)(2,1)S(1)}, u32[]{:S(2)}, u32[]{:S(2)}) async-start(bf16[16,4,512]{2,1,0:T(4,128)(2,1)} %get-tuple-element.28), calls=%async_computation | async-start | bytes 131072 | tf_op jit(solution)/shard_map/all_to_all | solution.py:414
  29.8 0.0 collective-permute-done.3
  29.8 1.9 %collective-permute-start.6 = (bf16[256,512]{1,0:T(8,128)(2,1)S(1)}, bf16[256,512]{1,0:T(8,128)(2,1)S(1)}, u32[]{:S(2)}, u32[]{:S(2)}) collective-permute-start(bf16[256,512]{1,0:T(8,128)(2,1)S(1)} %constant_dynamic-update-slice_fusion.2.own_ref), channel_id=1, source_target_pairs={{0,32},{32,0},{1,33},{33,1},{2,34},{34,2},{3,35},{35,3},{4,36},{36... | collective-permute-start | bytes 786440 | tf_op jit(solution)/shard_map/ppermute | solution.py:418
  31.8 4.1 %collective-permute-start.1 = (bf16[128,128]{1,0:T(8,128)(2,1)S(1)}, bf16[128,128]{1,0:T(8,128)(2,1)S(1)}, u32[]{:S(2)}, u32[]{:S(2)}) collective-permute-start(bf16[128,128]{1,0:T(8,128)(2,1)S(1)} %constant_dynamic-update-slice_fusion.near_ref.queries_ref), channel_id=1, source_target_pairs={{0,24},{8,16},{16,8},{24,0},{1,25},{9,17},{17,9},{25,1},{2,26},{10... | collective-permute-start | bytes 98312 | tf_op jit(solution)/shard_map/ppermute | solution.py:418
  36.5 1.6 %fetch.1 = (bf16[1,512,1024]{2,1,0:T(8,128)(2,1)S(1)}, bf16[1,512,1024]{2,1,0:T(8,128)(2,1)S(1)}) custom-call(bf16[1,512,1024]{2,1,0:T(8,128)(2,1)} %keys_hbm, bf16[1,512,1024]{2,1,0:T(8,128)(2,1)} %values_hbm.1), custom_call_target="tpu_custom_call" | custom-call | flops 1 | bytes 1 | tf_op jit(solution)/shard_map/fetch/pallas_call | solution.py:145
  38.1 0.7 %collective-permute-done.1.far_ref = bf16[128,128]{1,0:T(8,128)(2,1)S(1)} collective-permute-done((bf16[128,128]{1,0:T(8,128)(2,1)S(1)}, bf16[128,128]{1,0:T(8,128)(2,1)S(1)}, u32[]{:S(2)}, u32[]{:S(2)}) %collective-permute-start.1) | collective-permute-done | bytes 32800 | tf_op jit(solution)/shard_map/ppermute | solution.py:418
  38.8 1.2 %attend.1 = (f32[2,72,128]{2,1,0:T(8,128)S(1)}, bf16[2,80,128]{2,1,0:T(8,128)(2,1)S(1)}) custom-call(s32[1,256]{1,0:T(1,128)S(1)} %broadcast_in_dim.2.lengths_ref, bf16[128,128]{1,0:T(8,128)(2,1)S(1)} %constant_dynamic-update-slice_fusion.near_ref.queries_ref, bf16[128,128]{1,0:T(8,128)(2,1)S(1)} %collective-permute-done.1.far_ref, ...), custom_call_target="tpu_custom_call" | custom-call | flops 1 | bytes 1 | tf_op jit(solution)/shard_map/attend/pallas_call | solution.py:222
  40.0 0.0 all-to-all-done.hidden_ref
  40.0 1.0 %project.1 = bf16[16,4,768]{2,1,0:T(4,128)(2,1)} custom-call(bf16[16,4,512]{2,1,0:T(4,128)(2,1)S(1)} %all-to-all-done.hidden_ref, bf16[256,512]{1,0:T(8,128)(2,1)S(1)} %constant_dynamic-update-slice_fusion.2.own_ref, bf16[256,512]{1,0:T(8,128)(2,1)S(1)} %collective-permute-done.6.other_ref), custom_call_target="tpu_custom_call" | custom-call | flops 33554432 | bytes 1048576 | tf_op jit(solution)/shard_map/project/pallas_call | solution.py:301
  40.9 5.4 %all-to-all-start.1 = ((bf16[16,4,768]{2,1,0:T(4,128)(2,1)}), bf16[16,4,768]{2,1,0:T(4,128)(2,1)S(1)}, u32[]{:S(2)}, u32[]{:S(2)}) async-start(bf16[16,4,768]{2,1,0:T(4,128)(2,1)} %project.1), calls=%async_computation.1 | async-start | bytes 196608 | tf_op jit(solution)/shard_map/all_to_all | solution.py:414
  46.4 4.1 %collective-permute-start.4 = (bf16[2,80,128]{2,1,0:T(8,128)(2,1)S(1)}, bf16[2,80,128]{2,1,0:T(8,128)(2,1)S(1)}, u32[]{:S(2)}, u32[]{:S(2)}) collective-permute-start(bf16[2,80,128]{2,1,0:T(8,128)(2,1)S(1)} %get-tuple-element.24), channel_id=1, source_target_pairs={{0,24},{8,16},{16,8},{24,0},{1,25},{9,17},{17,9},{25,1},{2,26},{10... | collective-permute-start | bytes 122888 | tf_op jit(solution)/shard_map/ppermute | solution.py:418
  50.5 0.1 fusion
  50.6 2.9 %collective-permute-done.4.come_ref = bf16[2,80,128]{2,1,0:T(8,128)(2,1)S(1)} collective-permute-done((bf16[2,80,128]{2,1,0:T(8,128)(2,1)S(1)}, bf16[2,80,128]{2,1,0:T(8,128)(2,1)S(1)}, u32[]{:S(2)}, u32[]{:S(2)}) %collective-permute-start.4) | collective-permute-done | bytes 40992 | tf_op jit(solution)/shard_map/ppermute | solution.py:418
  53.5 0.2 merge.1
  53.7 1.9 %collective-permute-start.5 = (bf16[80,128]{1,0:T(8,128)(2,1)S(1)}, bf16[80,128]{1,0:T(8,128)(2,1)S(1)}, u32[]{:S(2)}, u32[]{:S(2)}) collective-permute-start(bf16[80,128]{1,0:T(8,128)(2,1)S(1)} %get-tuple-element.26), channel_id=1, source_target_pairs={{0,8},{8,0},{16,24},{24,16},{1,9},{9,1},{17,25},{25,17},{2,10},{10... | collective-permute-start | bytes 61448 | tf_op jit(solution)/shard_map/ppermute | solution.py:418
  55.7 0.1 pad_maximum_fusion.1
  55.7 3.7 %collective-permute-done.5.part1_ref = bf16[80,128]{1,0:T(8,128)(2,1)S(1)} collective-permute-done((bf16[80,128]{1,0:T(8,128)(2,1)S(1)}, bf16[80,128]{1,0:T(8,128)(2,1)S(1)}, u32[]{:S(2)}, u32[]{:S(2)}) %collective-permute-start.5) | collective-permute-done | bytes 20512 | tf_op jit(solution)/shard_map/ppermute | solution.py:418
  59.4 1.1 %finish.1 = (bf16[4,2048]{1,0:T(4,128)(2,1)}, bf16[4,256]{1,0:T(4,128)(2,1)}, bf16[4,256]{1,0:T(4,128)(2,1)}) custom-call(f32[72,128]{1,0:T(8,128)S(1)} %get-tuple-element.25.part0_ref, bf16[80,128]{1,0:T(8,128)(2,1)S(1)} %collective-permute-done.5.part1_ref, bf16[16,4,768]{2,1,0:T(4,128)(2,1)S(1)} %all-to-all-done.1.sums_ref, ...), custom_call_target="tpu_custom_call" | custom-call | flops 1048576 | bytes 524288 | tf_op jit(solution)/shard_map/finish/pallas_call | solution.py:382
  (12 shorter events, 0.1 us)
Async XLA Ops:
  1.5 8.5 %collective-permute-start.2 = (bf16[64,512]{1,0:T(8,128)(2,1)S(1)}, bf16[64,512]{1,0:T(8,128)(2,1)S(1)}, u32[]{:S(2)}, u32[]{:S(2)}) collective-permute-start(bf16[64,512]{1,0:T(8,128)(2,1)S(1)} %bitcast.10), channel_id=1, source_target_pairs={{0,2},{2,0},{4,6},{6,4},{1,3},{3,1},{5,7},{7,5},{8,10},{10,8},{12,... | collective-permute-start | bytes 196616 | tf_op jit(solution)/shard_map/ppermute | solution.py:418
  6.5 25.2 %collective-permute-start = (bf16[64,128]{1,0:T(8,128)(2,1)S(1)}, bf16[64,128]{1,0:T(8,128)(2,1)S(1)}, u32[]{:S(2)}, u32[]{:S(2)}) collective-permute-start(bf16[64,128]{1,0:T(8,128)(2,1)S(1)} %get-tuple-element.19), channel_id=1, source_target_pairs={{0,8},{8,0},{16,24},{24,16},{1,9},{9,1},{17,25},{25,17},{2,10},{10... | collective-permute-start | bytes 49160 | tf_op jit(solution)/shard_map/ppermute | solution.py:418
  10.0 19.8 %collective-permute-start.3 = (bf16[128,512]{1,0:T(8,128)(2,1)S(1)}, bf16[128,512]{1,0:T(8,128)(2,1)S(1)}, u32[]{:S(2)}, u32[]{:S(2)}) collective-permute-start(bf16[128,512]{1,0:T(8,128)(2,1)S(1)} %pad_maximum_fusion), channel_id=1, source_target_pairs={{0,6},{2,4},{4,2},{6,0},{1,7},{3,5},{5,3},{7,1},{8,14},{10,12},{12... | collective-permute-start | bytes 393224 | tf_op jit(solution)/shard_map/ppermute | solution.py:418
  14.1 25.9 %all-to-all-start = ((bf16[16,4,512]{2,1,0:T(4,128)(2,1)}), bf16[16,4,512]{2,1,0:T(4,128)(2,1)S(1)}, u32[]{:S(2)}, u32[]{:S(2)}) async-start(bf16[16,4,512]{2,1,0:T(4,128)(2,1)} %get-tuple-element.28), calls=%async_computation | async-start | bytes 131072 | tf_op jit(solution)/shard_map/all_to_all | solution.py:414
  29.8 10.2 %collective-permute-start.6 = (bf16[256,512]{1,0:T(8,128)(2,1)S(1)}, bf16[256,512]{1,0:T(8,128)(2,1)S(1)}, u32[]{:S(2)}, u32[]{:S(2)}) collective-permute-start(bf16[256,512]{1,0:T(8,128)(2,1)S(1)} %constant_dynamic-update-slice_fusion.2.own_ref), channel_id=1, source_target_pairs={{0,32},{32,0},{1,33},{33,1},{2,34},{34,2},{3,35},{35,3},{4,36},{36... | collective-permute-start | bytes 786440 | tf_op jit(solution)/shard_map/ppermute | solution.py:418
  31.8 7.0 %collective-permute-start.1 = (bf16[128,128]{1,0:T(8,128)(2,1)S(1)}, bf16[128,128]{1,0:T(8,128)(2,1)S(1)}, u32[]{:S(2)}, u32[]{:S(2)}) collective-permute-start(bf16[128,128]{1,0:T(8,128)(2,1)S(1)} %constant_dynamic-update-slice_fusion.near_ref.queries_ref), channel_id=1, source_target_pairs={{0,24},{8,16},{16,8},{24,0},{1,25},{9,17},{17,9},{25,1},{2,26},{10... | collective-permute-start | bytes 98312 | tf_op jit(solution)/shard_map/ppermute | solution.py:418
  40.9 18.5 %all-to-all-start.1 = ((bf16[16,4,768]{2,1,0:T(4,128)(2,1)}), bf16[16,4,768]{2,1,0:T(4,128)(2,1)S(1)}, u32[]{:S(2)}, u32[]{:S(2)}) async-start(bf16[16,4,768]{2,1,0:T(4,128)(2,1)} %project.1), calls=%async_computation.1 | async-start | bytes 196608 | tf_op jit(solution)/shard_map/all_to_all | solution.py:414
  46.4 7.1 %collective-permute-start.4 = (bf16[2,80,128]{2,1,0:T(8,128)(2,1)S(1)}, bf16[2,80,128]{2,1,0:T(8,128)(2,1)S(1)}, u32[]{:S(2)}, u32[]{:S(2)}) collective-permute-start(bf16[2,80,128]{2,1,0:T(8,128)(2,1)S(1)} %get-tuple-element.24), channel_id=1, source_target_pairs={{0,24},{8,16},{16,8},{24,0},{1,25},{9,17},{17,9},{25,1},{2,26},{10... | collective-permute-start | bytes 122888 | tf_op jit(solution)/shard_map/ppermute | solution.py:418
  53.7 5.7 %collective-permute-start.5 = (bf16[80,128]{1,0:T(8,128)(2,1)S(1)}, bf16[80,128]{1,0:T(8,128)(2,1)S(1)}, u32[]{:S(2)}, u32[]{:S(2)}) collective-permute-start(bf16[80,128]{1,0:T(8,128)(2,1)S(1)} %get-tuple-element.26), channel_id=1, source_target_pairs={{0,8},{8,0},{16,24},{24,16},{1,9},{9,1},{17,25},{25,17},{2,10},{10... | collective-permute-start | bytes 61448 | tf_op jit(solution)/shard_map/ppermute | solution.py:418

commit v6 on v5

--- a/solution.py
+++ b/solution.py
@@ -48,14 +48,7 @@
     return pltpu.with_memory_space_constraint(array, pltpu.HBM)
 
 
-def prepare_kernel(
-    hidden_hbm, queries_hbm, hidden_out, queries_out, rows, hidden_ref, queries_ref, sems
-):
-    query_copy = pltpu.make_async_copy(queries_hbm, queries_ref, sems.at[0])
-    hidden_copy = pltpu.make_async_copy(hidden_hbm, hidden_ref, sems.at[1])
-    query_copy.start()
-    hidden_copy.start()
-    query_copy.wait()
+def prepare_kernel(hidden_ref, queries_ref, hidden_out, queries_out, rows):
     for head in range(LOCAL_HEADS):
         for member in range(GROUP):
             at = (head * GROUP + member) * HD
@@ -64,7 +57,6 @@
                 row = head * HEAD_ROWS + step * GROUP + member
                 rows[row : row + 1, :] = piece[step : step + 1, :]
     queries_out[...] = rows[...].astype(BF16)
-    hidden_copy.wait()
     low = lane_iota((STEPS, 128)) < 64
     for zlo in range(8):
         for pair in range(4):
@@ -85,18 +77,13 @@
             jax.ShapeDtypeStruct((16, STEPS, 512), BF16),
             jax.ShapeDtypeStruct((OWN_ROWS, HD), BF16),
         ),
-        in_specs=[HBM, HBM],
+        in_specs=[VMEM, VMEM],
         out_specs=(VMEM, VMEM),
-        scratch_shapes=[
-            pltpu.VMEM((OWN_ROWS, HD), F32),
-            pltpu.VMEM(hidden.shape, BF16),
-            pltpu.VMEM(queries.shape, BF16),
-            pltpu.SemaphoreType.DMA((2,)),
-        ],
+        scratch_shapes=[pltpu.VMEM((OWN_ROWS, HD), F32)],
         compiler_params=PARAMS,
         cost_estimate=pl.CostEstimate(flops=1 << 16, bytes_accessed=1 << 18, transcendentals=0),
         name="prepare",
-    )(in_hbm(hidden), in_hbm(queries))
+    )(hidden, queries)
 
 
 ORDER = (0, 1, 3, 2)

time: 61.1 us -> 60.2 us (0.985)
  Pallas kernels: 6.66 us -> 5.77 us
    pallas_call x1, Pallas kernels: 1.61 us -> 0.74 us  [prepare(): pl.pallas_call(prepare_kernel, out_shape=(jax.ShapeDtypeStruct((16, STEPS...]
  transfers between devices with their start and end apart: 9 -> 9, of which waited for: 3 -> 3; matrix products, arithmetic and copies ran while one was open for 0% -> 0% of each run, Pallas kernels for 8% -> 6%
where the time goes in v6:
time: 60.2 us; the launch traced here: 59.7 us
  starting transfers between devices  44 us (73%)
  waiting for transfers between devices  7.27 us (12%)
  Pallas kernels  5.77 us (10%)
  between operations  1.48 us (2%)
  local copies, waits for them, and re-layouts  0.92 us (2%)
    ppermute x7, starting transfers between devices, with_partner(): return lax.ppermute(values, axis, [(i, i ^ flip) for i in range(size)])  22.9 us
    all_to_all x2, starting transfers between devices, exchange_z(): return lax.all_to_all(blocks, Z_AXES, 0, 0, axis_index_groups=[order])  21.1 us
    ppermute x7, waiting for transfers between devices, with_partner(): return lax.ppermute(values, axis, [(i, i ^ flip) for i in range(size)])  7.26 us
    pallas_call x1, Pallas kernels, fetch(): pl.pallas_call(fetch_kernel, out_shape=(pltpu.VMEM(keys.shape, BF16), plt...  1.56 us
  transfers between devices with their start and end apart: 9, of which 3 were waited for; matrix products, arithmetic and copies ran while one was open for 0% of the time, Pallas kernels for 6%

profile of v6, /device:TPU:32, one launch (start us, length us, event | category | flops | bytes accessed | tf_op | source)
XLA Modules:
  0.0 59.7 jit_solution(7083238956741421369)
XLA Ops:
  0.7 0.9 %copy.9 = bf16[8,8,2,256]{3,1,2,0:T(8,128)(2,1)S(1)} copy(bf16[8,8,2,256]{3,2,1,0:T(2,128)(2,1)} %bitcast.15) | data formatting | bytes 131072
  1.5 3.4 %collective-permute-start.2 = (bf16[64,512]{1,0:T(8,128)(2,1)S(1)}, bf16[64,512]{1,0:T(8,128)(2,1)S(1)}, u32[]{:S(2)}, u32[]{:S(2)}) collective-permute-start(bf16[64,512]{1,0:T(8,128)(2,1)S(1)} %bitcast.12), channel_id=1, source_target_pairs={{0,2},{2,0},{4,6},{6,4},{1,3},{3,1},{5,7},{7,5},{8,10},{10,8},{12,... | collective-permute-start | bytes 196616 | tf_op jit(solution)/shard_map/ppermute | solution.py:405
  5.0 0.7 %prepare.1 = (bf16[16,4,512]{2,1,0:T(4,128)(2,1)}, bf16[64,128]{1,0:T(8,128)(2,1)S(1)}) custom-call(bf16[4,8192]{1,0:T(4,128)(2,1)S(1)} %bitcast.10, bf16[4,2048]{1,0:T(4,128)(2,1)S(1)} %bitcast.11), custom_call_target="tpu_custom_call" | custom-call | flops 65536 | bytes 262144 | tf_op jit(solution)/shard_map/prepare/pallas_call | solution.py:74
  5.7 3.5 %collective-permute-start = (bf16[64,128]{1,0:T(8,128)(2,1)S(1)}, bf16[64,128]{1,0:T(8,128)(2,1)S(1)}, u32[]{:S(2)}, u32[]{:S(2)}) collective-permute-start(bf16[64,128]{1,0:T(8,128)(2,1)S(1)} %get-tuple-element.19), channel_id=1, source_target_pairs={{0,8},{8,0},{16,24},{24,16},{1,9},{9,1},{17,25},{25,17},{2,10},{10... | collective-permute-start | bytes 49160 | tf_op jit(solution)/shard_map/ppermute | solution.py:405
  9.2 0.0 collective-permute-done.2
  9.2 4.0 %collective-permute-start.3 = (bf16[128,512]{1,0:T(8,128)(2,1)S(1)}, bf16[128,512]{1,0:T(8,128)(2,1)S(1)}, u32[]{:S(2)}, u32[]{:S(2)}) collective-permute-start(bf16[128,512]{1,0:T(8,128)(2,1)S(1)} %pad_maximum_fusion), channel_id=1, source_target_pairs={{0,6},{2,4},{4,2},{6,0},{1,7},{3,5},{5,3},{7,1},{8,14},{10,12},{12... | collective-permute-start | bytes 393224 | tf_op jit(solution)/shard_map/ppermute | solution.py:405
  13.2 15.7 %all-to-all-start = ((bf16[16,4,512]{2,1,0:T(4,128)(2,1)}), bf16[16,4,512]{2,1,0:T(4,128)(2,1)S(1)}, u32[]{:S(2)}, u32[]{:S(2)}) async-start(bf16[16,4,512]{2,1,0:T(4,128)(2,1)} %get-tuple-element.28), calls=%async_computation | async-start | bytes 131072 | tf_op jit(solution)/shard_map/all_to_all | solution.py:401
  29.0 0.0 collective-permute-done.3
  29.0 1.9 %collective-permute-start.6 = (bf16[256,512]{1,0:T(8,128)(2,1)S(1)}, bf16[256,512]{1,0:T(8,128)(2,1)S(1)}, u32[]{:S(2)}, u32[]{:S(2)}) collective-permute-start(bf16[256,512]{1,0:T(8,128)(2,1)S(1)} %constant_dynamic-update-slice_fusion.2.own_ref), channel_id=1, source_target_pairs={{0,32},{32,0},{1,33},{33,1},{2,34},{34,2},{3,35},{35,3},{4,36},{36... | collective-permute-start | bytes 786440 | tf_op jit(solution)/shard_map/ppermute | solution.py:405
  30.9 0.0 collective-permute-done
  30.9 4.1 %collective-permute-start.1 = (bf16[128,128]{1,0:T(8,128)(2,1)S(1)}, bf16[128,128]{1,0:T(8,128)(2,1)S(1)}, u32[]{:S(2)}, u32[]{:S(2)}) collective-permute-start(bf16[128,128]{1,0:T(8,128)(2,1)S(1)} %constant_dynamic-update-slice_fusion.near_ref.queries_ref), channel_id=1, source_target_pairs={{0,24},{8,16},{16,8},{24,0},{1,25},{9,17},{17,9},{25,1},{2,26},{10... | collective-permute-start | bytes 98312 | tf_op jit(solution)/shard_map/ppermute | solution.py:405
  35.7 1.6 %fetch.1 = (bf16[1,512,1024]{2,1,0:T(8,128)(2,1)S(1)}, bf16[1,512,1024]{2,1,0:T(8,128)(2,1)S(1)}) custom-call(bf16[1,512,1024]{2,1,0:T(8,128)(2,1)} %keys_hbm, bf16[1,512,1024]{2,1,0:T(8,128)(2,1)} %values_hbm.1), custom_call_target="tpu_custom_call" | custom-call | flops 1 | bytes 1 | tf_op jit(solution)/shard_map/fetch/pallas_call | solution.py:132
  37.3 0.7 %collective-permute-done.1.far_ref = bf16[128,128]{1,0:T(8,128)(2,1)S(1)} collective-permute-done((bf16[128,128]{1,0:T(8,128)(2,1)S(1)}, bf16[128,128]{1,0:T(8,128)(2,1)S(1)}, u32[]{:S(2)}, u32[]{:S(2)}) %collective-permute-start.1) | collective-permute-done | bytes 32800 | tf_op jit(solution)/shard_map/ppermute | solution.py:405
  38.0 1.2 %attend.1 = (f32[2,72,128]{2,1,0:T(8,128)S(1)}, bf16[2,80,128]{2,1,0:T(8,128)(2,1)S(1)}) custom-call(s32[1,256]{1,0:T(1,128)S(1)} %broadcast_in_dim.2.lengths_ref, bf16[128,128]{1,0:T(8,128)(2,1)S(1)} %constant_dynamic-update-slice_fusion.near_ref.queries_ref, bf16[128,128]{1,0:T(8,128)(2,1)S(1)} %collective-permute-done.1.far_ref, ...), custom_call_target="tpu_custom_call" | custom-call | flops 1 | bytes 1 | tf_op jit(solution)/shard_map/attend/pallas_call | solution.py:209
  39.2 0.9 %project.1 = bf16[16,4,768]{2,1,0:T(4,128)(2,1)} custom-call(bf16[16,4,512]{2,1,0:T(4,128)(2,1)S(1)} %all-to-all-done.hidden_ref, bf16[256,512]{1,0:T(8,128)(2,1)S(1)} %constant_dynamic-update-slice_fusion.2.own_ref, bf16[256,512]{1,0:T(8,128)(2,1)S(1)} %collective-permute-done.6.other_ref), custom_call_target="tpu_custom_call" | custom-call | flops 33554432 | bytes 1048576 | tf_op jit(solution)/shard_map/project/pallas_call | solution.py:288
  40.1 5.4 %all-to-all-start.1 = ((bf16[16,4,768]{2,1,0:T(4,128)(2,1)}), bf16[16,4,768]{2,1,0:T(4,128)(2,1)S(1)}, u32[]{:S(2)}, u32[]{:S(2)}) async-start(bf16[16,4,768]{2,1,0:T(4,128)(2,1)} %project.1), calls=%async_computation.1 | async-start | bytes 196608 | tf_op jit(solution)/shard_map/all_to_all | solution.py:401
  45.5 4.1 %collective-permute-start.4 = (bf16[2,80,128]{2,1,0:T(8,128)(2,1)S(1)}, bf16[2,80,128]{2,1,0:T(8,128)(2,1)S(1)}, u32[]{:S(2)}, u32[]{:S(2)}) collective-permute-start(bf16[2,80,128]{2,1,0:T(8,128)(2,1)S(1)} %get-tuple-element.24), channel_id=1, source_target_pairs={{0,24},{8,16},{16,8},{24,0},{1,25},{9,17},{17,9},{25,1},{2,26},{10... | collective-permute-start | bytes 122888 | tf_op jit(solution)/shard_map/ppermute | solution.py:405
  49.6 0.1 fusion
  49.7 2.9 %collective-permute-done.4.come_ref = bf16[2,80,128]{2,1,0:T(8,128)(2,1)S(1)} collective-permute-done((bf16[2,80,128]{2,1,0:T(8,128)(2,1)S(1)}, bf16[2,80,128]{2,1,0:T(8,128)(2,1)S(1)}, u32[]{:S(2)}, u32[]{:S(2)}) %collective-permute-start.4) | collective-permute-done | bytes 40992 | tf_op jit(solution)/shard_map/ppermute | solution.py:405
  52.6 0.2 merge.1
  52.9 1.9 %collective-permute-start.5 = (bf16[80,128]{1,0:T(8,128)(2,1)S(1)}, bf16[80,128]{1,0:T(8,128)(2,1)S(1)}, u32[]{:S(2)}, u32[]{:S(2)}) collective-permute-start(bf16[80,128]{1,0:T(8,128)(2,1)S(1)} %get-tuple-element.26), channel_id=1, source_target_pairs={{0,8},{8,0},{16,24},{24,16},{1,9},{9,1},{17,25},{25,17},{2,10},{10... | collective-permute-start | bytes 61448 | tf_op jit(solution)/shard_map/ppermute | solution.py:405
  54.8 0.1 pad_maximum_fusion.1
  54.9 3.7 %collective-permute-done.5.part1_ref = bf16[80,128]{1,0:T(8,128)(2,1)S(1)} collective-permute-done((bf16[80,128]{1,0:T(8,128)(2,1)S(1)}, bf16[80,128]{1,0:T(8,128)(2,1)S(1)}, u32[]{:S(2)}, u32[]{:S(2)}) %collective-permute-start.5) | collective-permute-done | bytes 20512 | tf_op jit(solution)/shard_map/ppermute | solution.py:405
  58.6 1.1 %finish.1 = (bf16[4,2048]{1,0:T(4,128)(2,1)}, bf16[4,256]{1,0:T(4,128)(2,1)}, bf16[4,256]{1,0:T(4,128)(2,1)}) custom-call(f32[72,128]{1,0:T(8,128)S(1)} %get-tuple-element.25.part0_ref, bf16[80,128]{1,0:T(8,128)(2,1)S(1)} %collective-permute-done.5.part1_ref, bf16[16,4,768]{2,1,0:T(4,128)(2,1)S(1)} %all-to-all-done.1.sums_ref, ...), custom_call_target="tpu_custom_call" | custom-call | flops 1048576 | bytes 524288 | tf_op jit(solution)/shard_map/finish/pallas_call | solution.py:369
  (16 shorter events, 0.1 us)
Async XLA Ops:
  0.6 4.3 %copy-start = (bf16[4,1,8192]{2,0,1:T(4,128)(2,1)S(1)}, bf16[4,1,8192]{2,0,1:T(4,128)(2,1)}, u32[]{:S(2)}) copy-start(bf16[4,1,8192]{2,0,1:T(4,128)(2,1)} %param.6) | copy-start | bytes 196612
  0.6 4.3 %copy-start.1 = (bf16[4,1,2048]{2,0,1:T(4,128)(2,1)S(1)}, bf16[4,1,2048]{2,0,1:T(4,128)(2,1)}, u32[]{:S(2)}) copy-start(bf16[4,1,2048]{2,0,1:T(4,128)(2,1)} %param.8) | copy-start | bytes 49156
  1.5 7.6 %collective-permute-start.2 = (bf16[64,512]{1,0:T(8,128)(2,1)S(1)}, bf16[64,512]{1,0:T(8,128)(2,1)S(1)}, u32[]{:S(2)}, u32[]{:S(2)}) collective-permute-start(bf16[64,512]{1,0:T(8,128)(2,1)S(1)} %bitcast.12), channel_id=1, source_target_pairs={{0,2},{2,0},{4,6},{6,4},{1,3},{3,1},{5,7},{7,5},{8,10},{10,8},{12,... | collective-permute-start | bytes 196616 | tf_op jit(solution)/shard_map/ppermute | solution.py:405
  5.7 25.2 %collective-permute-start = (bf16[64,128]{1,0:T(8,128)(2,1)S(1)}, bf16[64,128]{1,0:T(8,128)(2,1)S(1)}, u32[]{:S(2)}, u32[]{:S(2)}) collective-permute-start(bf16[64,128]{1,0:T(8,128)(2,1)S(1)} %get-tuple-element.19), channel_id=1, source_target_pairs={{0,8},{8,0},{16,24},{24,16},{1,9},{9,1},{17,25},{25,17},{2,10},{10... | collective-permute-start | bytes 49160 | tf_op jit(solution)/shard_map/ppermute | solution.py:405
  9.2 19.8 %collective-permute-start.3 = (bf16[128,512]{1,0:T(8,128)(2,1)S(1)}, bf16[128,512]{1,0:T(8,128)(2,1)S(1)}, u32[]{:S(2)}, u32[]{:S(2)}) collective-permute-start(bf16[128,512]{1,0:T(8,128)(2,1)S(1)} %pad_maximum_fusion), channel_id=1, source_target_pairs={{0,6},{2,4},{4,2},{6,0},{1,7},{3,5},{5,3},{7,1},{8,14},{10,12},{12... | collective-permute-start | bytes 393224 | tf_op jit(solution)/shard_map/ppermute | solution.py:405
  13.2 25.9 %all-to-all-start = ((bf16[16,4,512]{2,1,0:T(4,128)(2,1)}), bf16[16,4,512]{2,1,0:T(4,128)(2,1)S(1)}, u32[]{:S(2)}, u32[]{:S(2)}) async-start(bf16[16,4,512]{2,1,0:T(4,128)(2,1)} %get-tuple-element.28), calls=%async_computation | async-start | bytes 131072 | tf_op jit(solution)/shard_map/all_to_all | solution.py:401
  29.0 10.2 %collective-permute-start.6 = (bf16[256,512]{1,0:T(8,128)(2,1)S(1)}, bf16[256,512]{1,0:T(8,128)(2,1)S(1)}, u32[]{:S(2)}, u32[]{:S(2)}) collective-permute-start(bf16[256,512]{1,0:T(8,128)(2,1)S(1)} %constant_dynamic-update-slice_fusion.2.own_ref), channel_id=1, source_target_pairs={{0,32},{32,0},{1,33},{33,1},{2,34},{34,2},{3,35},{35,3},{4,36},{36... | collective-permute-start | bytes 786440 | tf_op jit(solution)/shard_map/ppermute | solution.py:405
  30.9 7.0 %collective-permute-start.1 = (bf16[128,128]{1,0:T(8,128)(2,1)S(1)}, bf16[128,128]{1,0:T(8,128)(2,1)S(1)}, u32[]{:S(2)}, u32[]{:S(2)}) collective-permute-start(bf16[128,128]{1,0:T(8,128)(2,1)S(1)} %constant_dynamic-update-slice_fusion.near_ref.queries_ref), channel_id=1, source_target_pairs={{0,24},{8,16},{16,8},{24,0},{1,25},{9,17},{17,9},{25,1},{2,26},{10... | collective-permute-start | bytes 98312 | tf_op jit(solution)/shard_map/ppermute | solution.py:405
  40.1 18.5 %all-to-all-start.1 = ((bf16[16,4,768]{2,1,0:T(4,128)(2,1)}), bf16[16,4,768]{2,1,0:T(4,128)(2,1)S(1)}, u32[]{:S(2)}, u32[]{:S(2)}) async-start(bf16[16,4,768]{2,1,0:T(4,128)(2,1)} %project.1), calls=%async_computation.1 | async-start | bytes 196608 | tf_op jit(solution)/shard_map/all_to_all | solution.py:401
  45.5 7.1 %collective-permute-start.4 = (bf16[2,80,128]{2,1,0:T(8,128)(2,1)S(1)}, bf16[2,80,128]{2,1,0:T(8,128)(2,1)S(1)}, u32[]{:S(2)}, u32[]{:S(2)}) collective-permute-start(bf16[2,80,128]{2,1,0:T(8,128)(2,1)S(1)} %get-tuple-element.24), channel_id=1, source_target_pairs={{0,24},{8,16},{16,8},{24,0},{1,25},{9,17},{17,9},{25,1},{2,26},{10... | collective-permute-start | bytes 122888 | tf_op jit(solution)/shard_map/ppermute | solution.py:405
  52.9 5.7 %collective-permute-start.5 = (bf16[80,128]{1,0:T(8,128)(2,1)S(1)}, bf16[80,128]{1,0:T(8,128)(2,1)S(1)}, u32[]{:S(2)}, u32[]{:S(2)}) collective-permute-start(bf16[80,128]{1,0:T(8,128)(2,1)S(1)} %get-tuple-element.26), channel_id=1, source_target_pairs={{0,8},{8,0},{16,24},{24,16},{1,9},{9,1},{17,25},{25,17},{2,10},{10... | collective-permute-start | bytes 61448 | tf_op jit(solution)/shard_map/ppermute | solution.py:405

commit v7 on v6

--- a/solution.py
+++ b/solution.py
@@ -86,7 +86,7 @@
     )(hidden, queries)
 
 
-ORDER = (0, 1, 3, 2)
+ORDER = (0, 3, 1, 2)
 
 
 PART = (OWN_ROWS + 8, HD)
@@ -159,9 +159,9 @@
         starts.append(start)
         for head in range(LOCAL_HEADS):
             lanes = pl.ds(pl.multiple_of(start + head * HD, HD), HD)
-            at = (k % 2) * OWN_ROWS + head * HEAD_ROWS
+            at = (k // 2) * OWN_ROWS + head * HEAD_ROWS
             to = k * OWN_ROWS + head * HEAD_ROWS
-            piece = (near_ref, far_ref)[k // 2][at : at + HEAD_ROWS, :]
+            piece = (near_ref, far_ref)[k % 2][at : at + HEAD_ROWS, :]
             spread[to : to + HEAD_ROWS, lanes] = piece
     scores = lax.dot_general(
         keys_ref[0], spread[...], (((1,), (1,)), ((), ())), preferred_element_type=F32
@@ -264,18 +264,22 @@
     odd = x % 2 == 1
     for z in range(16):
         tokens[z * STEPS : (z + 1) * STEPS, :] = hidden_ref[z].astype(F32)
-    partial = jnp.zeros((16 * STEPS, 512), F32)
+    partials = []
     for swap, weight_ref in enumerate((own_ref, other_ref)):
+        blocks = []
         for pair in range(2):
             at = (core ^ swap) * 256 + ((x // 2) ^ pair) * 128
             block = tokens[:, pl.ds(pl.multiple_of(at, 128), 128)]
             turned = pltpu.roll(block, 64, 1)
-            block = jnp.where(odd, *((block, turned) if pair else (turned, block)))
-            partial += jnp.dot(
-                block.astype(BF16),
-                weight_ref[pair * 128 : pair * 128 + 128, :],
+            blocks.append(jnp.where(odd, *((block, turned) if pair else (turned, block))))
+        partials.append(
+            jnp.dot(
+                jnp.concatenate(blocks, axis=1).astype(BF16),
+                weight_ref[...],
                 preferred_element_type=F32,
             )
+        )
+    partial = partials[0] + partials[1]
     leading = partial.astype(BF16).astype(F32)
     trailing = (partial - leading)[:, :WIDTH]
     for z in range(16):
@@ -421,8 +425,8 @@
     other = with_partner(weight, "core", 1, 2)
     partial = project(tokens, weight, gate(other, kept))
     sums = exchange_z(partial, SUMS_ORDER)
-    own_part, next_part = merge(kept, with_partner(sent, "tensor", 3))
-    parts = (own_part, with_partner(next_part, "tensor", 1))
+    own_part, next_part = merge(kept, with_partner(sent, "tensor", 1))
+    parts = (own_part, with_partner(next_part, "tensor", 3))
     cos_part, sin_part = rotation(lengths)
     outs = finish(parts, sums, near, cos_part, sin_part)
     return tuple(out.reshape(STEPS, 1, -1) for out in outs)

time: 60.2 us -> 60.2 us (level)
  starting transfers between devices: 44 us -> 44.8 us
  waiting for transfers between devices: 7.27 us -> 6.54 us
    ppermute x7, starting transfers between devices: 22.9 us -> 23.6 us  [with_partner(): return lax.ppermute(values, axis, [(i, i ^ flip) for i in range(size)])]
    ppermute x7, waiting for transfers between devices: 7.26 us -> 6.54 us  [with_partner(): return lax.ppermute(values, axis, [(i, i ^ flip) for i in range(size)])]
where the time goes in v7:
time: 60.2 us; the launch traced here: 59.7 us
  starting transfers between devices  44.8 us (74%)
  waiting for transfers between devices  6.54 us (11%)
  Pallas kernels  5.75 us (10%)
  between operations  1.48 us (2%)
  local copies, waits for them, and re-layouts  0.92 us (2%)
    ppermute x7, starting transfers between devices, with_partner(): return lax.ppermute(values, axis, [(i, i ^ flip) for i in range(size)])  23.6 us
    all_to_all x2, starting transfers between devices, exchange_z(): return lax.all_to_all(blocks, Z_AXES, 0, 0, axis_index_groups=[order])  21.1 us
    ppermute x7, waiting for transfers between devices, with_partner(): return lax.ppermute(values, axis, [(i, i ^ flip) for i in range(size)])  6.54 us
    pallas_call x1, Pallas kernels, fetch(): pl.pallas_call(fetch_kernel, out_shape=(pltpu.VMEM(keys.shape, BF16), plt...  1.56 us
  transfers between devices with their start and end apart: 9, of which 3 were waited for; matrix products, arithmetic and copies ran while one was open for 0% of the time, Pallas kernels for 6%

profile of v7, /device:TPU:32, one launch (start us, length us, event | category | flops | bytes accessed | tf_op | source)
XLA Modules:
  0.0 59.7 jit_solution(18244934988548409729)
XLA Ops:
  0.7 0.9 %copy.9 = bf16[8,8,2,256]{3,1,2,0:T(8,128)(2,1)S(1)} copy(bf16[8,8,2,256]{3,2,1,0:T(2,128)(2,1)} %bitcast.15) | data formatting | bytes 131072
  1.5 3.4 %collective-permute-start.2 = (bf16[64,512]{1,0:T(8,128)(2,1)S(1)}, bf16[64,512]{1,0:T(8,128)(2,1)S(1)}, u32[]{:S(2)}, u32[]{:S(2)}) collective-permute-start(bf16[64,512]{1,0:T(8,128)(2,1)S(1)} %bitcast.12), channel_id=1, source_target_pairs={{0,2},{2,0},{4,6},{6,4},{1,3},{3,1},{5,7},{7,5},{8,10},{10,8},{12,... | collective-permute-start | bytes 196616 | tf_op jit(solution)/shard_map/ppermute | solution.py:409
  5.0 0.7 %prepare.1 = (bf16[16,4,512]{2,1,0:T(4,128)(2,1)}, bf16[64,128]{1,0:T(8,128)(2,1)S(1)}) custom-call(bf16[4,8192]{1,0:T(4,128)(2,1)S(1)} %bitcast.10, bf16[4,2048]{1,0:T(4,128)(2,1)S(1)} %bitcast.11), custom_call_target="tpu_custom_call" | custom-call | flops 65536 | bytes 262144 | tf_op jit(solution)/shard_map/prepare/pallas_call | solution.py:74
  5.7 3.5 %collective-permute-start = (bf16[64,128]{1,0:T(8,128)(2,1)S(1)}, bf16[64,128]{1,0:T(8,128)(2,1)S(1)}, u32[]{:S(2)}, u32[]{:S(2)}) collective-permute-start(bf16[64,128]{1,0:T(8,128)(2,1)S(1)} %get-tuple-element.19), channel_id=1, source_target_pairs={{0,8},{8,0},{16,24},{24,16},{1,9},{9,1},{17,25},{25,17},{2,10},{10... | collective-permute-start | bytes 49160 | tf_op jit(solution)/shard_map/ppermute | solution.py:409
  9.2 0.0 collective-permute-done.2
  9.2 4.0 %collective-permute-start.3 = (bf16[128,512]{1,0:T(8,128)(2,1)S(1)}, bf16[128,512]{1,0:T(8,128)(2,1)S(1)}, u32[]{:S(2)}, u32[]{:S(2)}) collective-permute-start(bf16[128,512]{1,0:T(8,128)(2,1)S(1)} %pad_maximum_fusion), channel_id=1, source_target_pairs={{0,6},{2,4},{4,2},{6,0},{1,7},{3,5},{5,3},{7,1},{8,14},{10,12},{12... | collective-permute-start | bytes 393224 | tf_op jit(solution)/shard_map/ppermute | solution.py:409
  13.2 15.7 %all-to-all-start = ((bf16[16,4,512]{2,1,0:T(4,128)(2,1)}), bf16[16,4,512]{2,1,0:T(4,128)(2,1)S(1)}, u32[]{:S(2)}, u32[]{:S(2)}) async-start(bf16[16,4,512]{2,1,0:T(4,128)(2,1)} %get-tuple-element.28), calls=%async_computation | async-start | bytes 131072 | tf_op jit(solution)/shard_map/all_to_all | solution.py:405
  29.0 0.0 collective-permute-done.3
  29.0 1.9 %collective-permute-start.6 = (bf16[256,512]{1,0:T(8,128)(2,1)S(1)}, bf16[256,512]{1,0:T(8,128)(2,1)S(1)}, u32[]{:S(2)}, u32[]{:S(2)}) collective-permute-start(bf16[256,512]{1,0:T(8,128)(2,1)S(1)} %constant_dynamic-update-slice_fusion.2.own_ref), channel_id=1, source_target_pairs={{0,32},{32,0},{1,33},{33,1},{2,34},{34,2},{3,35},{35,3},{4,36},{36... | collective-permute-start | bytes 786440 | tf_op jit(solution)/shard_map/ppermute | solution.py:409
  30.9 4.1 %collective-permute-start.1 = (bf16[128,128]{1,0:T(8,128)(2,1)S(1)}, bf16[128,128]{1,0:T(8,128)(2,1)S(1)}, u32[]{:S(2)}, u32[]{:S(2)}) collective-permute-start(bf16[128,128]{1,0:T(8,128)(2,1)S(1)} %constant_dynamic-update-slice_fusion.near_ref.queries_ref), channel_id=1, source_target_pairs={{0,24},{8,16},{16,8},{24,0},{1,25},{9,17},{17,9},{25,1},{2,26},{10... | collective-permute-start | bytes 98312 | tf_op jit(solution)/shard_map/ppermute | solution.py:409
  35.7 1.6 %fetch.1 = (bf16[1,512,1024]{2,1,0:T(8,128)(2,1)S(1)}, bf16[1,512,1024]{2,1,0:T(8,128)(2,1)S(1)}) custom-call(bf16[1,512,1024]{2,1,0:T(8,128)(2,1)} %keys_hbm, bf16[1,512,1024]{2,1,0:T(8,128)(2,1)} %values_hbm.1), custom_call_target="tpu_custom_call" | custom-call | flops 1 | bytes 1 | tf_op jit(solution)/shard_map/fetch/pallas_call | solution.py:132
  37.3 0.7 %collective-permute-done.1.far_ref = bf16[128,128]{1,0:T(8,128)(2,1)S(1)} collective-permute-done((bf16[128,128]{1,0:T(8,128)(2,1)S(1)}, bf16[128,128]{1,0:T(8,128)(2,1)S(1)}, u32[]{:S(2)}, u32[]{:S(2)}) %collective-permute-start.1) | collective-permute-done | bytes 32800 | tf_op jit(solution)/shard_map/ppermute | solution.py:409
  38.0 1.2 %attend.1 = (f32[2,72,128]{2,1,0:T(8,128)S(1)}, bf16[2,80,128]{2,1,0:T(8,128)(2,1)S(1)}) custom-call(s32[1,256]{1,0:T(1,128)S(1)} %broadcast_in_dim.2.lengths_ref, bf16[128,128]{1,0:T(8,128)(2,1)S(1)} %constant_dynamic-update-slice_fusion.near_ref.queries_ref, bf16[128,128]{1,0:T(8,128)(2,1)S(1)} %collective-permute-done.1.far_ref, ...), custom_call_target="tpu_custom_call" | custom-call | flops 1 | bytes 1 | tf_op jit(solution)/shard_map/attend/pallas_call | solution.py:209
  39.1 0.0 collective-permute-done.6.other_ref
  39.2 0.9 %project.1 = bf16[16,4,768]{2,1,0:T(4,128)(2,1)} custom-call(bf16[16,4,512]{2,1,0:T(4,128)(2,1)S(1)} %all-to-all-done.hidden_ref, bf16[256,512]{1,0:T(8,128)(2,1)S(1)} %constant_dynamic-update-slice_fusion.2.own_ref, bf16[256,512]{1,0:T(8,128)(2,1)S(1)} %collective-permute-done.6.other_ref), custom_call_target="tpu_custom_call" | custom-call | flops 33554432 | bytes 1048576 | tf_op jit(solution)/shard_map/project/pallas_call | solution.py:292
  40.1 5.4 %all-to-all-start.1 = ((bf16[16,4,768]{2,1,0:T(4,128)(2,1)}), bf16[16,4,768]{2,1,0:T(4,128)(2,1)S(1)}, u32[]{:S(2)}, u32[]{:S(2)}) async-start(bf16[16,4,768]{2,1,0:T(4,128)(2,1)} %project.1), calls=%async_computation.1 | async-start | bytes 196608 | tf_op jit(solution)/shard_map/all_to_all | solution.py:405
  45.5 2.6 %collective-permute-start.4 = (bf16[2,80,128]{2,1,0:T(8,128)(2,1)S(1)}, bf16[2,80,128]{2,1,0:T(8,128)(2,1)S(1)}, u32[]{:S(2)}, u32[]{:S(2)}) collective-permute-start(bf16[2,80,128]{2,1,0:T(8,128)(2,1)S(1)} %get-tuple-element.24), channel_id=1, source_target_pairs={{0,8},{8,0},{16,24},{24,16},{1,9},{9,1},{17,25},{25,17},{2,10},{10... | collective-permute-start | bytes 122888 | tf_op jit(solution)/shard_map/ppermute | solution.py:409
  48.2 0.1 fusion
  48.3 3.1 %collective-permute-done.4.come_ref = bf16[2,80,128]{2,1,0:T(8,128)(2,1)S(1)} collective-permute-done((bf16[2,80,128]{2,1,0:T(8,128)(2,1)S(1)}, bf16[2,80,128]{2,1,0:T(8,128)(2,1)S(1)}, u32[]{:S(2)}, u32[]{:S(2)}) %collective-permute-start.4) | collective-permute-done | bytes 40992 | tf_op jit(solution)/shard_map/ppermute | solution.py:409
  51.4 0.2 merge.1
  51.7 4.1 %collective-permute-start.5 = (bf16[80,128]{1,0:T(8,128)(2,1)S(1)}, bf16[80,128]{1,0:T(8,128)(2,1)S(1)}, u32[]{:S(2)}, u32[]{:S(2)}) collective-permute-start(bf16[80,128]{1,0:T(8,128)(2,1)S(1)} %get-tuple-element.26), channel_id=1, source_target_pairs={{0,24},{8,16},{16,8},{24,0},{1,25},{9,17},{17,9},{25,1},{2,26},{10... | collective-permute-start | bytes 61448 | tf_op jit(solution)/shard_map/ppermute | solution.py:409
  55.8 0.1 pad_maximum_fusion.1
  55.8 2.7 %collective-permute-done.5.part1_ref = bf16[80,128]{1,0:T(8,128)(2,1)S(1)} collective-permute-done((bf16[80,128]{1,0:T(8,128)(2,1)S(1)}, bf16[80,128]{1,0:T(8,128)(2,1)S(1)}, u32[]{:S(2)}, u32[]{:S(2)}) %collective-permute-start.5) | collective-permute-done | bytes 20512 | tf_op jit(solution)/shard_map/ppermute | solution.py:409
  58.5 1.1 %finish.1 = (bf16[4,2048]{1,0:T(4,128)(2,1)}, bf16[4,256]{1,0:T(4,128)(2,1)}, bf16[4,256]{1,0:T(4,128)(2,1)}) custom-call(f32[72,128]{1,0:T(8,128)S(1)} %get-tuple-element.25.part0_ref, bf16[80,128]{1,0:T(8,128)(2,1)S(1)} %collective-permute-done.5.part1_ref, bf16[16,4,768]{2,1,0:T(4,128)(2,1)S(1)} %all-to-all-done.1.sums_ref, ...), custom_call_target="tpu_custom_call" | custom-call | flops 1048576 | bytes 524288 | tf_op jit(solution)/shard_map/finish/pallas_call | solution.py:373
  (16 shorter events, 0.1 us)
Async XLA Ops:
  0.6 4.3 %copy-start = (bf16[4,1,8192]{2,0,1:T(4,128)(2,1)S(1)}, bf16[4,1,8192]{2,0,1:T(4,128)(2,1)}, u32[]{:S(2)}) copy-start(bf16[4,1,8192]{2,0,1:T(4,128)(2,1)} %param.6) | copy-start | bytes 196612
  0.6 4.3 %copy-start.1 = (bf16[4,1,2048]{2,0,1:T(4,128)(2,1)S(1)}, bf16[4,1,2048]{2,0,1:T(4,128)(2,1)}, u32[]{:S(2)}) copy-start(bf16[4,1,2048]{2,0,1:T(4,128)(2,1)} %param.8) | copy-start | bytes 49156
  1.5 7.6 %collective-permute-start.2 = (bf16[64,512]{1,0:T(8,128)(2,1)S(1)}, bf16[64,512]{1,0:T(8,128)(2,1)S(1)}, u32[]{:S(2)}, u32[]{:S(2)}) collective-permute-start(bf16[64,512]{1,0:T(8,128)(2,1)S(1)} %bitcast.12), channel_id=1, source_target_pairs={{0,2},{2,0},{4,6},{6,4},{1,3},{3,1},{5,7},{7,5},{8,10},{10,8},{12,... | collective-permute-start | bytes 196616 | tf_op jit(solution)/shard_map/ppermute | solution.py:409
  5.7 25.2 %collective-permute-start = (bf16[64,128]{1,0:T(8,128)(2,1)S(1)}, bf16[64,128]{1,0:T(8,128)(2,1)S(1)}, u32[]{:S(2)}, u32[]{:S(2)}) collective-permute-start(bf16[64,128]{1,0:T(8,128)(2,1)S(1)} %get-tuple-element.19), channel_id=1, source_target_pairs={{0,8},{8,0},{16,24},{24,16},{1,9},{9,1},{17,25},{25,17},{2,10},{10... | collective-permute-start | bytes 49160 | tf_op jit(solution)/shard_map/ppermute | solution.py:409
  9.2 19.8 %collective-permute-start.3 = (bf16[128,512]{1,0:T(8,128)(2,1)S(1)}, bf16[128,512]{1,0:T(8,128)(2,1)S(1)}, u32[]{:S(2)}, u32[]{:S(2)}) collective-permute-start(bf16[128,512]{1,0:T(8,128)(2,1)S(1)} %pad_maximum_fusion), channel_id=1, source_target_pairs={{0,6},{2,4},{4,2},{6,0},{1,7},{3,5},{5,3},{7,1},{8,14},{10,12},{12... | collective-permute-start | bytes 393224 | tf_op jit(solution)/shard_map/ppermute | solution.py:409
  13.2 25.9 %all-to-all-start = ((bf16[16,4,512]{2,1,0:T(4,128)(2,1)}), bf16[16,4,512]{2,1,0:T(4,128)(2,1)S(1)}, u32[]{:S(2)}, u32[]{:S(2)}) async-start(bf16[16,4,512]{2,1,0:T(4,128)(2,1)} %get-tuple-element.28), calls=%async_computation | async-start | bytes 131072 | tf_op jit(solution)/shard_map/all_to_all | solution.py:405
  29.0 10.2 %collective-permute-start.6 = (bf16[256,512]{1,0:T(8,128)(2,1)S(1)}, bf16[256,512]{1,0:T(8,128)(2,1)S(1)}, u32[]{:S(2)}, u32[]{:S(2)}) collective-permute-start(bf16[256,512]{1,0:T(8,128)(2,1)S(1)} %constant_dynamic-update-slice_fusion.2.own_ref), channel_id=1, source_target_pairs={{0,32},{32,0},{1,33},{33,1},{2,34},{34,2},{3,35},{35,3},{4,36},{36... | collective-permute-start | bytes 786440 | tf_op jit(solution)/shard_map/ppermute | solution.py:409
  30.9 7.0 %collective-permute-start.1 = (bf16[128,128]{1,0:T(8,128)(2,1)S(1)}, bf16[128,128]{1,0:T(8,128)(2,1)S(1)}, u32[]{:S(2)}, u32[]{:S(2)}) collective-permute-start(bf16[128,128]{1,0:T(8,128)(2,1)S(1)} %constant_dynamic-update-slice_fusion.near_ref.queries_ref), channel_id=1, source_target_pairs={{0,24},{8,16},{16,8},{24,0},{1,25},{9,17},{17,9},{25,1},{2,26},{10... | collective-permute-start | bytes 98312 | tf_op jit(solution)/shard_map/ppermute | solution.py:409
  40.1 18.5 %all-to-all-start.1 = ((bf16[16,4,768]{2,1,0:T(4,128)(2,1)}), bf16[16,4,768]{2,1,0:T(4,128)(2,1)S(1)}, u32[]{:S(2)}, u32[]{:S(2)}) async-start(bf16[16,4,768]{2,1,0:T(4,128)(2,1)} %project.1), calls=%async_computation.1 | async-start | bytes 196608 | tf_op jit(solution)/shard_map/all_to_all | solution.py:405
  45.5 5.9 %collective-permute-start.4 = (bf16[2,80,128]{2,1,0:T(8,128)(2,1)S(1)}, bf16[2,80,128]{2,1,0:T(8,128)(2,1)S(1)}, u32[]{:S(2)}, u32[]{:S(2)}) collective-permute-start(bf16[2,80,128]{2,1,0:T(8,128)(2,1)S(1)} %get-tuple-element.24), channel_id=1, source_target_pairs={{0,8},{8,0},{16,24},{24,16},{1,9},{9,1},{17,25},{25,17},{2,10},{10... | collective-permute-start | bytes 122888 | tf_op jit(solution)/shard_map/ppermute | solution.py:409
  51.7 6.9 %collective-permute-start.5 = (bf16[80,128]{1,0:T(8,128)(2,1)S(1)}, bf16[80,128]{1,0:T(8,128)(2,1)S(1)}, u32[]{:S(2)}, u32[]{:S(2)}) collective-permute-start(bf16[80,128]{1,0:T(8,128)(2,1)S(1)} %get-tuple-element.26), channel_id=1, source_target_pairs={{0,24},{8,16},{16,8},{24,0},{1,25},{9,17},{17,9},{25,1},{2,26},{10... | collective-permute-start | bytes 61448 | tf_op jit(solution)/shard_map/ppermute | solution.py:409

commit v8 on v6

--- a/solution.py
+++ b/solution.py
@@ -27,8 +27,15 @@
     return [(first + hops) % 16 for hops in range(16)]
 
 
+def outward(first):
+    order = [first]
+    for hops in range(1, 8):
+        order += [(first + hops) % 16, (first - hops) % 16]
+    return order + [(first + 8) % 16]
+
+
 TOKENS_ORDER = ring(11)
-SUMS_ORDER = ring(0)
+SUMS_ORDER = outward(0)
 
 
 def lane_iota(shape):

time: 60.2 us -> 60.2 us (level)
  no operation moved by 1% of the time
where the time goes in v8:
time: 60.2 us; the launch traced here: 59.7 us
  starting transfers between devices  44 us (73%)
  waiting for transfers between devices  7.27 us (12%)
  Pallas kernels  5.77 us (10%)
  between operations  1.48 us (2%)
  local copies, waits for them, and re-layouts  0.92 us (2%)
    ppermute x7, starting transfers between devices, with_partner(): return lax.ppermute(values, axis, [(i, i ^ flip) for i in range(size)])  22.9 us
    all_to_all x2, starting transfers between devices, exchange_z(): return lax.all_to_all(blocks, Z_AXES, 0, 0, axis_index_groups=[order])  21.1 us
    ppermute x7, waiting for transfers between devices, with_partner(): return lax.ppermute(values, axis, [(i, i ^ flip) for i in range(size)])  7.26 us
    pallas_call x1, Pallas kernels, fetch(): pl.pallas_call(fetch_kernel, out_shape=(pltpu.VMEM(keys.shape, BF16), plt...  1.56 us
  transfers between devices with their start and end apart: 9, of which 3 were waited for; matrix products, arithmetic and copies ran while one was open for 0% of the time, Pallas kernels for 6%

profile of v8, /device:TPU:32, one launch (start us, length us, event | category | flops | bytes accessed | tf_op | source)
XLA Modules:
  0.0 59.7 jit_solution(16187205081038646788)
XLA Ops:
  0.7 0.9 %copy.9 = bf16[8,8,2,256]{3,1,2,0:T(8,128)(2,1)S(1)} copy(bf16[8,8,2,256]{3,2,1,0:T(2,128)(2,1)} %bitcast.15) | data formatting | bytes 131072
  1.5 3.4 %collective-permute-start.2 = (bf16[64,512]{1,0:T(8,128)(2,1)S(1)}, bf16[64,512]{1,0:T(8,128)(2,1)S(1)}, u32[]{:S(2)}, u32[]{:S(2)}) collective-permute-start(bf16[64,512]{1,0:T(8,128)(2,1)S(1)} %bitcast.12), channel_id=1, source_target_pairs={{0,2},{2,0},{4,6},{6,4},{1,3},{3,1},{5,7},{7,5},{8,10},{10,8},{12,... | collective-permute-start | bytes 196616 | tf_op jit(solution)/shard_map/ppermute | solution.py:412
  5.0 0.7 %prepare.1 = (bf16[16,4,512]{2,1,0:T(4,128)(2,1)}, bf16[64,128]{1,0:T(8,128)(2,1)S(1)}) custom-call(bf16[4,8192]{1,0:T(4,128)(2,1)S(1)} %bitcast.10, bf16[4,2048]{1,0:T(4,128)(2,1)S(1)} %bitcast.11), custom_call_target="tpu_custom_call" | custom-call | flops 65536 | bytes 262144 | tf_op jit(solution)/shard_map/prepare/pallas_call | solution.py:81
  5.7 3.5 %collective-permute-start = (bf16[64,128]{1,0:T(8,128)(2,1)S(1)}, bf16[64,128]{1,0:T(8,128)(2,1)S(1)}, u32[]{:S(2)}, u32[]{:S(2)}) collective-permute-start(bf16[64,128]{1,0:T(8,128)(2,1)S(1)} %get-tuple-element.19), channel_id=1, source_target_pairs={{0,8},{8,0},{16,24},{24,16},{1,9},{9,1},{17,25},{25,17},{2,10},{10... | collective-permute-start | bytes 49160 | tf_op jit(solution)/shard_map/ppermute | solution.py:412
  9.2 0.0 collective-permute-done.2
  9.2 4.0 %collective-permute-start.3 = (bf16[128,512]{1,0:T(8,128)(2,1)S(1)}, bf16[128,512]{1,0:T(8,128)(2,1)S(1)}, u32[]{:S(2)}, u32[]{:S(2)}) collective-permute-start(bf16[128,512]{1,0:T(8,128)(2,1)S(1)} %pad_maximum_fusion), channel_id=1, source_target_pairs={{0,6},{2,4},{4,2},{6,0},{1,7},{3,5},{5,3},{7,1},{8,14},{10,12},{12... | collective-permute-start | bytes 393224 | tf_op jit(solution)/shard_map/ppermute | solution.py:412
  13.2 15.7 %all-to-all-start = ((bf16[16,4,512]{2,1,0:T(4,128)(2,1)}), bf16[16,4,512]{2,1,0:T(4,128)(2,1)S(1)}, u32[]{:S(2)}, u32[]{:S(2)}) async-start(bf16[16,4,512]{2,1,0:T(4,128)(2,1)} %get-tuple-element.28), calls=%async_computation | async-start | bytes 131072 | tf_op jit(solution)/shard_map/all_to_all | solution.py:408
  29.0 0.0 collective-permute-done.3
  29.0 1.9 %collective-permute-start.6 = (bf16[256,512]{1,0:T(8,128)(2,1)S(1)}, bf16[256,512]{1,0:T(8,128)(2,1)S(1)}, u32[]{:S(2)}, u32[]{:S(2)}) collective-permute-start(bf16[256,512]{1,0:T(8,128)(2,1)S(1)} %constant_dynamic-update-slice_fusion.2.own_ref), channel_id=1, source_target_pairs={{0,32},{32,0},{1,33},{33,1},{2,34},{34,2},{3,35},{35,3},{4,36},{36... | collective-permute-start | bytes 786440 | tf_op jit(solution)/shard_map/ppermute | solution.py:412
  30.9 4.1 %collective-permute-start.1 = (bf16[128,128]{1,0:T(8,128)(2,1)S(1)}, bf16[128,128]{1,0:T(8,128)(2,1)S(1)}, u32[]{:S(2)}, u32[]{:S(2)}) collective-permute-start(bf16[128,128]{1,0:T(8,128)(2,1)S(1)} %constant_dynamic-update-slice_fusion.near_ref.queries_ref), channel_id=1, source_target_pairs={{0,24},{8,16},{16,8},{24,0},{1,25},{9,17},{17,9},{25,1},{2,26},{10... | collective-permute-start | bytes 98312 | tf_op jit(solution)/shard_map/ppermute | solution.py:412
  35.7 1.6 %fetch.1 = (bf16[1,512,1024]{2,1,0:T(8,128)(2,1)S(1)}, bf16[1,512,1024]{2,1,0:T(8,128)(2,1)S(1)}) custom-call(bf16[1,512,1024]{2,1,0:T(8,128)(2,1)} %keys_hbm, bf16[1,512,1024]{2,1,0:T(8,128)(2,1)} %values_hbm.1), custom_call_target="tpu_custom_call" | custom-call | flops 1 | bytes 1 | tf_op jit(solution)/shard_map/fetch/pallas_call | solution.py:139
  37.3 0.7 %collective-permute-done.1.far_ref = bf16[128,128]{1,0:T(8,128)(2,1)S(1)} collective-permute-done((bf16[128,128]{1,0:T(8,128)(2,1)S(1)}, bf16[128,128]{1,0:T(8,128)(2,1)S(1)}, u32[]{:S(2)}, u32[]{:S(2)}) %collective-permute-start.1) | collective-permute-done | bytes 32800 | tf_op jit(solution)/shard_map/ppermute | solution.py:412
  38.0 1.2 %attend.1 = (f32[2,72,128]{2,1,0:T(8,128)S(1)}, bf16[2,80,128]{2,1,0:T(8,128)(2,1)S(1)}) custom-call(s32[1,256]{1,0:T(1,128)S(1)} %broadcast_in_dim.2.lengths_ref, bf16[128,128]{1,0:T(8,128)(2,1)S(1)} %constant_dynamic-update-slice_fusion.near_ref.queries_ref, bf16[128,128]{1,0:T(8,128)(2,1)S(1)} %collective-permute-done.1.far_ref, ...), custom_call_target="tpu_custom_call" | custom-call | flops 1 | bytes 1 | tf_op jit(solution)/shard_map/attend/pallas_call | solution.py:216
  39.1 0.0 collective-permute-done.6.other_ref
  39.2 0.9 %project.1 = bf16[16,4,768]{2,1,0:T(4,128)(2,1)} custom-call(bf16[16,4,512]{2,1,0:T(4,128)(2,1)S(1)} %all-to-all-done.hidden_ref, bf16[256,512]{1,0:T(8,128)(2,1)S(1)} %constant_dynamic-update-slice_fusion.2.own_ref, bf16[256,512]{1,0:T(8,128)(2,1)S(1)} %collective-permute-done.6.other_ref), custom_call_target="tpu_custom_call" | custom-call | flops 33554432 | bytes 1048576 | tf_op jit(solution)/shard_map/project/pallas_call | solution.py:295
  40.1 5.4 %all-to-all-start.1 = ((bf16[16,4,768]{2,1,0:T(4,128)(2,1)}), bf16[16,4,768]{2,1,0:T(4,128)(2,1)S(1)}, u32[]{:S(2)}, u32[]{:S(2)}) async-start(bf16[16,4,768]{2,1,0:T(4,128)(2,1)} %project.1), calls=%async_computation.1 | async-start | bytes 196608 | tf_op jit(solution)/shard_map/all_to_all | solution.py:408
  45.5 4.1 %collective-permute-start.4 = (bf16[2,80,128]{2,1,0:T(8,128)(2,1)S(1)}, bf16[2,80,128]{2,1,0:T(8,128)(2,1)S(1)}, u32[]{:S(2)}, u32[]{:S(2)}) collective-permute-start(bf16[2,80,128]{2,1,0:T(8,128)(2,1)S(1)} %get-tuple-element.24), channel_id=1, source_target_pairs={{0,24},{8,16},{16,8},{24,0},{1,25},{9,17},{17,9},{25,1},{2,26},{10... | collective-permute-start | bytes 122888 | tf_op jit(solution)/shard_map/ppermute | solution.py:412
  49.6 0.1 fusion
  49.7 2.9 %collective-permute-done.4.come_ref = bf16[2,80,128]{2,1,0:T(8,128)(2,1)S(1)} collective-permute-done((bf16[2,80,128]{2,1,0:T(8,128)(2,1)S(1)}, bf16[2,80,128]{2,1,0:T(8,128)(2,1)S(1)}, u32[]{:S(2)}, u32[]{:S(2)}) %collective-permute-start.4) | collective-permute-done | bytes 40992 | tf_op jit(solution)/shard_map/ppermute | solution.py:412
  52.6 0.2 merge.1
  52.9 1.9 %collective-permute-start.5 = (bf16[80,128]{1,0:T(8,128)(2,1)S(1)}, bf16[80,128]{1,0:T(8,128)(2,1)S(1)}, u32[]{:S(2)}, u32[]{:S(2)}) collective-permute-start(bf16[80,128]{1,0:T(8,128)(2,1)S(1)} %get-tuple-element.26), channel_id=1, source_target_pairs={{0,8},{8,0},{16,24},{24,16},{1,9},{9,1},{17,25},{25,17},{2,10},{10... | collective-permute-start | bytes 61448 | tf_op jit(solution)/shard_map/ppermute | solution.py:412
  54.8 0.1 pad_maximum_fusion.1
  54.9 3.7 %collective-permute-done.5.part1_ref = bf16[80,128]{1,0:T(8,128)(2,1)S(1)} collective-permute-done((bf16[80,128]{1,0:T(8,128)(2,1)S(1)}, bf16[80,128]{1,0:T(8,128)(2,1)S(1)}, u32[]{:S(2)}, u32[]{:S(2)}) %collective-permute-start.5) | collective-permute-done | bytes 20512 | tf_op jit(solution)/shard_map/ppermute | solution.py:412
  58.6 1.1 %finish.1 = (bf16[4,2048]{1,0:T(4,128)(2,1)}, bf16[4,256]{1,0:T(4,128)(2,1)}, bf16[4,256]{1,0:T(4,128)(2,1)}) custom-call(f32[72,128]{1,0:T(8,128)S(1)} %get-tuple-element.25.part0_ref, bf16[80,128]{1,0:T(8,128)(2,1)S(1)} %collective-permute-done.5.part1_ref, bf16[16,4,768]{2,1,0:T(4,128)(2,1)S(1)} %all-to-all-done.1.sums_ref, ...), custom_call_target="tpu_custom_call" | custom-call | flops 1048576 | bytes 524288 | tf_op jit(solution)/shard_map/finish/pallas_call | solution.py:376
  (16 shorter events, 0.1 us)
Async XLA Ops:
  0.6 4.3 %copy-start = (bf16[4,1,8192]{2,0,1:T(4,128)(2,1)S(1)}, bf16[4,1,8192]{2,0,1:T(4,128)(2,1)}, u32[]{:S(2)}) copy-start(bf16[4,1,8192]{2,0,1:T(4,128)(2,1)} %param.6) | copy-start | bytes 196612
  0.6 4.3 %copy-start.1 = (bf16[4,1,2048]{2,0,1:T(4,128)(2,1)S(1)}, bf16[4,1,2048]{2,0,1:T(4,128)(2,1)}, u32[]{:S(2)}) copy-start(bf16[4,1,2048]{2,0,1:T(4,128)(2,1)} %param.8) | copy-start | bytes 49156
  1.5 7.6 %collective-permute-start.2 = (bf16[64,512]{1,0:T(8,128)(2,1)S(1)}, bf16[64,512]{1,0:T(8,128)(2,1)S(1)}, u32[]{:S(2)}, u32[]{:S(2)}) collective-permute-start(bf16[64,512]{1,0:T(8,128)(2,1)S(1)} %bitcast.12), channel_id=1, source_target_pairs={{0,2},{2,0},{4,6},{6,4},{1,3},{3,1},{5,7},{7,5},{8,10},{10,8},{12,... | collective-permute-start | bytes 196616 | tf_op jit(solution)/shard_map/ppermute | solution.py:412
  5.7 25.2 %collective-permute-start = (bf16[64,128]{1,0:T(8,128)(2,1)S(1)}, bf16[64,128]{1,0:T(8,128)(2,1)S(1)}, u32[]{:S(2)}, u32[]{:S(2)}) collective-permute-start(bf16[64,128]{1,0:T(8,128)(2,1)S(1)} %get-tuple-element.19), channel_id=1, source_target_pairs={{0,8},{8,0},{16,24},{24,16},{1,9},{9,1},{17,25},{25,17},{2,10},{10... | collective-permute-start | bytes 49160 | tf_op jit(solution)/shard_map/ppermute | solution.py:412
  9.2 19.8 %collective-permute-start.3 = (bf16[128,512]{1,0:T(8,128)(2,1)S(1)}, bf16[128,512]{1,0:T(8,128)(2,1)S(1)}, u32[]{:S(2)}, u32[]{:S(2)}) collective-permute-start(bf16[128,512]{1,0:T(8,128)(2,1)S(1)} %pad_maximum_fusion), channel_id=1, source_target_pairs={{0,6},{2,4},{4,2},{6,0},{1,7},{3,5},{5,3},{7,1},{8,14},{10,12},{12... | collective-permute-start | bytes 393224 | tf_op jit(solution)/shard_map/ppermute | solution.py:412
  13.2 25.9 %all-to-all-start = ((bf16[16,4,512]{2,1,0:T(4,128)(2,1)}), bf16[16,4,512]{2,1,0:T(4,128)(2,1)S(1)}, u32[]{:S(2)}, u32[]{:S(2)}) async-start(bf16[16,4,512]{2,1,0:T(4,128)(2,1)} %get-tuple-element.28), calls=%async_computation | async-start | bytes 131072 | tf_op jit(solution)/shard_map/all_to_all | solution.py:408
  29.0 10.2 %collective-permute-start.6 = (bf16[256,512]{1,0:T(8,128)(2,1)S(1)}, bf16[256,512]{1,0:T(8,128)(2,1)S(1)}, u32[]{:S(2)}, u32[]{:S(2)}) collective-permute-start(bf16[256,512]{1,0:T(8,128)(2,1)S(1)} %constant_dynamic-update-slice_fusion.2.own_ref), channel_id=1, source_target_pairs={{0,32},{32,0},{1,33},{33,1},{2,34},{34,2},{3,35},{35,3},{4,36},{36... | collective-permute-start | bytes 786440 | tf_op jit(solution)/shard_map/ppermute | solution.py:412
  30.9 7.0 %collective-permute-start.1 = (bf16[128,128]{1,0:T(8,128)(2,1)S(1)}, bf16[128,128]{1,0:T(8,128)(2,1)S(1)}, u32[]{:S(2)}, u32[]{:S(2)}) collective-permute-start(bf16[128,128]{1,0:T(8,128)(2,1)S(1)} %constant_dynamic-update-slice_fusion.near_ref.queries_ref), channel_id=1, source_target_pairs={{0,24},{8,16},{16,8},{24,0},{1,25},{9,17},{17,9},{25,1},{2,26},{10... | collective-permute-start | bytes 98312 | tf_op jit(solution)/shard_map/ppermute | solution.py:412
  40.1 18.5 %all-to-all-start.1 = ((bf16[16,4,768]{2,1,0:T(4,128)(2,1)}), bf16[16,4,768]{2,1,0:T(4,128)(2,1)S(1)}, u32[]{:S(2)}, u32[]{:S(2)}) async-start(bf16[16,4,768]{2,1,0:T(4,128)(2,1)} %project.1), calls=%async_computation.1 | async-start | bytes 196608 | tf_op jit(solution)/shard_map/all_to_all | solution.py:408
  45.5 7.1 %collective-permute-start.4 = (bf16[2,80,128]{2,1,0:T(8,128)(2,1)S(1)}, bf16[2,80,128]{2,1,0:T(8,128)(2,1)S(1)}, u32[]{:S(2)}, u32[]{:S(2)}) collective-permute-start(bf16[2,80,128]{2,1,0:T(8,128)(2,1)S(1)} %get-tuple-element.24), channel_id=1, source_target_pairs={{0,24},{8,16},{16,8},{24,0},{1,25},{9,17},{17,9},{25,1},{2,26},{10... | collective-permute-start | bytes 122888 | tf_op jit(solution)/shard_map/ppermute | solution.py:412
  52.9 5.7 %collective-permute-start.5 = (bf16[80,128]{1,0:T(8,128)(2,1)S(1)}, bf16[80,128]{1,0:T(8,128)(2,1)S(1)}, u32[]{:S(2)}, u32[]{:S(2)}) collective-permute-start(bf16[80,128]{1,0:T(8,128)(2,1)S(1)} %get-tuple-element.26), channel_id=1, source_target_pairs={{0,8},{8,0},{16,24},{24,16},{1,9},{9,1},{17,25},{25,17},{2,10},{10... | collective-permute-start | bytes 61448 | tf_op jit(solution)/shard_map/ppermute | solution.py:412
